TPU v7x, 32 devices: a whole 2x2x4 slice. The times are simulated.
32 devices in a mesh: tile: 2 (over core), lvl: 16 (over z, y, x).
Axes of the slice: x: 2, y: 2, z: 4, core: 2. Of those that a mesh axis runs over, the one named last changes fastest.
Arguments:
- parents: int32 [3, 256, 4], P(None, ('tile', 'lvl')), may hold values from -1 to 767, as said below
- factors: bfloat16 [3, 256, 4, 256, 256], P(None, ('tile', 'lvl')), may hold values from -0.125 to 0.125
- chol: bfloat16 [4, 256, 256, 256], P(None, ('tile', 'lvl')), as said below
- noise: bfloat16 [4, 256, 256, 256], P(None, ('tile', 'lvl')), may hold values from -6 to 6
Outputs:
- samples: bfloat16 [4, 256, 256, 256], P(None, ('tile', 'lvl'))
Inputs may be any that keep to these rules, and one draw needn't show every extreme that they name: `parents`: parents of a block of level s + 1 are blocks of levels 0 to s owned by a device of the same spatial tile or of the tile with index one less. Among the 32 entries of one device's blocks of one level, at most 2 name blocks owned by any one device of the same tile and at most 1 name blocks owned by any one device of the previous tile; in every draw, both bounds are reached by some device (devices of tile 0 have no previous tile, so their previous-tile entries are -1). `chol`: lower triangular with a positive diagonal.
All inputs are finite; a program needn't handle non-finite values.
Results may differ from a plain program's by a relative error of at most 0.0032.
Values may be sent and summed in bfloat16 or wider, within the bound.
No kernel may reach another device: no remote copies, remote signals or barrier semaphores. Data moves between devices by JAX's collectives and lax.ppermute only.
A program may use at most 128 MiB of HBM per device.

v0:
```python
import jax
import jax.numpy as jnp
from jax import lax
from jax.sharding import PartitionSpec as P

NPAR = 4
CAP = 2
CAPX = 1


def passed_along(value, axis, steps):
    count = lax.axis_size(axis)
    first, last = (max(0, -steps), min(count, count - steps))
    return lax.ppermute(value, axis, [(source, source + steps) for source in range(first, last)])


def decode(block_ids, requester_tile, total_blocks, local_blocks, peer_count):
    is_valid = block_ids >= 0
    clipped = jnp.maximum(block_ids, 0)
    parent_level = clipped // total_blocks
    parent_block = clipped % total_blocks
    owner_dev = parent_block // local_blocks
    owner_tile = owner_dev // peer_count
    owner_lane = owner_dev % peer_count
    within = parent_block % local_blocks
    from_prior = owner_tile != requester_tile
    column = owner_lane + peer_count * from_prior.astype(jnp.int32)
    onehot = ((column[..., None] == jnp.arange(2 * peer_count)) & is_valid[..., None]).astype(
        jnp.int32
    )
    before = jnp.cumsum(onehot, axis=-2) - onehot
    slot_rank = jnp.sum(before * onehot, axis=-1)
    return (is_valid, parent_level * local_blocks + within, owner_lane, from_prior, slot_rank)


def slot_table(matched, source, slot_index, width):
    hits = matched[..., None] & (slot_index[..., None] == jnp.arange(width))
    return jnp.sum(jnp.where(hits, source[..., None] + 1, 0), axis=1) - 1


def fill_slots(held_blocks, picked):
    rows = held_blocks[jnp.maximum(picked, 0)]
    return jnp.where((picked >= 0)[..., None, None], rows, jnp.zeros((), rows.dtype))


def noise_part(lower, draws):
    return jnp.einsum("kij,kjr->kir", lower, draws, preferred_element_type=jnp.float32)


def shards(parents, factors, chol, noise):
    peer_count = lax.axis_size("lvl")
    tile_count = lax.axis_size("tile")
    own_lane = lax.axis_index("lvl")
    own_tile = lax.axis_index("tile")
    depth = chol.shape[0]
    local_blocks = chol.shape[1]
    block_rows = chol.shape[2]
    realize = noise.shape[3]
    total_blocks = local_blocks * peer_count * tile_count
    refs_dev = local_blocks * NPAR
    gathered = lax.all_gather(parents, "lvl", axis=1, tiled=True).reshape(
        depth - 1, peer_count, refs_dev
    )
    held_blocks = jnp.zeros(((2 * depth - 1) * local_blocks, block_rows, realize), jnp.bfloat16)
    following = passed_along(gathered, "tile", -1)
    following = jnp.where(own_tile + 1 < tile_count, following, -1)
    latest = noise_part(chol[0], noise[0]).astype(jnp.bfloat16)
    held_blocks = held_blocks.at[0:local_blocks].set(latest)
    outputs = [latest]
    for section in range(1, depth):
        mine_valid, mine_source, mine_lane, mine_prior, mine_rank = decode(
            parents[section - 1].reshape(refs_dev), own_tile, total_blocks, local_blocks, peer_count
        )
        is_valid, source, owner_lane, from_prior, slot_rank = decode(
            gathered[section - 1], own_tile, total_blocks, local_blocks, peer_count
        )
        matched = is_valid & jnp.logical_not(from_prior) & (owner_lane == own_lane)
        same_sent = fill_slots(held_blocks, slot_table(matched, source, slot_rank, CAP))
        same_got = lax.all_to_all(same_sent, "lvl", split_axis=0, concat_axis=0, tiled=True)
        next_valid, next_source, next_lane, next_prior, next_rank = decode(
            following[section - 1], own_tile + 1, total_blocks, local_blocks, peer_count
        )
        next_match = next_valid & next_prior & (next_lane == own_lane)
        prior_sent = fill_slots(held_blocks, slot_table(next_match, next_source, next_rank, CAPX))
        spread = lax.all_to_all(prior_sent, "lvl", split_axis=0, concat_axis=0, tiled=True)
        crossed = passed_along(spread, "tile", 1)
        same_vals = same_got.reshape(-1, block_rows, realize)[
            mine_lane * CAP + jnp.minimum(mine_rank, CAP - 1)
        ]
        prior_vals = crossed.reshape(-1, block_rows, realize)[
            mine_lane * CAPX + jnp.minimum(mine_rank, CAPX - 1)
        ]
        parent_vals = jnp.where(mine_prior[:, None, None], prior_vals, same_vals)
        parent_vals = jnp.where(
            mine_valid[:, None, None], parent_vals, jnp.zeros((), parent_vals.dtype)
        )
        parent_vals = parent_vals.reshape(local_blocks, NPAR, block_rows, realize)
        mixed = jnp.einsum(
            "ksij,ksjr->kir", factors[section - 1], parent_vals, preferred_element_type=jnp.float32
        )
        latest = (mixed + noise_part(chol[section], noise[section])).astype(jnp.bfloat16)
        held_blocks = held_blocks.at[section * local_blocks : (section + 1) * local_blocks].set(
            latest
        )
        outputs.append(latest)
    return jnp.stack(outputs)


def solution(mesh):
    placed = (
        P(None, ("tile", "lvl"), None),
        P(None, ("tile", "lvl"), None, None, None),
        P(None, ("tile", "lvl"), None, None),
        P(None, ("tile", "lvl"), None, None),
    )
    return jax.shard_map(
        shards,
        mesh=mesh,
        in_specs=placed,
        out_specs=P(None, ("tile", "lvl"), None, None),
        check_vma=False,
    )
```

profile of v0, /device:TPU:14, one launch (start us, length us, event | category | flops | bytes accessed | tf_op | source)
XLA Modules:
  0.0 587.3 jit_solution(14911395338951220198)
XLA Ops:
  0.8 29.5 %all_gather.3 = s32[3,128,4]{2,0,1:T(4,128)S(1)} all-gather(s32[3,8,4]{2,0,1:T(4,128)S(1)} %copy.149), channel_id=1, replica_groups=mesh['tile'=2,'lvl'=16] {'lvl'}, dimensions={1}, use_global_device_ids=true | all-gather | bytes 6528 | tf_op jit(solution)/shard_map/all_gather | solution.py:61
  31.8 2.0 convolution_convert_fusion
  33.8 3.8 scatter.10
  41.6 3.8 gather_fusion
  45.4 1.6 fusion.26
  47.0 16.7 %all-to-all-start = ((bf16[16,1,256,256]{3,2,1,0:T(8,128)(2,1)}), bf16[16,1,256,256]{3,2,1,0:T(8,128)(2,1)S(1)}, u32[]{:S(2)}, u32[]{:S(2)}) async-start(bf16[16,1,256,256]{3,2,1,0:T(8,128)(2,1)} %fusion.26), calls=%async_computation | async-start | bytes 4194304 | tf_op jit(solution)/shard_map/all_to_all | solution.py:85
  63.7 1.8 and_reduce_fusion
  70.7 2.2 compare_reduce_fusion.1
  77.1 5.9 %gather_fusion.2 = bf16[32,256,256]{2,1,0:T(8,128)(2,1)} fusion(bf16[56,256,256]{2,1,0:T(8,128)(2,1)} %scatter.10, s32[1024]{0:T(1024)S(1)} %pad_clamp_fusion.9), kind=kCustom, calls=%fused_computation.2 | custom fusion | bytes 8388736 | tf_op jit(solution)/shard_map/gather | solution.py:42
  83.1 4.6 broadcast_select_fusion.2
  87.7 27.0 %all-to-all-done = bf16[16,1,256,256]{3,2,1,0:T(8,128)(2,1)S(1)} async-done(((bf16[16,1,256,256]{3,2,1,0:T(8,128)(2,1)}), bf16[16,1,256,256]{3,2,1,0:T(8,128)(2,1)S(1)}, u32[]{:S(2)}, u32[]{:S(2)}) %all-to-all-start) | async-done | bytes 2097184 | tf_op jit(solution)/shard_map/all_to_all | solution.py:85
  114.7 5.1 all-to-all-start.1
  120.7 1.8 collective-permute-start.1
  122.9 3.4 fusion.59
  126.3 2.8 gather_fusion.1
  129.1 6.5 %copy.170 = bf16[8,4,256,256]{2,3,1,0:T(8,128)(2,1)} copy(bf16[8,4,256,256]{3,2,1,0:T(8,128)(2,1)} %bitcast.304) | data formatting | bytes 8388608 | tf_op jit(solution)/shard_map/gather | solution.py:90
  135.6 79.7 %all-to-all-done.1 = bf16[16,2,256,256]{3,2,1,0:T(8,128)(2,1)} async-done(((bf16[16,2,256,256]{3,2,1,0:T(8,128)(2,1)}), bf16[16,2,256,256]{3,2,1,0:T(8,128)(2,1)}, u32[]{:S(2)}, u32[]{:S(2)}) %all-to-all-start.1) | async-done | bytes 4194336 | tf_op jit(solution)/shard_map/all_to_all | solution.py:79
  215.3 5.0 gather_fusion.3
  220.3 6.6 %copy.171 = bf16[8,4,256,256]{2,3,1,0:T(8,128)(2,1)} copy(bf16[8,4,256,256]{3,2,1,0:T(8,128)(2,1)} %bitcast.305) | data formatting | bytes 8388608 | tf_op jit(solution)/shard_map/gather | solution.py:87
  226.9 7.6 %constant_dynamic-update-slice_fusion.1 = (bf16[56,256,256]{2,1,0:T(8,128)(2,1)}, bf16[8,256,256]{2,1,0:T(8,128)(2,1)}) fusion(bf16[56,256,256]{2,1,0:T(8,128)(2,1)} %scatter.10, f32[8,256,256]{2,1,0:T(8,128)S(1)} %copy-done.4, bf16[3,8,4,256,256]{4,3,2,1,0:T(8,128)(2,1)} %param.11, bf16[8,4,256,256]{2,3,1,0:T(8,128)(2,1)} %copy.170, ...), kind=kOutput, calls=%fused_computation.555 | convolution fusion | flops 1078984704 | bytes 16777280 | tf_op jit(solution)/shard_map/ksij,ksjr->kir/dot_general | solution.py:98
  234.5 3.8 gather_fusion.4
  240.0 5.1 all-to-all-start.2
  248.4 5.9 %gather_fusion.6 = bf16[32,256,256]{2,1,0:T(8,128)(2,1)} fusion(bf16[56,256,256]{2,1,0:T(8,128)(2,1)} %get-tuple-element.83, s32[1024]{0:T(1024)S(1)} %pad_clamp_fusion.5), kind=kCustom, calls=%fused_computation.6 | custom fusion | bytes 8388736 | tf_op jit(solution)/shard_map/gather | solution.py:42
  254.3 4.6 broadcast_select_fusion.1
  258.9 33.5 %all-to-all-done.2 = bf16[16,1,256,256]{3,2,1,0:T(8,128)(2,1)S(1)} async-done(((bf16[16,1,256,256]{3,2,1,0:T(8,128)(2,1)}), bf16[16,1,256,256]{3,2,1,0:T(8,128)(2,1)S(1)}, u32[]{:S(2)}, u32[]{:S(2)}) %all-to-all-start.2) | async-done | bytes 2097184 | tf_op jit(solution)/shard_map/all_to_all | solution.py:85
  293.6 5.1 all-to-all-start.3
  301.1 3.4 fusion.56
  304.4 2.8 gather_fusion.5
  307.3 6.5 %copy.193 = bf16[8,4,256,256]{2,3,1,0:T(8,128)(2,1)} copy(bf16[8,4,256,256]{3,2,1,0:T(8,128)(2,1)} %bitcast.306) | data formatting | bytes 8388608 | tf_op jit(solution)/shard_map/gather | solution.py:90
  313.7 77.6 %all-to-all-done.3 = bf16[16,2,256,256]{3,2,1,0:T(8,128)(2,1)} async-done(((bf16[16,2,256,256]{3,2,1,0:T(8,128)(2,1)}), bf16[16,2,256,256]{3,2,1,0:T(8,128)(2,1)}, u32[]{:S(2)}, u32[]{:S(2)}) %all-to-all-start.3) | async-done | bytes 4194336 | tf_op jit(solution)/shard_map/all_to_all | solution.py:79
  391.3 5.0 gather_fusion.7
  396.3 6.6 %copy.194 = bf16[8,4,256,256]{2,3,1,0:T(8,128)(2,1)} copy(bf16[8,4,256,256]{3,2,1,0:T(8,128)(2,1)} %bitcast.307) | data formatting | bytes 8388608 | tf_op jit(solution)/shard_map/gather | solution.py:87
  402.9 7.6 %constant_dynamic-update-slice_fusion = (bf16[56,256,256]{2,1,0:T(8,128)(2,1)}, bf16[8,256,256]{2,1,0:T(8,128)(2,1)}) fusion(bf16[56,256,256]{2,1,0:T(8,128)(2,1)} %get-tuple-element.83, f32[8,256,256]{2,1,0:T(8,128)S(1)} %copy-done.3, bf16[3,8,4,256,256]{4,3,2,1,0:T(8,128)(2,1)} %param.11, bf16[8,4,256,256]{2,3,1,0:T(8,128)(2,1)} %copy.193, ...), kind=kOutput, calls=%fused_computation.554 | convolution fusion | flops 1078984704 | bytes 16777280 | tf_op jit(solution)/shard_map/ksij,ksjr->kir/dot_general | solution.py:98
  410.5 3.8 gather_fusion.8
  414.2 1.6 fusion.24
  415.8 5.1 all-to-all-start.4
  422.7 5.9 %gather_fusion.10 = bf16[32,256,256]{2,1,0:T(8,128)(2,1)} fusion(bf16[56,256,256]{2,1,0:T(8,128)(2,1)} %get-tuple-element.85, s32[1024]{0:T(1024)S(1)} %pad_clamp_fusion.1), kind=kCustom, calls=%fused_computation.10 | custom fusion | bytes 8388736 | tf_op jit(solution)/shard_map/gather | solution.py:42
  428.6 4.5 broadcast_select_fusion
  433.1 35.1 %all-to-all-done.4 = bf16[16,1,256,256]{3,2,1,0:T(8,128)(2,1)S(1)} async-done(((bf16[16,1,256,256]{3,2,1,0:T(8,128)(2,1)}), bf16[16,1,256,256]{3,2,1,0:T(8,128)(2,1)S(1)}, u32[]{:S(2)}, u32[]{:S(2)}) %all-to-all-start.4) | async-done | bytes 2097184 | tf_op jit(solution)/shard_map/all_to_all | solution.py:85
  469.5 5.1 all-to-all-start.5
  477.1 3.3 fusion.53
  480.4 2.8 gather_fusion.9
  483.2 6.4 %copy.216 = bf16[8,4,256,256]{2,3,1,0:T(8,128)(2,1)} copy(bf16[8,4,256,256]{3,2,1,0:T(8,128)(2,1)} %bitcast.308) | data formatting | bytes 8388608 | tf_op jit(solution)/shard_map/gather | solution.py:90
  489.7 77.3 %all-to-all-done.5 = bf16[16,2,256,256]{3,2,1,0:T(8,128)(2,1)} async-done(((bf16[16,2,256,256]{3,2,1,0:T(8,128)(2,1)}), bf16[16,2,256,256]{3,2,1,0:T(8,128)(2,1)}, u32[]{:S(2)}, u32[]{:S(2)}) %all-to-all-start.5) | async-done | bytes 4194336 | tf_op jit(solution)/shard_map/all_to_all | solution.py:79
  567.0 5.0 gather_fusion.11
  572.0 6.6 %copy.217 = bf16[8,4,256,256]{2,3,1,0:T(8,128)(2,1)} copy(bf16[8,4,256,256]{3,2,1,0:T(8,128)(2,1)} %bitcast.309) | data formatting | bytes 8388608 | tf_op jit(solution)/shard_map/gather | solution.py:87
  578.6 6.4 %fusion.42 = bf16[1,8,256,256]{3,2,1,0:T(8,128)(2,1)S(1)} fusion(f32[8,256,256]{2,1,0:T(8,128)S(1)} %copy-done.5, bf16[3,8,4,256,256]{4,3,2,1,0:T(8,128)(2,1)} %param.11, bf16[8,4,256,256]{2,3,1,0:T(8,128)(2,1)} %copy.216, bf16[8,4,256,256]{2,3,1,0:T(8,128)(2,1)} %copy.217, pred[8,4]{1,0:T(8,128)(4,1)S(1)} %copy.197, pred[8,4]{1,0:T(8,128)(4,1)S(1)} %copy.196), kind=kOutput, calls=%fused_computation.53 | convolution fusion | flops 1078984704 | bytes 15728704 | tf_op jit(solution)/shard_map/ksij,ksjr->kir/dot_general | solution.py:98
  585.0 2.3 pad_maximum_fusion
  (170 shorter events, 30.9 us)
Async XLA Ops:
  30.5 7.1 %collective-permute-start = (s32[3,16,32]{1,2,0:T(8,128)S(1)}, s32[3,16,32]{1,2,0:T(8,128)S(1)}, u32[]{:S(2)}, u32[]{:S(2)}) collective-permute-start(s32[3,16,32]{1,2,0:T(8,128)S(1)} %copy.151), channel_id=1, source_target_pairs={{16,0},{17,1},{18,2},{19,3},{20,4},{21,5},{22,6},{23,7},{24,8},{25... | collective-permute-start | bytes 18440 | tf_op jit(solution)/shard_map/ppermute | solution.py:14
  47.0 67.8 %all-to-all-start = ((bf16[16,1,256,256]{3,2,1,0:T(8,128)(2,1)}), bf16[16,1,256,256]{3,2,1,0:T(8,128)(2,1)S(1)}, u32[]{:S(2)}, u32[]{:S(2)}) async-start(bf16[16,1,256,256]{3,2,1,0:T(8,128)(2,1)} %fusion.26), calls=%async_computation | async-start | bytes 4194304 | tf_op jit(solution)/shard_map/all_to_all | solution.py:85
  87.7 32.2 %copy-start.10 = (s32[3,8,4]{1,2,0:T(4,128)S(1)}, s32[3,8,4]{1,2,0:T(4,128)}, u32[]{:S(2)}) copy-start(s32[3,8,4]{1,2,0:T(4,128)} %param.10) | copy-start | bytes 1156
  114.7 5.1 copy-start
  114.7 100.6 %all-to-all-start.1 = ((bf16[16,2,256,256]{3,2,1,0:T(8,128)(2,1)}), bf16[16,2,256,256]{3,2,1,0:T(8,128)(2,1)}, u32[]{:S(2)}, u32[]{:S(2)}) async-start(bf16[16,2,256,256]{3,2,1,0:T(8,128)(2,1)} %broadcast_select_fusion.2), calls=%async_computation.1 | async-start | bytes 8388608 | tf_op jit(solution)/shard_map/all_to_all | solution.py:79
  119.9 6.4 %copy-start.16 = (s32[16]{0:T(128)S(1)}, s32[16]{0:T(128)}, u32[]{:S(2)}) copy-start(s32[16]{0:T(128)} %get-tuple-element.54) | copy-start | bytes 196
  120.7 5.6 collective-permute-start.1
  220.3 6.6 %copy-start.4 = (f32[8,256,256]{2,1,0:T(8,128)S(1)}, f32[8,256,256]{2,1,0:T(8,128)}, u32[]{:S(2)}) copy-start(f32[8,256,256]{2,1,0:T(8,128)} %fusion.59) | copy-start | bytes 6291460
  238.3 6.8 %copy-start.9 = (s32[128,4]{1,0:T(8,128)S(1)}, s32[128,4]{1,0:T(8,128)}, u32[]{:S(2)}) copy-start(s32[128,4]{1,0:T(8,128)} %get-tuple-element.52) | copy-start | bytes 6148
  238.3 6.9 %copy-start.8 = (s32[128,4]{1,0:T(8,128)S(1)}, s32[128,4]{1,0:T(8,128)}, u32[]{:S(2)}) copy-start(s32[128,4]{1,0:T(8,128)} %get-tuple-element.47) | copy-start | bytes 6148
  238.3 7.4 %copy-start.14 = (pred[128,4]{1,0:T(8,128)(4,1)S(1)}, pred[128,4]{1,0:T(8,128)(4,1)}, u32[]{:S(2)}) copy-start(pred[128,4]{1,0:T(8,128)(4,1)} %get-tuple-element.43) | copy-start | bytes 1540
  238.3 7.6 %copy-start.13 = (pred[128,4]{1,0:T(8,128)(4,1)S(1)}, pred[128,4]{1,0:T(8,128)(4,1)}, u32[]{:S(2)}) copy-start(pred[128,4]{1,0:T(8,128)(4,1)} %get-tuple-element.42) | copy-start | bytes 1540
  238.3 7.8 %copy-start.12 = (pred[128,4]{1,0:T(8,128)(4,1)S(1)}, pred[128,4]{1,0:T(8,128)(4,1)}, u32[]{:S(2)}) copy-start(pred[128,4]{1,0:T(8,128)(4,1)} %get-tuple-element.45) | copy-start | bytes 1540
  238.4 9.2 %copy-start.11 = (pred[128,4]{1,0:T(8,128)(4,1)S(1)}, pred[128,4]{1,0:T(8,128)(4,1)}, u32[]{:S(2)}) copy-start(pred[128,4]{1,0:T(8,128)(4,1)} %get-tuple-element.41) | copy-start | bytes 1540
  240.0 52.4 %all-to-all-start.2 = ((bf16[16,1,256,256]{3,2,1,0:T(8,128)(2,1)}), bf16[16,1,256,256]{3,2,1,0:T(8,128)(2,1)S(1)}, u32[]{:S(2)}, u32[]{:S(2)}) async-start(bf16[16,1,256,256]{3,2,1,0:T(8,128)(2,1)} %fusion.25), calls=%async_computation.2 | async-start | bytes 4194304 | tf_op jit(solution)/shard_map/all_to_all | solution.py:85
  292.3 1.3 copy-start.1
  293.6 97.6 %all-to-all-start.3 = ((bf16[16,2,256,256]{3,2,1,0:T(8,128)(2,1)}), bf16[16,2,256,256]{3,2,1,0:T(8,128)(2,1)}, u32[]{:S(2)}, u32[]{:S(2)}) async-start(bf16[16,2,256,256]{3,2,1,0:T(8,128)(2,1)} %broadcast_select_fusion.1), calls=%async_computation.3 | async-start | bytes 8388608 | tf_op jit(solution)/shard_map/all_to_all | solution.py:79
  298.8 5.6 copy-start.15
  298.8 5.7 collective-permute-start.2
  396.3 6.6 %copy-start.3 = (f32[8,256,256]{2,1,0:T(8,128)S(1)}, f32[8,256,256]{2,1,0:T(8,128)}, u32[]{:S(2)}) copy-start(f32[8,256,256]{2,1,0:T(8,128)} %fusion.56) | copy-start | bytes 6291460
  415.8 52.3 %all-to-all-start.4 = ((bf16[16,1,256,256]{3,2,1,0:T(8,128)(2,1)}), bf16[16,1,256,256]{3,2,1,0:T(8,128)(2,1)S(1)}, u32[]{:S(2)}, u32[]{:S(2)}) async-start(bf16[16,1,256,256]{3,2,1,0:T(8,128)(2,1)} %fusion.24), calls=%async_computation.4 | async-start | bytes 4194304 | tf_op jit(solution)/shard_map/all_to_all | solution.py:85
  468.2 1.3 copy-start.2
  469.5 97.5 %all-to-all-start.5 = ((bf16[16,2,256,256]{3,2,1,0:T(8,128)(2,1)}), bf16[16,2,256,256]{3,2,1,0:T(8,128)(2,1)}, u32[]{:S(2)}, u32[]{:S(2)}) async-start(bf16[16,2,256,256]{3,2,1,0:T(8,128)(2,1)} %broadcast_select_fusion), calls=%async_computation.5 | async-start | bytes 8388608 | tf_op jit(solution)/shard_map/all_to_all | solution.py:79
  474.6 5.8 collective-permute-start.3
  572.0 6.6 %copy-start.5 = (f32[8,256,256]{2,1,0:T(8,128)S(1)}, f32[8,256,256]{2,1,0:T(8,128)}, u32[]{:S(2)}) copy-start(f32[8,256,256]{2,1,0:T(8,128)} %fusion.53) | copy-start | bytes 6291460
  578.6 6.4 %copy-start.6 = (bf16[8,256,256]{2,1,0:T(8,128)(2,1)S(1)}, bf16[8,256,256]{2,1,0:T(8,128)(2,1)}, u32[]{:S(2)}) copy-start(bf16[8,256,256]{2,1,0:T(8,128)(2,1)} %get-tuple-element.84) | copy-start | bytes 3145732
  578.6 6.4 %copy-start.7 = (bf16[8,256,256]{2,1,0:T(8,128)(2,1)S(1)}, bf16[8,256,256]{2,1,0:T(8,128)(2,1)}, u32[]{:S(2)}) copy-start(bf16[8,256,256]{2,1,0:T(8,128)(2,1)} %get-tuple-element.86) | copy-start | bytes 3145732
where the time goes:
time: 589 us; the launch traced here: 587 us
  waiting for transfers between devices  330 us (56%)
  local copies, waits for them, and re-layouts  111 us (19%)
  starting transfers between devices  48.2 us (8%)
  other arithmetic  34.4 us (6%)
  matrix products  33.5 us (6%)
  blocking collectives  29.5 us (5%)
    all_to_all x3, waiting for transfers between devices, shards(): lax.all_to_all(same_sent, 'lvl', split_axis=0, concat_axis=0, tiled=True)  235 us
    all_to_all x3, waiting for transfers between devices, shards(): lax.all_to_all(prior_sent, 'lvl', split_axis=0, concat_axis=0, tiled=True)  95.6 us
    gather x6, local copies, waits for them, and re-layouts, shards(): same_got.reshape(-1, block_rows, realize)  34.8 us
    all_gather x1, blocking collectives, shards(): lax.all_gather(parents, 'lvl', axis=1, tiled=True)  29.5 us
    gather x6, local copies, waits for them, and re-layouts, fill_slots(): rows = held_blocks[jnp.maximum(picked, 0)]  29 us
    gather x6, local copies, waits for them, and re-layouts, shards(): crossed.reshape(-1, block_rows, realize)  27.8 us
    all_to_all x3, starting transfers between devices, shards(): lax.all_to_all(prior_sent, 'lvl', split_axis=0, concat_axis=0, tiled=True)  27 us
    dot_general x3, matrix products, shards(): jnp.einsum('ksij,ksjr->kir', factors[section - 1], parent_vals, preferred...  21.5 us
  transfers between devices with their start and end apart: 10, of which 6 were waited for; matrix products, arithmetic and copies ran while one was open for 16% of the time, Pallas kernels for 0%

commit v1 on v0

v1 whole, which is shorter than its diff:
```python
import functools

import jax
import jax.numpy as jnp
from jax import lax
from jax.experimental import pallas as pl
from jax.experimental.pallas import tpu as pltpu
from jax.sharding import PartitionSpec as P

CAP = 2
CAPX = 1
COLS = 4
HALVES = 2
ANY = pl.BlockSpec(memory_space=pl.ANY)


def params(mib):
    return pltpu.CompilerParams(vmem_limit_bytes=mib * 1024 * 1024)


def first_level(chol, noise, out, half):
    depth, blocks, rows, _ = chol.shape
    width = noise.shape[3] // HALVES

    def body(*refs):
        lower, draws, latest, full = refs[0], refs[1], refs[-2], refs[-1]
        value = jnp.dot(lower[0, 0], draws[0, 0], preferred_element_type=jnp.float32)
        value = value.astype(jnp.bfloat16)
        latest[0] = value
        full[0, 0] = value

    carried = [] if out is None else [out]
    return pl.pallas_call(
        body,
        grid=(blocks,),
        in_specs=[
            pl.BlockSpec((1, 1, rows, rows), lambda b: (0, b, 0, 0)),
            pl.BlockSpec((1, 1, rows, width), lambda b: (0, b, 0, half)),
        ]
        + [ANY] * len(carried),
        out_specs=[
            pl.BlockSpec((1, rows, width), lambda b: (b, 0, 0)),
            pl.BlockSpec((1, 1, rows, width), lambda b: (0, b, 0, half)),
        ],
        out_shape=[
            jax.ShapeDtypeStruct((blocks, rows, width), jnp.bfloat16),
            jax.ShapeDtypeStruct(noise.shape, jnp.bfloat16),
        ],
        input_output_aliases={2: 1} if carried else {},
        compiler_params=params(16),
        cost_estimate=pl.CostEstimate(
            flops=2 * blocks * rows * rows * width, bytes_accessed=4_000_000, transcendentals=0
        ),
        name=f"first_{half}",
    )(chol, noise, *carried)


def pick_payload(table, on_middle, fresh, pool, section):
    own, near, mid, far, mid_relay, far_relay = fresh
    blocks, rows, width = own.shape
    same_slots, prior_slots = COLS * CAP, COLS * CAPX
    total = COLS * (same_slots + prior_slots)
    level = section - 1
    has_pool = pool is not None

    def body(tbl, flag, own, near, mid, far, mid_relay, far_relay, *rest):
        rest = rest[1:] if has_pool else rest
        held = rest[0]
        same, prior = rest[1 : 1 + COLS], rest[1 + COLS : 1 + 2 * COLS]
        sems, put_sems = rest[1 + 2 * COLS :]

        def put(source, place):
            return pltpu.make_async_copy(source, held.at[level, place], put_sems.at[place])

        put(own, 0).start()
        put(near, 1).start()

        @pl.when(flag[0] == 1)
        def _():
            put(mid_relay, 2).start()
            put(mid, 3).start()

        @pl.when(flag[0] != 1)
        def _():
            put(far, 2).start()
            put(far_relay, 3).start()

        for place in range(4):
            put(own, place).wait()

        def slot_copy(slot):
            if slot < COLS * same_slots:
                target = same[slot // same_slots].at[slot % same_slots]
            else:
                left = slot - COLS * same_slots
                target = prior[left // prior_slots].at[left % prior_slots]
            where = jnp.maximum(tbl[slot], 0)
            source = held.at[where // (4 * blocks), (where // blocks) % 4, where % blocks]
            return pltpu.make_async_copy(source, target, sems.at[slot])

        for slot in range(total):

            @pl.when(tbl[slot] >= 0)
            def _():
                slot_copy(slot).start()

        for slot in range(total):

            @pl.when(tbl[slot] >= 0)
            def _():
                slot_copy(slot).wait()

    pool_shape = (3, 4, blocks, rows, width)
    carried = [pool] if has_pool else []
    out = pl.pallas_call(
        body,
        in_specs=[pl.BlockSpec(memory_space=pltpu.SMEM)] * 2 + [ANY] * (6 + len(carried)),
        out_specs=[ANY] * (1 + 2 * COLS),
        out_shape=[jax.ShapeDtypeStruct(pool_shape, jnp.bfloat16)]
        + [jax.ShapeDtypeStruct((same_slots, rows, width), jnp.bfloat16)] * COLS
        + [jax.ShapeDtypeStruct((prior_slots, rows, width), jnp.bfloat16)] * COLS,
        scratch_shapes=[pltpu.SemaphoreType.DMA((total,)), pltpu.SemaphoreType.DMA((4,))],
        input_output_aliases={8: 0} if has_pool else {},
        compiler_params=params(16),
        cost_estimate=pl.CostEstimate(flops=0, bytes_accessed=10_000_000, transcendentals=0),
        name=f"pick_{section}",
    )(table, on_middle, *fresh, *carried)
    return out[0], out[1 : 1 + COLS], out[1 + COLS :]


def next_level(places, factors, chol, noise, got, out, section, half):
    depth, blocks, rows, _ = chol.shape
    slots = factors.shape[2]
    width = noise.shape[3] // HALVES
    sizes = [ref.shape[0] for ref in got]
    starts = [sum(sizes[:i]) for i in range(len(sizes))]

    def body(tbl, mats, lower, draws, *rest):
        got = rest[: len(sizes)]
        latest, full, held, sems = rest[len(sizes) + 1 :]
        block = pl.program_id(0)

        def fetch(i):
            return pltpu.make_async_copy(
                got[i], held.at[pl.ds(starts[i], sizes[i])], sems.at[i]
            )

        @pl.when(block == 0)
        def _():
            for i in range(len(sizes)):
                fetch(i).start()

        total = jnp.dot(lower[0, 0], draws[0, 0], preferred_element_type=jnp.float32)

        @pl.when(block == 0)
        def _():
            for i in range(len(sizes)):
                fetch(i).wait()

        for j in range(slots):
            place = tbl[block * slots + j]
            parent = held[jnp.maximum(place, 0)]
            parent = jnp.where(place >= 0, parent, jnp.zeros_like(parent))
            total += jnp.dot(mats[0, 0, j], parent, preferred_element_type=jnp.float32)
        value = total.astype(jnp.bfloat16)
        latest[0] = value
        full[0, 0] = value

    n_got = len(sizes)
    return pl.pallas_call(
        body,
        grid=(blocks,),
        in_specs=[
            pl.BlockSpec(memory_space=pltpu.SMEM),
            pl.BlockSpec((1, 1, slots, rows, rows), lambda b: (section - 1, b, 0, 0, 0)),
            pl.BlockSpec((1, 1, rows, rows), lambda b: (section, b, 0, 0)),
            pl.BlockSpec((1, 1, rows, width), lambda b: (section, b, 0, half)),
        ]
        + [ANY] * (n_got + 1),
        out_specs=[
            pl.BlockSpec((1, rows, width), lambda b: (b, 0, 0)),
            pl.BlockSpec((1, 1, rows, width), lambda b: (section, b, 0, half)),
        ],
        out_shape=[
            jax.ShapeDtypeStruct((blocks, rows, width), jnp.bfloat16),
            jax.ShapeDtypeStruct(noise.shape, jnp.bfloat16),
        ],
        scratch_shapes=[
            pltpu.VMEM((sum(sizes), rows, width), jnp.bfloat16),
            pltpu.SemaphoreType.DMA((n_got,)),
        ],
        input_output_aliases={4 + n_got: 1},
        compiler_params=params(24),
        cost_estimate=pl.CostEstimate(
            flops=2 * (slots + 1) * blocks * rows * rows * width,
            bytes_accessed=10_000_000,
            transcendentals=0,
        ),
        name=f"level_{section}_{half}",
    )(places, factors, chol, noise, *got, out)


def ranks(active, lane):
    count = lane.shape[-1]
    earlier = jnp.arange(count)[:, None] > jnp.arange(count)[None, :]
    alike = (lane[..., :, None] == lane[..., None, :]) & active[..., None, :] & earlier
    return jnp.sum(alike.astype(jnp.int32), axis=-1)


def tables(parents, total_blocks, local_blocks, peer_count, tile_count):
    sections = parents.shape[0]
    own_lane, own_tile = lax.axis_index("lvl"), lax.axis_index("tile")
    own_z, own_col = own_lane // COLS, own_lane % COLS
    mine = parents.reshape(sections, -1)
    onward = lax.ppermute(
        mine,
        "tile",
        [(t + 1, t) for t in range(tile_count - 1)],
    )
    onward = jnp.where(own_tile + 1 < tile_count, onward, -1)
    pair = jnp.stack([mine, onward])
    lists = jnp.stack([pair] + [lax.ppermute(pair, "lvl", across(k, peer_count)) for k in (1, 2, 3)])

    def decode(ids):
        clipped = jnp.maximum(ids, 0)
        level, block = clipped // total_blocks, clipped % total_blocks
        dev = block // local_blocks
        return ids >= 0, level, dev // peer_count, dev % peer_count, block % local_blocks

    valid, level, tile, lane, within = decode(lists)
    active = valid & (tile == own_tile) & (lane % COLS == own_col)
    rank = ranks(active, lane)
    slot = (lane // COLS) * CAP + jnp.minimum(rank, CAP - 1)
    source = (level * 4 + ((lane // COLS) ^ own_z)) * local_blocks + within
    hits = active[..., None] & (slot[..., None] == jnp.arange(COLS * CAP))
    table = jnp.sum(jnp.where(hits, source[..., None] + 1, 0), axis=-2) - 1
    same = table[:, 0]
    prior = table[:, 1, :, ::CAP]
    sends = jnp.concatenate(
        [
            same.transpose(1, 0, 2).reshape(sections, -1),
            prior.transpose(1, 0, 2).reshape(sections, -1),
        ],
        axis=1,
    )
    valid, level, tile, lane, within = decode(mine)
    from_prior = tile != own_tile
    rank = ranks(valid, lane + peer_count * from_prior.astype(jnp.int32))
    apart = (lane % COLS) ^ own_col
    zed = lane // COLS
    place = jnp.where(
        from_prior,
        COLS * COLS * CAP + apart * COLS * CAPX + zed,
        apart * COLS * CAP + zed * CAP + jnp.minimum(rank, CAP - 1),
    )
    return sends, jnp.where(valid, place, -1)


def across(k, peer_count):
    return [(lane, lane ^ k) for lane in range(peer_count)]


def along(links):
    return [(COLS * a + c, COLS * b + c) for a, b in links for c in range(COLS)]


def spread_z(latest):
    send = functools.partial(lax.ppermute, axis_name="lvl")
    near = send(latest, perm=along([(0, 1), (1, 0), (2, 3), (3, 2)]))
    mid = send(latest, perm=along([(1, 2), (2, 1)]))
    mid_relay = send(near, perm=along([(1, 2), (2, 1)]))
    far = send(mid, perm=along([(1, 0), (2, 3)]))
    far_relay = send(mid_relay, perm=along([(1, 0), (2, 3)]))
    return latest, near, mid, far, mid_relay, far_relay


def swap_plane(same, prior, peer_count, tile_count):
    got = [same[0]]
    for k in (1, 2, 3):
        got.append(lax.ppermute(same[k], "lvl", across(k, peer_count)))
    for k in (0, 1, 2, 3):
        links = [
            (t * peer_count + a, (t + 1) * peer_count + b)
            for t in range(tile_count - 1)
            for a, b in across(k, peer_count)
        ]
        got.append(lax.ppermute(prior[k], ("tile", "lvl"), links))
    return got


def shards(parents, factors, chol, noise):
    peer_count = lax.axis_size("lvl")
    tile_count = lax.axis_size("tile")
    depth, local_blocks = chol.shape[:2]
    total_blocks = local_blocks * peer_count * tile_count
    out = None
    latest, pools = [None] * HALVES, [None] * HALVES
    for half in range(HALVES):
        latest[half], out = first_level(chol, noise, out, half)
    sends, places = tables(parents, total_blocks, local_blocks, peer_count, tile_count)
    own_z = lax.axis_index("lvl") // COLS
    on_middle = ((own_z == 1) | (own_z == 2)).astype(jnp.int32).reshape(1)
    for section in range(1, depth):
        for half in range(HALVES):
            fresh = spread_z(latest[half])
            pools[half], same, prior = pick_payload(
                sends[section - 1], on_middle, fresh, pools[half], section
            )
            got = swap_plane(same, prior, peer_count, tile_count)
            latest[half], out = next_level(
                places[section - 1], factors, chol, noise, got, out, section, half
            )
    return out


def solution(mesh):
    placed = (
        P(None, ("tile", "lvl"), None),
        P(None, ("tile", "lvl"), None, None, None),
        P(None, ("tile", "lvl"), None, None),
        P(None, ("tile", "lvl"), None, None),
    )
    return jax.shard_map(
        shards,
        mesh=mesh,
        in_specs=placed,
        out_specs=P(None, ("tile", "lvl"), None, None),
        check_vma=False,
    )
```

time: 589 us -> 441 us (0.75)
  the two profiles are of different devices: /device:TPU:14 before, /device:TPU:1 now
where the time goes in v1:
time: 441 us; the launch traced here: 439 us
  waiting for transfers between devices  262 us (59%)
  starting transfers between devices  85.9 us (19%)
  Pallas kernels  62.1 us (14%)
  local copies, waits for them, and re-layouts  26.5 us (6%)
    ppermute x24, waiting for transfers between devices, swap_plane(): got.append(lax.ppermute(prior[k], ('tile', 'lvl'), links))  109 us
    ppermute x6, waiting for transfers between devices, spread_z(): far_relay = send(mid_relay, perm=along([(1, 0), (2, 3)]))  62 us
    ppermute x6, waiting for transfers between devices, spread_z(): near = send(latest, perm=along([(0, 1), (1, 0), (2, 3), (3, 2)]))  48 us
    ppermute x6, waiting for transfers between devices, spread_z(): far = send(mid, perm=along([(1, 0), (2, 3)]))  34 us
    pallas_call x6, Pallas kernels, next_level(): pl.pallas_call(body, grid=(blocks,), in_specs=[pl.BlockSpec(memory_space=...  31.9 us
    ppermute x24, starting transfers between devices, swap_plane(): got.append(lax.ppermute(prior[k], ('tile', 'lvl'), links))  30.9 us
    unnamed x39, local copies, waits for them, and re-layouts  25.8 us
    pallas_call x6, Pallas kernels, pick_payload(): pl.pallas_call(body, in_specs=[pl.BlockSpec(memory_space=pltpu.SMEM)] * 2...  23.1 us
  transfers between devices with their start and end apart: 76, of which 28 were waited for; matrix products, arithmetic and copies ran while one was open for 1% of the time, Pallas kernels for 13%

profile of v1, /device:TPU:1, one launch (start us, length us, event | category | flops | bytes accessed | tf_op | source)
XLA Modules:
  0.0 439.3 jit_solution(17978243096727507861)
XLA Ops:
  0.9 2.0 collective-permute-start
  2.8 2.2 copy-done.1
  5.0 2.2 copy-done.3
  7.2 3.5 first_0.1
  10.7 3.6 first_1.1
  14.3 2.7 collective-permute-start.4
  23.3 16.9 %collective-permute-done.16.near = bf16[8,256,128]{2,1,0:T(8,128)(2,1)S(1)} collective-permute-done((bf16[8,256,128]{2,1,0:T(8,128)(2,1)S(1)}, bf16[8,256,128]{2,1,0:T(8,128)(2,1)S(1)}, u32[]{:S(2)}, u32[]{:S(2)}) %collective-permute-start.16) | collective-permute-done | bytes 524320 | tf_op jit(solution)/shard_map/ppermute | solution.py:269
  51.4 11.5 %collective-permute-done.18.far = bf16[8,256,128]{2,1,0:T(8,128)(2,1)} collective-permute-done((bf16[8,256,128]{2,1,0:T(8,128)(2,1)}, bf16[8,256,128]{2,1,0:T(8,128)(2,1)}, u32[]{:S(2)}, u32[]{:S(2)}) %collective-permute-start.18) | collective-permute-done | bytes 524320 | tf_op jit(solution)/shard_map/ppermute | solution.py:272
  62.9 11.2 %collective-permute-done.20.far_relay = bf16[8,256,128]{2,1,0:T(8,128)(2,1)} collective-permute-done((bf16[8,256,128]{2,1,0:T(8,128)(2,1)}, bf16[8,256,128]{2,1,0:T(8,128)(2,1)}, u32[]{:S(2)}, u32[]{:S(2)}) %collective-permute-start.20) | collective-permute-done | bytes 524320 | tf_op jit(solution)/shard_map/ppermute | solution.py:273
  76.1 4.2 pick_1.3
  80.3 2.6 copy-done.8
  87.9 8.5 %collective-permute-done.8.far_relay = bf16[8,256,128]{2,1,0:T(8,128)(2,1)S(1)} collective-permute-done((bf16[8,256,128]{2,1,0:T(8,128)(2,1)}, bf16[8,256,128]{2,1,0:T(8,128)(2,1)S(1)}, u32[]{:S(2)}, u32[]{:S(2)}) %collective-permute-start.8) | collective-permute-done | bytes 524320 | tf_op jit(solution)/shard_map/ppermute | solution.py:273
  97.7 4.1 pick_1.2
  101.8 2.7 copy-done.6
  107.1 2.1 collective-permute-start.22
  111.4 6.7 %collective-permute-done.13.rest_5_ = bf16[4,256,128]{2,1,0:T(8,128)(2,1)S(1)} collective-permute-done((bf16[4,256,128]{2,1,0:T(8,128)(2,1)S(1)}, bf16[4,256,128]{2,1,0:T(8,128)(2,1)S(1)}, u32[]{:S(2)}, u32[]{:S(2)}) %collective-permute-start.13) | collective-permute-done | bytes 262176 | tf_op jit(solution)/shard_map/ppermute | solution.py:287
  118.7 2.7 collective-permute-start.11
  121.7 8.6 %collective-permute-done.22.rest_2_ = bf16[8,256,128]{2,1,0:T(8,128)(2,1)S(1)} collective-permute-done((bf16[8,256,128]{2,1,0:T(8,128)(2,1)S(1)}, bf16[8,256,128]{2,1,0:T(8,128)(2,1)S(1)}, u32[]{:S(2)}, u32[]{:S(2)}) %collective-permute-start.22) | collective-permute-done | bytes 524320 | tf_op jit(solution)/shard_map/ppermute | solution.py:280
  133.0 4.6 %copy-done = bf16[3,8,4,256,256]{4,3,2,1,0:T(8,128)(2,1)S(1)} copy-done((bf16[3,8,4,256,256]{4,3,2,1,0:T(8,128)(2,1)S(1)}, bf16[3,8,4,256,256]{4,3,2,1,0:T(8,128)(2,1)}, u32[]{:S(2)}) %copy-start) | copy-done | bytes 12582936
  137.5 2.2 copy-done.4
  139.7 5.3 %level_1_0.1 = (bf16[8,256,128]{2,1,0:T(8,128)(2,1)S(1)}, bf16[4,8,256,256]{3,2,1,0:T(8,128)(2,1)}) custom-call(s32[32]{0:T(128)S(1)} %get-tuple-element.146.tbl, bf16[3,8,4,256,256]{4,3,2,1,0:T(8,128)(2,1)S(1)} %copy-done, bf16[4,8,256,256]{3,2,1,0:T(8,128)(2,1)S(1)} %copy-done.2, ...), custom_call_target="tpu_custom_call", output_to_operand_aliasing={{1}: (12, {})} | custom-call | flops 671088640 | bytes 10000000 | tf_op jit(solution)/shard_map/level_1_0/pallas_call | solution.py:170
  145.0 15.7 %collective-permute-done.14.rest_6_ = bf16[4,256,128]{2,1,0:T(8,128)(2,1)S(1)} collective-permute-done((bf16[4,256,128]{2,1,0:T(8,128)(2,1)S(1)}, bf16[4,256,128]{2,1,0:T(8,128)(2,1)S(1)}, u32[]{:S(2)}, u32[]{:S(2)}) %collective-permute-start.14) | collective-permute-done | bytes 262176 | tf_op jit(solution)/shard_map/ppermute | solution.py:287
  160.7 5.3 %level_1_1.1 = (bf16[8,256,128]{2,1,0:T(8,128)(2,1)S(1)}, bf16[4,8,256,256]{3,2,1,0:T(8,128)(2,1)}) custom-call(s32[32]{0:T(128)S(1)} %get-tuple-element.146.tbl, bf16[3,8,4,256,256]{4,3,2,1,0:T(8,128)(2,1)S(1)} %copy-done, bf16[4,8,256,256]{3,2,1,0:T(8,128)(2,1)S(1)} %copy-done.2, ...), custom_call_target="tpu_custom_call", output_to_operand_aliasing={{1}: (12, {})} | custom-call | flops 671088640 | bytes 10000000 | tf_op jit(solution)/shard_map/level_1_1/pallas_call | solution.py:170
  168.3 6.1 %collective-permute-done.40.near = bf16[8,256,128]{2,1,0:T(8,128)(2,1)S(1)} collective-permute-done((bf16[8,256,128]{2,1,0:T(8,128)(2,1)S(1)}, bf16[8,256,128]{2,1,0:T(8,128)(2,1)S(1)}, u32[]{:S(2)}, u32[]{:S(2)}) %collective-permute-start.40) | collective-permute-done | bytes 524320 | tf_op jit(solution)/shard_map/ppermute | solution.py:269
  175.7 9.8 %collective-permute-done.28.near = bf16[8,256,128]{2,1,0:T(8,128)(2,1)S(1)} collective-permute-done((bf16[8,256,128]{2,1,0:T(8,128)(2,1)S(1)}, bf16[8,256,128]{2,1,0:T(8,128)(2,1)S(1)}, u32[]{:S(2)}, u32[]{:S(2)}) %collective-permute-start.28) | collective-permute-done | bytes 524320 | tf_op jit(solution)/shard_map/ppermute | solution.py:269
  191.5 10.6 %collective-permute-done.42.far = bf16[8,256,128]{2,1,0:T(8,128)(2,1)S(1)} collective-permute-done((bf16[8,256,128]{2,1,0:T(8,128)(2,1)S(1)}, bf16[8,256,128]{2,1,0:T(8,128)(2,1)S(1)}, u32[]{:S(2)}, u32[]{:S(2)}) %collective-permute-start.42) | collective-permute-done | bytes 524320 | tf_op jit(solution)/shard_map/ppermute | solution.py:272
  202.0 11.2 %collective-permute-done.44.far_relay = bf16[8,256,128]{2,1,0:T(8,128)(2,1)S(1)} collective-permute-done((bf16[8,256,128]{2,1,0:T(8,128)(2,1)S(1)}, bf16[8,256,128]{2,1,0:T(8,128)(2,1)S(1)}, u32[]{:S(2)}, u32[]{:S(2)}) %collective-permute-start.44) | collective-permute-done | bytes 524320 | tf_op jit(solution)/shard_map/ppermute | solution.py:273
  213.3 2.9 copy-done.9
  216.2 3.9 pick_2.3
  225.8 9.9 %collective-permute-done.32.far_relay = bf16[8,256,128]{2,1,0:T(8,128)(2,1)S(1)} collective-permute-done((bf16[8,256,128]{2,1,0:T(8,128)(2,1)S(1)}, bf16[8,256,128]{2,1,0:T(8,128)(2,1)S(1)}, u32[]{:S(2)}, u32[]{:S(2)}) %collective-permute-start.32) | collective-permute-done | bytes 524320 | tf_op jit(solution)/shard_map/ppermute | solution.py:273
  235.8 4.1 pick_2.2
  244.9 2.3 collective-permute-done.36.rest_4_
  247.6 20.4 %collective-permute-done.37.rest_5_ = bf16[4,256,128]{2,1,0:T(8,128)(2,1)S(1)} collective-permute-done((bf16[4,256,128]{2,1,0:T(8,128)(2,1)S(1)}, bf16[4,256,128]{2,1,0:T(8,128)(2,1)S(1)}, u32[]{:S(2)}, u32[]{:S(2)}) %collective-permute-start.37) | collective-permute-done | bytes 262176 | tf_op jit(solution)/shard_map/ppermute | solution.py:287
  272.2 5.3 %level_2_0.1 = (bf16[8,256,128]{2,1,0:T(8,128)(2,1)S(1)}, bf16[4,8,256,256]{3,2,1,0:T(8,128)(2,1)}) custom-call(s32[32]{0:T(128)S(1)} %get-tuple-element.147.tbl, bf16[3,8,4,256,256]{4,3,2,1,0:T(8,128)(2,1)S(1)} %bitcast.31, bf16[4,8,256,256]{3,2,1,0:T(8,128)(2,1)S(1)} %copy-done.2, ...), custom_call_target="tpu_custom_call", output_to_operand_aliasing={{1}: (12, {})} | custom-call | flops 671088640 | bytes 10000000 | tf_op jit(solution)/shard_map/level_2_0/pallas_call | solution.py:170
  277.5 20.3 %collective-permute-done.38.rest_6_ = bf16[4,256,128]{2,1,0:T(8,128)(2,1)S(1)} collective-permute-done((bf16[4,256,128]{2,1,0:T(8,128)(2,1)S(1)}, bf16[4,256,128]{2,1,0:T(8,128)(2,1)S(1)}, u32[]{:S(2)}, u32[]{:S(2)}) %collective-permute-start.38) | collective-permute-done | bytes 262176 | tf_op jit(solution)/shard_map/ppermute | solution.py:287
  297.9 5.3 %level_2_1.1 = (bf16[8,256,128]{2,1,0:T(8,128)(2,1)S(1)}, bf16[4,8,256,256]{3,2,1,0:T(8,128)(2,1)}) custom-call(s32[32]{0:T(128)S(1)} %get-tuple-element.147.tbl, bf16[3,8,4,256,256]{4,3,2,1,0:T(8,128)(2,1)S(1)} %bitcast.31, bf16[4,8,256,256]{3,2,1,0:T(8,128)(2,1)S(1)} %copy-done.2, ...), custom_call_target="tpu_custom_call", output_to_operand_aliasing={{1}: (12, {})} | custom-call | flops 671088640 | bytes 10000000 | tf_op jit(solution)/shard_map/level_2_1/pallas_call | solution.py:170
  305.4 6.4 %collective-permute-done.64.near = bf16[8,256,128]{2,1,0:T(8,128)(2,1)S(1)} collective-permute-done((bf16[8,256,128]{2,1,0:T(8,128)(2,1)S(1)}, bf16[8,256,128]{2,1,0:T(8,128)(2,1)S(1)}, u32[]{:S(2)}, u32[]{:S(2)}) %collective-permute-start.64) | collective-permute-done | bytes 524320 | tf_op jit(solution)/shard_map/ppermute | solution.py:269
  313.1 8.8 %collective-permute-done.52.near = bf16[8,256,128]{2,1,0:T(8,128)(2,1)S(1)} collective-permute-done((bf16[8,256,128]{2,1,0:T(8,128)(2,1)S(1)}, bf16[8,256,128]{2,1,0:T(8,128)(2,1)S(1)}, u32[]{:S(2)}, u32[]{:S(2)}) %collective-permute-start.52) | collective-permute-done | bytes 524320 | tf_op jit(solution)/shard_map/ppermute | solution.py:269
  327.8 10.3 %collective-permute-done.66.far = bf16[8,256,128]{2,1,0:T(8,128)(2,1)S(1)} collective-permute-done((bf16[8,256,128]{2,1,0:T(8,128)(2,1)S(1)}, bf16[8,256,128]{2,1,0:T(8,128)(2,1)S(1)}, u32[]{:S(2)}, u32[]{:S(2)}) %collective-permute-start.66) | collective-permute-done | bytes 524320 | tf_op jit(solution)/shard_map/ppermute | solution.py:272
  338.2 11.2 %collective-permute-done.68.far_relay = bf16[8,256,128]{2,1,0:T(8,128)(2,1)S(1)} collective-permute-done((bf16[8,256,128]{2,1,0:T(8,128)(2,1)S(1)}, bf16[8,256,128]{2,1,0:T(8,128)(2,1)S(1)}, u32[]{:S(2)}, u32[]{:S(2)}) %collective-permute-start.68) | collective-permute-done | bytes 524320 | tf_op jit(solution)/shard_map/ppermute | solution.py:273
  349.4 2.8 copy-done.11
  352.2 3.5 pick_3.3
  361.9 9.9 %collective-permute-done.56.far_relay = bf16[8,256,128]{2,1,0:T(8,128)(2,1)S(1)} collective-permute-done((bf16[8,256,128]{2,1,0:T(8,128)(2,1)S(1)}, bf16[8,256,128]{2,1,0:T(8,128)(2,1)S(1)}, u32[]{:S(2)}, u32[]{:S(2)}) %collective-permute-start.56) | collective-permute-done | bytes 524320 | tf_op jit(solution)/shard_map/ppermute | solution.py:273
  372.9 3.5 pick_3.2
  383.6 20.0 %collective-permute-done.61.rest_5_ = bf16[4,256,128]{2,1,0:T(8,128)(2,1)S(1)} collective-permute-done((bf16[4,256,128]{2,1,0:T(8,128)(2,1)S(1)}, bf16[4,256,128]{2,1,0:T(8,128)(2,1)S(1)}, u32[]{:S(2)}, u32[]{:S(2)}) %collective-permute-start.61) | collective-permute-done | bytes 262176 | tf_op jit(solution)/shard_map/ppermute | solution.py:287
  408.0 5.4 %level_3_0.1 = (bf16[8,256,128]{2,1,0:T(8,128)(2,1)}, bf16[4,8,256,256]{3,2,1,0:T(8,128)(2,1)}) custom-call(s32[32]{0:T(128)S(1)} %get-tuple-element.148.tbl, bf16[3,8,4,256,256]{4,3,2,1,0:T(8,128)(2,1)S(1)} %bitcast.31, bf16[4,8,256,256]{3,2,1,0:T(8,128)(2,1)S(1)} %copy-done.2, ...), custom_call_target="tpu_custom_call", output_to_operand_aliasing={{1}: (12, {})} | custom-call | flops 671088640 | bytes 10000000 | tf_op jit(solution)/shard_map/level_3_0/pallas_call | solution.py:170
  413.4 20.3 %collective-permute-done.62.rest_6_ = bf16[4,256,128]{2,1,0:T(8,128)(2,1)S(1)} collective-permute-done((bf16[4,256,128]{2,1,0:T(8,128)(2,1)S(1)}, bf16[4,256,128]{2,1,0:T(8,128)(2,1)S(1)}, u32[]{:S(2)}, u32[]{:S(2)}) %collective-permute-start.62) | collective-permute-done | bytes 262176 | tf_op jit(solution)/shard_map/ppermute | solution.py:287
  433.7 5.4 %level_3_1.1 = (bf16[8,256,128]{2,1,0:T(8,128)(2,1)}, bf16[4,8,256,256]{3,2,1,0:T(8,128)(2,1)}) custom-call(s32[32]{0:T(128)S(1)} %get-tuple-element.148.tbl, bf16[3,8,4,256,256]{4,3,2,1,0:T(8,128)(2,1)S(1)} %bitcast.31, bf16[4,8,256,256]{3,2,1,0:T(8,128)(2,1)S(1)} %copy-done.2, ...), custom_call_target="tpu_custom_call", output_to_operand_aliasing={{1}: (12, {})} | custom-call | flops 671088640 | bytes 10000000 | tf_op jit(solution)/shard_map/level_3_1/pallas_call | solution.py:170
  (182 shorter events, 87.9 us)
Async XLA Ops:
  14.3 28.9 %collective-permute-start.4 = (bf16[8,256,128]{2,1,0:T(8,128)(2,1)}, bf16[8,256,128]{2,1,0:T(8,128)(2,1)}, u32[]{:S(2)}, u32[]{:S(2)}) collective-permute-start(bf16[8,256,128]{2,1,0:T(8,128)(2,1)} %get-tuple-element.72.own), channel_id=1, source_target_pairs={{0,4},{1,5},{2,6},{3,7},{4,0},{5,1},{6,2},{7,3},{8,12},{9,13},{10,... | collective-permute-start | bytes 1572872 | tf_op jit(solution)/shard_map/ppermute | solution.py:269
  17.0 23.2 %collective-permute-start.16 = (bf16[8,256,128]{2,1,0:T(8,128)(2,1)S(1)}, bf16[8,256,128]{2,1,0:T(8,128)(2,1)S(1)}, u32[]{:S(2)}, u32[]{:S(2)}) collective-permute-start(bf16[8,256,128]{2,1,0:T(8,128)(2,1)S(1)} %get-tuple-element.81.own), channel_id=1, source_target_pairs={{0,4},{1,5},{2,6},{3,7},{4,0},{5,1},{6,2},{7,3},{8,12},{9,13},{10,... | collective-permute-start | bytes 1572872 | tf_op jit(solution)/shard_map/ppermute | solution.py:269
  20.1 28.3 %collective-permute-start.5 = (bf16[8,256,128]{2,1,0:T(8,128)(2,1)}, bf16[8,256,128]{2,1,0:T(8,128)(2,1)}, u32[]{:S(2)}, u32[]{:S(2)}) collective-permute-start(bf16[8,256,128]{2,1,0:T(8,128)(2,1)} %get-tuple-element.72.own), channel_id=1, source_target_pairs={{4,8},{5,9},{6,10},{7,11},{8,4},{9,5},{10,6},{11,7},{20,24},{21,25... | collective-permute-start | bytes 1572872 | tf_op jit(solution)/shard_map/ppermute | solution.py:270
  21.6 23.6 %collective-permute-start.17 = (bf16[8,256,128]{2,1,0:T(8,128)(2,1)S(1)}, bf16[8,256,128]{2,1,0:T(8,128)(2,1)}, u32[]{:S(2)}, u32[]{:S(2)}) collective-permute-start(bf16[8,256,128]{2,1,0:T(8,128)(2,1)S(1)} %get-tuple-element.81.own), channel_id=1, source_target_pairs={{4,8},{5,9},{6,10},{7,11},{8,4},{9,5},{10,6},{11,7},{20,24},{21,25... | collective-permute-start | bytes 1572872 | tf_op jit(solution)/shard_map/ppermute | solution.py:270
  46.5 27.5 %collective-permute-start.20 = (bf16[8,256,128]{2,1,0:T(8,128)(2,1)}, bf16[8,256,128]{2,1,0:T(8,128)(2,1)}, u32[]{:S(2)}, u32[]{:S(2)}) collective-permute-start(bf16[8,256,128]{2,1,0:T(8,128)(2,1)} %collective-permute-done.19.mid_relay), channel_id=1, source_target_pairs={{4,0},{5,1},{6,2},{7,3},{8,12},{9,13},{10,14},{11,15},{20,16},{21,... | collective-permute-start | bytes 1572872 | tf_op jit(solution)/shard_map/ppermute | solution.py:273
  48.4 38.2 %collective-permute-start.6 = (bf16[8,256,128]{2,1,0:T(8,128)(2,1)}, bf16[8,256,128]{2,1,0:T(8,128)(2,1)S(1)}, u32[]{:S(2)}, u32[]{:S(2)}) collective-permute-start(bf16[8,256,128]{2,1,0:T(8,128)(2,1)} %collective-permute-done.5.mid), channel_id=1, source_target_pairs={{4,0},{5,1},{6,2},{7,3},{8,12},{9,13},{10,14},{11,15},{20,16},{21,... | collective-permute-start | bytes 1572872 | tf_op jit(solution)/shard_map/ppermute | solution.py:272
  50.0 46.4 %collective-permute-start.8 = (bf16[8,256,128]{2,1,0:T(8,128)(2,1)}, bf16[8,256,128]{2,1,0:T(8,128)(2,1)S(1)}, u32[]{:S(2)}, u32[]{:S(2)}) collective-permute-start(bf16[8,256,128]{2,1,0:T(8,128)(2,1)} %collective-permute-done.7.mid_relay), channel_id=1, source_target_pairs={{4,0},{5,1},{6,2},{7,3},{8,12},{9,13},{10,14},{11,15},{20,16},{21,... | collective-permute-start | bytes 1572872 | tf_op jit(solution)/shard_map/ppermute | solution.py:273
  82.8 21.6 %collective-permute-start.24 = (bf16[4,256,128]{2,1,0:T(8,128)(2,1)S(1)}, bf16[4,256,128]{2,1,0:T(8,128)(2,1)S(1)}, u32[]{:S(2)}, u32[]{:S(2)}) collective-permute-start(bf16[4,256,128]{2,1,0:T(8,128)(2,1)S(1)} %get-tuple-element.86), channel_id=1, source_target_pairs={{0,16},{1,17},{2,18},{3,19},{4,20},{5,21},{6,22},{7,23},{8,24},{9,... | collective-permute-start | bytes 786440 | tf_op jit(solution)/shard_map/ppermute | solution.py:287
  84.1 21.6 %collective-permute-start.25 = (bf16[4,256,128]{2,1,0:T(8,128)(2,1)S(1)}, bf16[4,256,128]{2,1,0:T(8,128)(2,1)S(1)}, u32[]{:S(2)}, u32[]{:S(2)}) collective-permute-start(bf16[4,256,128]{2,1,0:T(8,128)(2,1)S(1)} %get-tuple-element.87), channel_id=1, source_target_pairs={{0,17},{1,16},{2,19},{3,18},{4,21},{5,20},{6,23},{7,22},{8,25},{9,... | collective-permute-start | bytes 786440 | tf_op jit(solution)/shard_map/ppermute | solution.py:287
  85.4 33.3 %collective-permute-start.21 = (bf16[8,256,128]{2,1,0:T(8,128)(2,1)S(1)}, bf16[8,256,128]{2,1,0:T(8,128)(2,1)S(1)}, u32[]{:S(2)}, u32[]{:S(2)}) collective-permute-start(bf16[8,256,128]{2,1,0:T(8,128)(2,1)S(1)} %get-tuple-element.83), channel_id=1, source_target_pairs={{0,1},{1,0},{2,3},{3,2},{4,5},{5,4},{6,7},{7,6},{8,9},{9,8},{10,11... | collective-permute-start | bytes 1572872 | tf_op jit(solution)/shard_map/ppermute | solution.py:280
  86.6 20.5 %collective-permute-start.26 = (bf16[4,256,128]{2,1,0:T(8,128)(2,1)S(1)}, bf16[4,256,128]{2,1,0:T(8,128)(2,1)S(1)}, u32[]{:S(2)}, u32[]{:S(2)}) collective-permute-start(bf16[4,256,128]{2,1,0:T(8,128)(2,1)S(1)} %get-tuple-element.88), channel_id=1, source_target_pairs={{0,18},{1,19},{2,16},{3,17},{4,22},{5,23},{6,20},{7,21},{8,26},{9,... | collective-permute-start | bytes 786440 | tf_op jit(solution)/shard_map/ppermute | solution.py:287
  107.1 23.2 %collective-permute-start.22 = (bf16[8,256,128]{2,1,0:T(8,128)(2,1)S(1)}, bf16[8,256,128]{2,1,0:T(8,128)(2,1)S(1)}, u32[]{:S(2)}, u32[]{:S(2)}) collective-permute-start(bf16[8,256,128]{2,1,0:T(8,128)(2,1)S(1)} %get-tuple-element.84), channel_id=1, source_target_pairs={{0,2},{1,3},{2,0},{3,1},{4,6},{5,7},{6,4},{7,5},{8,10},{9,11},{10,... | collective-permute-start | bytes 1572872 | tf_op jit(solution)/shard_map/ppermute | solution.py:280
  109.2 22.4 %collective-permute-start.23 = (bf16[8,256,128]{2,1,0:T(8,128)(2,1)S(1)}, bf16[8,256,128]{2,1,0:T(8,128)(2,1)S(1)}, u32[]{:S(2)}, u32[]{:S(2)}) collective-permute-start(bf16[8,256,128]{2,1,0:T(8,128)(2,1)S(1)} %get-tuple-element.85), channel_id=1, source_target_pairs={{0,3},{1,2},{2,1},{3,0},{4,7},{5,6},{6,5},{7,4},{8,11},{9,10},{10,... | collective-permute-start | bytes 1572872 | tf_op jit(solution)/shard_map/ppermute | solution.py:280
  111.4 49.3 %collective-permute-start.9 = (bf16[8,256,128]{2,1,0:T(8,128)(2,1)S(1)}, bf16[8,256,128]{2,1,0:T(8,128)(2,1)S(1)}, u32[]{:S(2)}, u32[]{:S(2)}) collective-permute-start(bf16[8,256,128]{2,1,0:T(8,128)(2,1)S(1)} %get-tuple-element.74), channel_id=1, source_target_pairs={{0,1},{1,0},{2,3},{3,2},{4,5},{5,4},{6,7},{7,6},{8,9},{9,8},{10,11... | collective-permute-start | bytes 1572872 | tf_op jit(solution)/shard_map/ppermute | solution.py:280
  118.1 42.6 %collective-permute-start.10 = (bf16[8,256,128]{2,1,0:T(8,128)(2,1)S(1)}, bf16[8,256,128]{2,1,0:T(8,128)(2,1)S(1)}, u32[]{:S(2)}, u32[]{:S(2)}) collective-permute-start(bf16[8,256,128]{2,1,0:T(8,128)(2,1)S(1)} %get-tuple-element.75), channel_id=1, source_target_pairs={{0,2},{1,3},{2,0},{3,1},{4,6},{5,7},{6,4},{7,5},{8,10},{9,11},{10,... | collective-permute-start | bytes 1572872 | tf_op jit(solution)/shard_map/ppermute | solution.py:280
  118.7 42.0 %collective-permute-start.11 = (bf16[8,256,128]{2,1,0:T(8,128)(2,1)S(1)}, bf16[8,256,128]{2,1,0:T(8,128)(2,1)S(1)}, u32[]{:S(2)}, u32[]{:S(2)}) collective-permute-start(bf16[8,256,128]{2,1,0:T(8,128)(2,1)S(1)} %get-tuple-element.76), channel_id=1, source_target_pairs={{0,3},{1,2},{2,1},{3,0},{4,7},{5,6},{6,5},{7,4},{8,11},{9,10},{10,... | collective-permute-start | bytes 1572872 | tf_op jit(solution)/shard_map/ppermute | solution.py:280
  130.3 30.4 %collective-permute-start.14 = (bf16[4,256,128]{2,1,0:T(8,128)(2,1)S(1)}, bf16[4,256,128]{2,1,0:T(8,128)(2,1)S(1)}, u32[]{:S(2)}, u32[]{:S(2)}) collective-permute-start(bf16[4,256,128]{2,1,0:T(8,128)(2,1)S(1)} %get-tuple-element.79), channel_id=1, source_target_pairs={{0,18},{1,19},{2,16},{3,17},{4,22},{5,23},{6,20},{7,21},{8,26},{9,... | collective-permute-start | bytes 786440 | tf_op jit(solution)/shard_map/ppermute | solution.py:287
  131.6 29.1 %collective-permute-start.15 = (bf16[4,256,128]{2,1,0:T(8,128)(2,1)S(1)}, bf16[4,256,128]{2,1,0:T(8,128)(2,1)S(1)}, u32[]{:S(2)}, u32[]{:S(2)}) collective-permute-start(bf16[4,256,128]{2,1,0:T(8,128)(2,1)S(1)} %get-tuple-element.80), channel_id=1, source_target_pairs={{0,19},{1,18},{2,17},{3,16},{4,23},{5,22},{6,21},{7,20},{8,27},{9,... | collective-permute-start | bytes 786440 | tf_op jit(solution)/shard_map/ppermute | solution.py:287
  166.0 19.5 %collective-permute-start.28 = (bf16[8,256,128]{2,1,0:T(8,128)(2,1)S(1)}, bf16[8,256,128]{2,1,0:T(8,128)(2,1)S(1)}, u32[]{:S(2)}, u32[]{:S(2)}) collective-permute-start(bf16[8,256,128]{2,1,0:T(8,128)(2,1)S(1)} %get-tuple-element.92.own), channel_id=1, source_target_pairs={{0,4},{1,5},{2,6},{3,7},{4,0},{5,1},{6,2},{7,3},{8,12},{9,13},{10,... | collective-permute-start | bytes 1572872 | tf_op jit(solution)/shard_map/ppermute | solution.py:269
  187.6 25.7 %collective-permute-start.44 = (bf16[8,256,128]{2,1,0:T(8,128)(2,1)S(1)}, bf16[8,256,128]{2,1,0:T(8,128)(2,1)S(1)}, u32[]{:S(2)}, u32[]{:S(2)}) collective-permute-start(bf16[8,256,128]{2,1,0:T(8,128)(2,1)S(1)} %collective-permute-done.43.mid_relay), channel_id=1, source_target_pairs={{4,0},{5,1},{6,2},{7,3},{8,12},{9,13},{10,14},{11,15},{20,16},{21,... | collective-permute-start | bytes 1572872 | tf_op jit(solution)/shard_map/ppermute | solution.py:273
  188.9 35.6 %collective-permute-start.30 = (bf16[8,256,128]{2,1,0:T(8,128)(2,1)S(1)}, bf16[8,256,128]{2,1,0:T(8,128)(2,1)S(1)}, u32[]{:S(2)}, u32[]{:S(2)}) collective-permute-start(bf16[8,256,128]{2,1,0:T(8,128)(2,1)S(1)} %collective-permute-done.29.mid), channel_id=1, source_target_pairs={{4,0},{5,1},{6,2},{7,3},{8,12},{9,13},{10,14},{11,15},{20,16},{21,... | collective-permute-start | bytes 1572872 | tf_op jit(solution)/shard_map/ppermute | solution.py:272
  190.2 45.6 %collective-permute-start.32 = (bf16[8,256,128]{2,1,0:T(8,128)(2,1)S(1)}, bf16[8,256,128]{2,1,0:T(8,128)(2,1)S(1)}, u32[]{:S(2)}, u32[]{:S(2)}) collective-permute-start(bf16[8,256,128]{2,1,0:T(8,128)(2,1)S(1)} %collective-permute-done.31.mid_relay), channel_id=1, source_target_pairs={{4,0},{5,1},{6,2},{7,3},{8,12},{9,13},{10,14},{11,15},{20,16},{21,... | collective-permute-start | bytes 1572872 | tf_op jit(solution)/shard_map/ppermute | solution.py:273
  220.1 19.7 %collective-permute-start.48 = (bf16[4,256,128]{2,1,0:T(8,128)(2,1)S(1)}, bf16[4,256,128]{2,1,0:T(8,128)(2,1)S(1)}, u32[]{:S(2)}, u32[]{:S(2)}) collective-permute-start(bf16[4,256,128]{2,1,0:T(8,128)(2,1)S(1)} %get-tuple-element.108), channel_id=1, source_target_pairs={{0,16},{1,17},{2,18},{3,19},{4,20},{5,21},{6,22},{7,23},{8,24},{9,... | collective-permute-start | bytes 786440 | tf_op jit(solution)/shard_map/ppermute | solution.py:287
  222.7 19.6 %collective-permute-start.50 = (bf16[4,256,128]{2,1,0:T(8,128)(2,1)S(1)}, bf16[4,256,128]{2,1,0:T(8,128)(2,1)S(1)}, u32[]{:S(2)}, u32[]{:S(2)}) collective-permute-start(bf16[4,256,128]{2,1,0:T(8,128)(2,1)S(1)} %get-tuple-element.110), channel_id=1, source_target_pairs={{0,18},{1,19},{2,16},{3,17},{4,22},{5,23},{6,20},{7,21},{8,26},{9,... | collective-permute-start | bytes 786440 | tf_op jit(solution)/shard_map/ppermute | solution.py:287
  235.7 32.3 %collective-permute-start.45 = (bf16[8,256,128]{2,1,0:T(8,128)(2,1)S(1)}, bf16[8,256,128]{2,1,0:T(8,128)(2,1)S(1)}, u32[]{:S(2)}, u32[]{:S(2)}) collective-permute-start(bf16[8,256,128]{2,1,0:T(8,128)(2,1)S(1)} %get-tuple-element.105), channel_id=1, source_target_pairs={{0,1},{1,0},{2,3},{3,2},{4,5},{5,4},{6,7},{7,6},{8,9},{9,8},{10,11... | collective-permute-start | bytes 1572872 | tf_op jit(solution)/shard_map/ppermute | solution.py:280
  239.8 29.7 %collective-permute-start.46 = (bf16[8,256,128]{2,1,0:T(8,128)(2,1)S(1)}, bf16[8,256,128]{2,1,0:T(8,128)(2,1)S(1)}, u32[]{:S(2)}, u32[]{:S(2)}) collective-permute-start(bf16[8,256,128]{2,1,0:T(8,128)(2,1)S(1)} %get-tuple-element.106), channel_id=1, source_target_pairs={{0,2},{1,3},{2,0},{3,1},{4,6},{5,7},{6,4},{7,5},{8,10},{9,11},{10,... | collective-permute-start | bytes 1572872 | tf_op jit(solution)/shard_map/ppermute | solution.py:280
  240.4 30.4 %collective-permute-start.47 = (bf16[8,256,128]{2,1,0:T(8,128)(2,1)S(1)}, bf16[8,256,128]{2,1,0:T(8,128)(2,1)S(1)}, u32[]{:S(2)}, u32[]{:S(2)}) collective-permute-start(bf16[8,256,128]{2,1,0:T(8,128)(2,1)S(1)} %get-tuple-element.107), channel_id=1, source_target_pairs={{0,3},{1,2},{2,1},{3,0},{4,7},{5,6},{6,5},{7,4},{8,11},{9,10},{10,... | collective-permute-start | bytes 1572872 | tf_op jit(solution)/shard_map/ppermute | solution.py:280
  243.6 24.5 %collective-permute-start.37 = (bf16[4,256,128]{2,1,0:T(8,128)(2,1)S(1)}, bf16[4,256,128]{2,1,0:T(8,128)(2,1)S(1)}, u32[]{:S(2)}, u32[]{:S(2)}) collective-permute-start(bf16[4,256,128]{2,1,0:T(8,128)(2,1)S(1)} %get-tuple-element.99), channel_id=1, source_target_pairs={{0,17},{1,16},{2,19},{3,18},{4,21},{5,20},{6,23},{7,22},{8,25},{9,... | collective-permute-start | bytes 786440 | tf_op jit(solution)/shard_map/ppermute | solution.py:287
  247.2 50.7 %collective-permute-start.33 = (bf16[8,256,128]{2,1,0:T(8,128)(2,1)S(1)}, bf16[8,256,128]{2,1,0:T(8,128)(2,1)S(1)}, u32[]{:S(2)}, u32[]{:S(2)}) collective-permute-start(bf16[8,256,128]{2,1,0:T(8,128)(2,1)S(1)} %get-tuple-element.95), channel_id=1, source_target_pairs={{0,1},{1,0},{2,3},{3,2},{4,5},{5,4},{6,7},{7,6},{8,9},{9,8},{10,11... | collective-permute-start | bytes 1572872 | tf_op jit(solution)/shard_map/ppermute | solution.py:280
  268.0 29.8 %collective-permute-start.34 = (bf16[8,256,128]{2,1,0:T(8,128)(2,1)S(1)}, bf16[8,256,128]{2,1,0:T(8,128)(2,1)S(1)}, u32[]{:S(2)}, u32[]{:S(2)}) collective-permute-start(bf16[8,256,128]{2,1,0:T(8,128)(2,1)S(1)} %get-tuple-element.96), channel_id=1, source_target_pairs={{0,2},{1,3},{2,0},{3,1},{4,6},{5,7},{6,4},{7,5},{8,10},{9,11},{10,... | collective-permute-start | bytes 1572872 | tf_op jit(solution)/shard_map/ppermute | solution.py:280
  268.0 29.8 %collective-permute-start.35 = (bf16[8,256,128]{2,1,0:T(8,128)(2,1)S(1)}, bf16[8,256,128]{2,1,0:T(8,128)(2,1)S(1)}, u32[]{:S(2)}, u32[]{:S(2)}) collective-permute-start(bf16[8,256,128]{2,1,0:T(8,128)(2,1)S(1)} %get-tuple-element.97), channel_id=1, source_target_pairs={{0,3},{1,2},{2,1},{3,0},{4,7},{5,6},{6,5},{7,4},{8,11},{9,10},{10,... | collective-permute-start | bytes 1572872 | tf_op jit(solution)/shard_map/ppermute | solution.py:280
  269.6 28.3 %collective-permute-start.38 = (bf16[4,256,128]{2,1,0:T(8,128)(2,1)S(1)}, bf16[4,256,128]{2,1,0:T(8,128)(2,1)S(1)}, u32[]{:S(2)}, u32[]{:S(2)}) collective-permute-start(bf16[4,256,128]{2,1,0:T(8,128)(2,1)S(1)} %get-tuple-element.100), channel_id=1, source_target_pairs={{0,18},{1,19},{2,16},{3,17},{4,22},{5,23},{6,20},{7,21},{8,26},{9,... | collective-permute-start | bytes 786440 | tf_op jit(solution)/shard_map/ppermute | solution.py:287
  270.9 27.0 %collective-permute-start.39 = (bf16[4,256,128]{2,1,0:T(8,128)(2,1)S(1)}, bf16[4,256,128]{2,1,0:T(8,128)(2,1)S(1)}, u32[]{:S(2)}, u32[]{:S(2)}) collective-permute-start(bf16[4,256,128]{2,1,0:T(8,128)(2,1)S(1)} %get-tuple-element.101), channel_id=1, source_target_pairs={{0,19},{1,18},{2,17},{3,16},{4,23},{5,22},{6,21},{7,20},{8,27},{9,... | collective-permute-start | bytes 786440 | tf_op jit(solution)/shard_map/ppermute | solution.py:287
  323.9 25.5 %collective-permute-start.68 = (bf16[8,256,128]{2,1,0:T(8,128)(2,1)S(1)}, bf16[8,256,128]{2,1,0:T(8,128)(2,1)S(1)}, u32[]{:S(2)}, u32[]{:S(2)}) collective-permute-start(bf16[8,256,128]{2,1,0:T(8,128)(2,1)S(1)} %collective-permute-done.67.mid_relay), channel_id=1, source_target_pairs={{4,0},{5,1},{6,2},{7,3},{8,12},{9,13},{10,14},{11,15},{20,16},{21,... | collective-permute-start | bytes 1572872 | tf_op jit(solution)/shard_map/ppermute | solution.py:273
  325.2 35.4 %collective-permute-start.54 = (bf16[8,256,128]{2,1,0:T(8,128)(2,1)S(1)}, bf16[8,256,128]{2,1,0:T(8,128)(2,1)S(1)}, u32[]{:S(2)}, u32[]{:S(2)}) collective-permute-start(bf16[8,256,128]{2,1,0:T(8,128)(2,1)S(1)} %collective-permute-done.53.mid), channel_id=1, source_target_pairs={{4,0},{5,1},{6,2},{7,3},{8,12},{9,13},{10,14},{11,15},{20,16},{21,... | collective-permute-start | bytes 1572872 | tf_op jit(solution)/shard_map/ppermute | solution.py:272
  326.5 45.3 %collective-permute-start.56 = (bf16[8,256,128]{2,1,0:T(8,128)(2,1)S(1)}, bf16[8,256,128]{2,1,0:T(8,128)(2,1)S(1)}, u32[]{:S(2)}, u32[]{:S(2)}) collective-permute-start(bf16[8,256,128]{2,1,0:T(8,128)(2,1)S(1)} %collective-permute-done.55.mid_relay), channel_id=1, source_target_pairs={{4,0},{5,1},{6,2},{7,3},{8,12},{9,13},{10,14},{11,15},{20,16},{21,... | collective-permute-start | bytes 1572872 | tf_op jit(solution)/shard_map/ppermute | solution.py:273
  355.7 20.7 %collective-permute-start.72 = (bf16[4,256,128]{2,1,0:T(8,128)(2,1)S(1)}, bf16[4,256,128]{2,1,0:T(8,128)(2,1)S(1)}, u32[]{:S(2)}, u32[]{:S(2)}) collective-permute-start(bf16[4,256,128]{2,1,0:T(8,128)(2,1)S(1)} %get-tuple-element.130), channel_id=1, source_target_pairs={{0,16},{1,17},{2,18},{3,19},{4,20},{5,21},{6,22},{7,23},{8,24},{9,... | collective-permute-start | bytes 786440 | tf_op jit(solution)/shard_map/ppermute | solution.py:287
  357.0 20.1 %collective-permute-start.73 = (bf16[4,256,128]{2,1,0:T(8,128)(2,1)S(1)}, bf16[4,256,128]{2,1,0:T(8,128)(2,1)S(1)}, u32[]{:S(2)}, u32[]{:S(2)}) collective-permute-start(bf16[4,256,128]{2,1,0:T(8,128)(2,1)S(1)} %get-tuple-element.131), channel_id=1, source_target_pairs={{0,17},{1,16},{2,19},{3,18},{4,21},{5,20},{6,23},{7,22},{8,25},{9,... | collective-permute-start | bytes 786440 | tf_op jit(solution)/shard_map/ppermute | solution.py:287
  358.3 19.5 %collective-permute-start.74 = (bf16[4,256,128]{2,1,0:T(8,128)(2,1)S(1)}, bf16[4,256,128]{2,1,0:T(8,128)(2,1)S(1)}, u32[]{:S(2)}, u32[]{:S(2)}) collective-permute-start(bf16[4,256,128]{2,1,0:T(8,128)(2,1)S(1)} %get-tuple-element.132), channel_id=1, source_target_pairs={{0,18},{1,19},{2,16},{3,17},{4,22},{5,23},{6,20},{7,21},{8,26},{9,... | collective-permute-start | bytes 786440 | tf_op jit(solution)/shard_map/ppermute | solution.py:287
  371.9 32.9 %collective-permute-start.69 = (bf16[8,256,128]{2,1,0:T(8,128)(2,1)S(1)}, bf16[8,256,128]{2,1,0:T(8,128)(2,1)S(1)}, u32[]{:S(2)}, u32[]{:S(2)}) collective-permute-start(bf16[8,256,128]{2,1,0:T(8,128)(2,1)S(1)} %get-tuple-element.127), channel_id=1, source_target_pairs={{0,1},{1,0},{2,3},{3,2},{4,5},{5,4},{6,7},{7,6},{8,9},{9,8},{10,11... | collective-permute-start | bytes 1572872 | tf_op jit(solution)/shard_map/ppermute | solution.py:280
  376.4 29.1 %collective-permute-start.70 = (bf16[8,256,128]{2,1,0:T(8,128)(2,1)S(1)}, bf16[8,256,128]{2,1,0:T(8,128)(2,1)S(1)}, u32[]{:S(2)}, u32[]{:S(2)}) collective-permute-start(bf16[8,256,128]{2,1,0:T(8,128)(2,1)S(1)} %get-tuple-element.128), channel_id=1, source_target_pairs={{0,2},{1,3},{2,0},{3,1},{4,6},{5,7},{6,4},{7,5},{8,10},{9,11},{10,... | collective-permute-start | bytes 1572872 | tf_op jit(solution)/shard_map/ppermute | solution.py:280
  377.1 29.6 %collective-permute-start.71 = (bf16[8,256,128]{2,1,0:T(8,128)(2,1)S(1)}, bf16[8,256,128]{2,1,0:T(8,128)(2,1)S(1)}, u32[]{:S(2)}, u32[]{:S(2)}) collective-permute-start(bf16[8,256,128]{2,1,0:T(8,128)(2,1)S(1)} %get-tuple-element.129), channel_id=1, source_target_pairs={{0,3},{1,2},{2,1},{3,0},{4,7},{5,6},{6,5},{7,4},{8,11},{9,10},{10,... | collective-permute-start | bytes 1572872 | tf_op jit(solution)/shard_map/ppermute | solution.py:280
  379.1 24.5 %collective-permute-start.61 = (bf16[4,256,128]{2,1,0:T(8,128)(2,1)S(1)}, bf16[4,256,128]{2,1,0:T(8,128)(2,1)S(1)}, u32[]{:S(2)}, u32[]{:S(2)}) collective-permute-start(bf16[4,256,128]{2,1,0:T(8,128)(2,1)S(1)} %get-tuple-element.121), channel_id=1, source_target_pairs={{0,17},{1,16},{2,19},{3,18},{4,21},{5,20},{6,23},{7,22},{8,25},{9,... | collective-permute-start | bytes 786440 | tf_op jit(solution)/shard_map/ppermute | solution.py:287
  382.2 51.5 %collective-permute-start.57 = (bf16[8,256,128]{2,1,0:T(8,128)(2,1)S(1)}, bf16[8,256,128]{2,1,0:T(8,128)(2,1)S(1)}, u32[]{:S(2)}, u32[]{:S(2)}) collective-permute-start(bf16[8,256,128]{2,1,0:T(8,128)(2,1)S(1)} %get-tuple-element.117), channel_id=1, source_target_pairs={{0,1},{1,0},{2,3},{3,2},{4,5},{5,4},{6,7},{7,6},{8,9},{9,8},{10,11... | collective-permute-start | bytes 1572872 | tf_op jit(solution)/shard_map/ppermute | solution.py:280
  403.6 30.1 %collective-permute-start.58 = (bf16[8,256,128]{2,1,0:T(8,128)(2,1)S(1)}, bf16[8,256,128]{2,1,0:T(8,128)(2,1)S(1)}, u32[]{:S(2)}, u32[]{:S(2)}) collective-permute-start(bf16[8,256,128]{2,1,0:T(8,128)(2,1)S(1)} %get-tuple-element.118), channel_id=1, source_target_pairs={{0,2},{1,3},{2,0},{3,1},{4,6},{5,7},{6,4},{7,5},{8,10},{9,11},{10,... | collective-permute-start | bytes 1572872 | tf_op jit(solution)/shard_map/ppermute | solution.py:280
  404.8 28.9 %collective-permute-start.59 = (bf16[8,256,128]{2,1,0:T(8,128)(2,1)S(1)}, bf16[8,256,128]{2,1,0:T(8,128)(2,1)S(1)}, u32[]{:S(2)}, u32[]{:S(2)}) collective-permute-start(bf16[8,256,128]{2,1,0:T(8,128)(2,1)S(1)} %get-tuple-element.119), channel_id=1, source_target_pairs={{0,3},{1,2},{2,1},{3,0},{4,7},{5,6},{6,5},{7,4},{8,11},{9,10},{10,... | collective-permute-start | bytes 1572872 | tf_op jit(solution)/shard_map/ppermute | solution.py:280
  405.4 28.3 %collective-permute-start.62 = (bf16[4,256,128]{2,1,0:T(8,128)(2,1)S(1)}, bf16[4,256,128]{2,1,0:T(8,128)(2,1)S(1)}, u32[]{:S(2)}, u32[]{:S(2)}) collective-permute-start(bf16[4,256,128]{2,1,0:T(8,128)(2,1)S(1)} %get-tuple-element.122), channel_id=1, source_target_pairs={{0,18},{1,19},{2,16},{3,17},{4,22},{5,23},{6,20},{7,21},{8,26},{9,... | collective-permute-start | bytes 786440 | tf_op jit(solution)/shard_map/ppermute | solution.py:287
  406.7 27.0 %collective-permute-start.63 = (bf16[4,256,128]{2,1,0:T(8,128)(2,1)S(1)}, bf16[4,256,128]{2,1,0:T(8,128)(2,1)S(1)}, u32[]{:S(2)}, u32[]{:S(2)}) collective-permute-start(bf16[4,256,128]{2,1,0:T(8,128)(2,1)S(1)} %get-tuple-element.123), channel_id=1, source_target_pairs={{0,19},{1,18},{2,17},{3,16},{4,23},{5,22},{6,21},{7,20},{8,27},{9,... | collective-permute-start | bytes 786440 | tf_op jit(solution)/shard_map/ppermute | solution.py:287
  (47 other events, 807.7 us)

commit v2 on v1

v2 whole, which is shorter than its diff:
```python
import functools

import jax
import jax.numpy as jnp
from jax import lax
from jax.experimental import pallas as pl
from jax.experimental.pallas import tpu as pltpu
from jax.sharding import PartitionSpec as P

CAP = 2
CAPX = 1
COLS = 4
GROUPS = (((0, 1), ()), ((2, 3), (0, 1, 2, 3)))
HALVES = 2
ANY = pl.BlockSpec(memory_space=pl.ANY)


def params(mib):
    return pltpu.CompilerParams(vmem_limit_bytes=mib * 1024 * 1024)


def first_level(chol, noise, out, half, after=()):
    depth, blocks, rows, _ = chol.shape
    width = noise.shape[3] // HALVES

    def body(*refs):
        lower, draws, latest, full = refs[0], refs[1], refs[-2], refs[-1]
        value = jnp.dot(lower[0, 0], draws[0, 0], preferred_element_type=jnp.float32)
        value = value.astype(jnp.bfloat16)
        latest[0] = value
        full[0, 0] = value

    carried = [] if out is None else [out, *after]
    return pl.pallas_call(
        body,
        grid=(blocks,),
        in_specs=[
            pl.BlockSpec((1, 1, rows, rows), lambda b: (0, b, 0, 0)),
            pl.BlockSpec((1, 1, rows, width), lambda b: (0, b, 0, half)),
        ]
        + [ANY] * len(carried),
        out_specs=[
            pl.BlockSpec((1, rows, width), lambda b: (b, 0, 0)),
            pl.BlockSpec((1, 1, rows, width), lambda b: (0, b, 0, half)),
        ],
        out_shape=[
            jax.ShapeDtypeStruct((blocks, rows, width), jnp.bfloat16),
            jax.ShapeDtypeStruct(noise.shape, jnp.bfloat16),
        ],
        input_output_aliases={2: 1} if carried else {},
        compiler_params=params(8),
        cost_estimate=pl.CostEstimate(
            flops=2 * blocks * rows * rows * width, bytes_accessed=4_000_000, transcendentals=0
        ),
        name=f"first_{half}",
    )(chol, noise, *carried)


def pick(table, held, group, name, after=()):
    blocks, rows, width = held[0][0].shape
    ks = sorted(set(group[0] + group[1]))
    same_slots, prior_slots = len(group[0]) * CAP, len(group[1]) * CAPX
    n_same, n_prior = COLS * bool(group[0]), COLS * bool(group[1])
    total = COLS * (same_slots + prior_slots)
    flat = [level[k] for level in held for k in ks]
    count, each, levels = len(flat), len(ks), len(held)

    def body(tbl, *refs):
        held = refs[:count]
        targets = refs[count + len(after) : -1]
        same, prior = targets[:n_same], targets[n_same:]
        sems = refs[-1]

        def slot_copy(slot, source):
            if slot < COLS * same_slots:
                target = same[slot // same_slots].at[slot % same_slots]
            else:
                left = slot - COLS * same_slots
                target = prior[left // prior_slots].at[left % prior_slots]
            return pltpu.make_async_copy(source, target, sems.at[slot])

        for slot in range(total):
            where = tbl[slot]
            if slot < COLS * same_slots:
                k = group[0][slot % same_slots // CAP]
            else:
                k = group[1][(slot - COLS * same_slots) % prior_slots // CAPX]
            at = ks.index(k)
            for level in range(levels):

                @pl.when((where >= level * blocks) & (where < (level + 1) * blocks))
                def _():
                    slot_copy(slot, held[level * each + at].at[where - level * blocks]).start()

        for slot in range(total):

            @pl.when(tbl[slot] >= 0)
            def _():
                slot_copy(slot, held[0].at[0]).wait()

    out = pl.pallas_call(
        body,
        in_specs=[pl.BlockSpec(memory_space=pltpu.SMEM)] + [ANY] * (count + len(after)),
        out_specs=[ANY] * (n_same + n_prior),
        out_shape=[jax.ShapeDtypeStruct((same_slots, rows, width), jnp.bfloat16)] * n_same
        + [jax.ShapeDtypeStruct((prior_slots, rows, width), jnp.bfloat16)] * n_prior,
        scratch_shapes=[pltpu.SemaphoreType.DMA((total,))],
        compiler_params=params(4),
        cost_estimate=pl.CostEstimate(flops=0, bytes_accessed=6_000_000, transcendentals=0),
        name=name,
    )(table, *flat, *after)
    return out[:n_same], out[n_same:]


def next_level(places, factors, chol, noise, got, out, section, half, after=()):
    depth, blocks, rows, _ = chol.shape
    slots = factors.shape[2]
    width = noise.shape[3] // HALVES
    sizes = [ref.shape[0] for ref in got]
    starts = [sum(sizes[:i]) for i in range(len(sizes))]

    def body(tbl, mats, lower, draws, *rest):
        got = rest[: len(sizes)]
        latest, full, held, sems = rest[len(sizes) + 1 + len(after) :]
        block = pl.program_id(0)

        def fetch(i):
            return pltpu.make_async_copy(
                got[i], held.at[pl.ds(starts[i], sizes[i])], sems.at[i]
            )

        @pl.when(block == 0)
        def _():
            for i in range(len(sizes)):
                fetch(i).start()

        total = jnp.dot(lower[0, 0], draws[0, 0], preferred_element_type=jnp.float32)

        @pl.when(block == 0)
        def _():
            for i in range(len(sizes)):
                fetch(i).wait()

        for j in range(slots):
            place = tbl[block * slots + j]
            parent = held[jnp.maximum(place, 0)]
            parent = jnp.where(place >= 0, parent, jnp.zeros_like(parent))
            total += jnp.dot(mats[0, 0, j], parent, preferred_element_type=jnp.float32)
        value = total.astype(jnp.bfloat16)
        latest[0] = value
        full[0, 0] = value

    n_got = len(sizes)
    return pl.pallas_call(
        body,
        grid=(blocks,),
        in_specs=[
            pl.BlockSpec(memory_space=pltpu.SMEM),
            pl.BlockSpec((1, 1, slots, rows, rows), lambda b: (section - 1, b, 0, 0, 0)),
            pl.BlockSpec((1, 1, rows, rows), lambda b: (section, b, 0, 0)),
            pl.BlockSpec((1, 1, rows, width), lambda b: (section, b, 0, half)),
        ]
        + [ANY] * (n_got + 1 + len(after)),
        out_specs=[
            pl.BlockSpec((1, rows, width), lambda b: (b, 0, 0)),
            pl.BlockSpec((1, 1, rows, width), lambda b: (section, b, 0, half)),
        ],
        out_shape=[
            jax.ShapeDtypeStruct((blocks, rows, width), jnp.bfloat16),
            jax.ShapeDtypeStruct(noise.shape, jnp.bfloat16),
        ],
        scratch_shapes=[
            pltpu.VMEM((sum(sizes), rows, width), jnp.bfloat16),
            pltpu.SemaphoreType.DMA((n_got,)),
        ],
        input_output_aliases={4 + n_got: 1},
        compiler_params=params(12),
        cost_estimate=pl.CostEstimate(
            flops=2 * (slots + 1) * blocks * rows * rows * width,
            bytes_accessed=10_000_000,
            transcendentals=0,
        ),
        name=f"level_{section}_{half}",
    )(places, factors, chol, noise, *got, out, *after)


def ranks(active, lane):
    count = lane.shape[-1]
    earlier = jnp.arange(count)[:, None] > jnp.arange(count)[None, :]
    alike = (lane[..., :, None] == lane[..., None, :]) & active[..., None, :] & earlier
    return jnp.sum(alike.astype(jnp.int32), axis=-1)


def tables(parents, total_blocks, local_blocks, peer_count, tile_count):
    sections = parents.shape[0]
    own_lane, own_tile = lax.axis_index("lvl"), lax.axis_index("tile")
    own_z, own_col = own_lane // COLS, own_lane % COLS
    mine = parents.reshape(sections, -1)
    onward = lax.ppermute(
        mine,
        "tile",
        [(t + 1, t) for t in range(tile_count - 1)],
    )
    onward = jnp.where(own_tile + 1 < tile_count, onward, -1)
    pair = jnp.stack([mine, onward])
    lists = jnp.stack([pair] + [lax.ppermute(pair, "lvl", across(k, peer_count)) for k in (1, 2, 3)])

    def decode(ids):
        clipped = jnp.maximum(ids, 0)
        level, block = clipped // total_blocks, clipped % total_blocks
        dev = block // local_blocks
        return ids >= 0, level, dev // peer_count, dev % peer_count, block % local_blocks

    valid, level, tile, lane, within = decode(lists)
    active = valid & (tile == own_tile) & (lane % COLS == own_col)
    rank = jnp.minimum(ranks(active, lane), CAP - 1)
    slot = ((own_z - lane // COLS) % 4) * CAP + rank
    hits = active[..., None] & (slot[..., None] == jnp.arange(4 * CAP))
    source = level * local_blocks + within
    table = jnp.sum(jnp.where(hits, source[..., None] + 1, 0), axis=-2) - 1
    table = table.reshape(COLS, 2, sections, 4, CAP).transpose(1, 2, 0, 3, 4)
    sends = []
    for same_ks, prior_ks in GROUPS:
        same = [table[0, :, c, k] for c in range(COLS) for k in same_ks]
        prior = [table[1, :, c, k, :1] for c in range(COLS) for k in prior_ks]
        sends.append(jnp.concatenate(same + prior, axis=1))

    valid, level, tile, lane, within = decode(mine)
    from_prior = (tile != own_tile).astype(jnp.int32)
    rank = jnp.minimum(ranks(valid, lane + peer_count * from_prior), CAP - 1)
    apart = (lane % COLS) ^ own_col
    ring = (own_z - lane // COLS) % 4
    place, base = jnp.zeros_like(lane), 0
    for same_ks, prior_ks in GROUPS:
        for at, k in enumerate(same_ks):
            slot = base + (apart * len(same_ks) + at) * CAP + rank
            place = jnp.where((ring == k) & (from_prior == 0), slot, place)
        base += COLS * len(same_ks) * CAP
        for at, k in enumerate(prior_ks):
            slot = base + (apart * len(prior_ks) + at) * CAPX
            place = jnp.where((ring == k) & (from_prior == 1), slot, place)
        base += COLS * len(prior_ks) * CAPX
    return sends, jnp.where(valid, place, -1)


def across(k, peer_count):
    return [(lane, lane ^ k) for lane in range(peer_count)]


def ring_z(latest, peer_count):
    links = [(lane, (lane + COLS) % peer_count) for lane in range(peer_count)]
    held = [latest]
    for _ in range(3):
        held.append(lax.ppermute(held[-1], "lvl", links))
    return held


def swap_plane(same, prior, peer_count, tile_count):
    got = list(same[:1])
    for k in range(1, len(same)):
        got.append(lax.ppermute(same[k], "lvl", across(k, peer_count)))
    for k in range(len(prior)):
        links = [
            (t * peer_count + a, (t + 1) * peer_count + b)
            for t in range(tile_count - 1)
            for a, b in across(k, peer_count)
        ]
        got.append(lax.ppermute(prior[k], ("tile", "lvl"), links))
    return got


def shards(parents, factors, chol, noise):
    peer_count = lax.axis_size("lvl")
    tile_count = lax.axis_size("tile")
    depth, local_blocks = chol.shape[:2]
    total_blocks = local_blocks * peer_count * tile_count
    sends, places = tables(parents, total_blocks, local_blocks, peer_count, tile_count)
    held = [[], []]

    def spread(latest, half):
        held[half].append(ring_z(latest, peer_count))
        return held[half][-1]

    def swap(section, half, after=()):
        got = []
        for group, ks in enumerate(GROUPS):
            same, prior = pick(
                sends[group][section], held[half], ks, f"pick_{section}_{half}_{group}", after
            )
            got += swap_plane(same, prior, peer_count, tile_count)
        return got

    lead, out = first_level(chol, noise, None, 0)
    ring = spread(lead, 0)
    lag, out = first_level(chol, noise, out, 1, [ring[1]])
    got = swap(0, 0, [lag])
    ring = spread(lag, 1)
    for section in range(1, depth):
        more = section + 1 < depth
        lead, out = next_level(
            places[section - 1], factors, chol, noise, got, out, section, 0, [ring[2]]
        )
        lag_got = swap(section - 1, 1, [lead])
        ring = spread(lead, 0) if more else None
        lag, out = next_level(
            places[section - 1], factors, chol, noise, lag_got, out, section, 1, [ring[2]] if more else ()
        )
        if more:
            got = swap(section, 0, [lag])
            ring = spread(lag, 1)
    return out


def solution(mesh):
    placed = (
        P(None, ("tile", "lvl"), None),
        P(None, ("tile", "lvl"), None, None, None),
        P(None, ("tile", "lvl"), None, None),
        P(None, ("tile", "lvl"), None, None),
    )
    return jax.shard_map(
        shards,
        mesh=mesh,
        in_specs=placed,
        out_specs=P(None, ("tile", "lvl"), None, None),
        check_vma=False,
    )
```

time: 441 us -> 338 us (0.77)
  waiting for transfers between devices: 262 us -> 161 us
  starting transfers between devices: 85.9 us -> 77.5 us
    ppermute x30 -> x18, waiting for transfers between devices: 144 us -> 55.7 us  [ring_z(): held.append(lax.ppermute(held[-1], 'lvl', links))]
    ppermute x24, waiting for transfers between devices: 109 us -> 43.7 us  [swap_plane(): got.append(lax.ppermute(prior[k], ('tile', 'lvl'), links))]
    ppermute x18 -> x36, waiting for transfers between devices: 8.67 us -> 58.7 us  [swap_plane(): got.append(lax.ppermute(same[k], 'lvl', across(k, peer_count)))]
    ppermute x30 -> x18, starting transfers between devices: 33 us -> 12.5 us  [ring_z(): held.append(lax.ppermute(held[-1], 'lvl', links))]
    ppermute x18 -> x36, starting transfers between devices: 17.4 us -> 29.5 us  [swap_plane(): got.append(lax.ppermute(same[k], 'lvl', across(k, peer_count)))]
    pallas_call x6 -> x12, Pallas kernels: 23.1 us -> 23.4 us  [pick(): pl.pallas_call(body, in_specs=[pl.BlockSpec(memory_space=pltpu.SMEM)] + [...]
  transfers between devices with their start and end apart: 76 -> 82, of which waited for: 28 -> 43; matrix products, arithmetic and copies ran while one was open for 1% -> 4% of each run, Pallas kernels for 13% -> 16%
where the time goes in v2:
time: 338 us; the launch traced here: 336 us
  waiting for transfers between devices  161 us (48%)
  starting transfers between devices  77.5 us (23%)
  Pallas kernels  63.5 us (19%)
  local copies, waits for them, and re-layouts  30.1 us (9%)
    ppermute x36, waiting for transfers between devices, swap_plane(): got.append(lax.ppermute(same[k], 'lvl', across(k, peer_count)))  58.7 us
    ppermute x18, waiting for transfers between devices, ring_z(): held.append(lax.ppermute(held[-1], 'lvl', links))  55.7 us
    ppermute x24, waiting for transfers between devices, swap_plane(): got.append(lax.ppermute(prior[k], ('tile', 'lvl'), links))  43.7 us
    pallas_call x6, Pallas kernels, next_level(): pl.pallas_call(body, grid=(blocks,), in_specs=[pl.BlockSpec(memory_space=...  33.1 us
    ppermute x24, starting transfers between devices, swap_plane(): got.append(lax.ppermute(prior[k], ('tile', 'lvl'), links))  30.8 us
    ppermute x36, starting transfers between devices, swap_plane(): got.append(lax.ppermute(same[k], 'lvl', across(k, peer_count)))  29.5 us
    unnamed x39, local copies, waits for them, and re-layouts  25.8 us
    pallas_call x12, Pallas kernels, pick(): pl.pallas_call(body, in_specs=[pl.BlockSpec(memory_space=pltpu.SMEM)] + [...  23.4 us
  transfers between devices with their start and end apart: 82, of which 43 were waited for; matrix products, arithmetic and copies ran while one was open for 4% of the time, Pallas kernels for 16%

profile of v2, /device:TPU:1, one launch (start us, length us, event | category | flops | bytes accessed | tf_op | source)
XLA Modules:
  0.0 335.6 jit_solution(7411064825327156098)
XLA Ops:
  5.0 2.2 copy-done.6
  7.2 3.5 %first_0.1 = (bf16[8,256,128]{2,1,0:T(8,128)(2,1)S(1)}, bf16[4,8,256,256]{3,2,1,0:T(8,128)(2,1)}) custom-call(bf16[4,8,256,256]{3,2,1,0:T(8,128)(2,1)S(1)} %copy-done.2, bf16[4,8,256,256]{3,2,1,0:T(8,128)(2,1)S(1)} %copy-done.6), custom_call_target="tpu_custom_call" | custom-call | flops 134217728 | bytes 4000000 | tf_op jit(solution)/shard_map/first_0/pallas_call | solution.py:34
  10.7 2.7 collective-permute-start.4
  14.2 2.2 collective-permute-start.3
  20.2 7.0 %collective-permute-done.4.refs_3_.refs_1_ = bf16[8,256,128]{2,1,0:T(8,128)(2,1)S(1)} collective-permute-done((bf16[8,256,128]{2,1,0:T(8,128)(2,1)S(1)}, bf16[8,256,128]{2,1,0:T(8,128)(2,1)S(1)}, u32[]{:S(2)}, u32[]{:S(2)}) %collective-permute-start.4) | collective-permute-done | bytes 524320 | tf_op jit(solution)/shard_map/ppermute | solution.py:254
  27.8 2.2 copy-done.3
  32.2 3.5 %first_1.1 = (bf16[8,256,128]{2,1,0:T(8,128)(2,1)S(1)}, bf16[4,8,256,256]{3,2,1,0:T(8,128)(2,1)}) custom-call(bf16[4,8,256,256]{3,2,1,0:T(8,128)(2,1)S(1)} %copy-done.3, bf16[4,8,256,256]{3,2,1,0:T(8,128)(2,1)S(1)} %copy-done.7, bf16[4,8,256,256]{3,2,1,0:T(8,128)(2,1)} %get-tuple-element.92.refs_2_, ...), custom_call_target="tpu_custom_call", output_to_operand_aliasing={{1}: (2, {})} | custom-call | flops 134217728 | bytes 4000000 | tf_op jit(solution)/shard_map/first_1/pallas_call | solution.py:34
  38.6 3.6 %collective-permute-done.9.refs_2_ = bf16[8,256,128]{2,1,0:T(8,128)(2,1)S(1)} collective-permute-done((bf16[8,256,128]{2,1,0:T(8,128)(2,1)S(1)}, bf16[8,256,128]{2,1,0:T(8,128)(2,1)S(1)}, u32[]{:S(2)}, u32[]{:S(2)}) %collective-permute-start.9) | collective-permute-done | bytes 524320 | tf_op jit(solution)/shard_map/ppermute | solution.py:254
  56.4 8.3 %collective-permute-done.10.refs_3_ = bf16[8,256,128]{2,1,0:T(8,128)(2,1)S(1)} collective-permute-done((bf16[8,256,128]{2,1,0:T(8,128)(2,1)S(1)}, bf16[8,256,128]{2,1,0:T(8,128)(2,1)S(1)}, u32[]{:S(2)}, u32[]{:S(2)}) %collective-permute-start.10) | collective-permute-done | bytes 524320 | tf_op jit(solution)/shard_map/ppermute | solution.py:254
  64.6 2.3 pick_0_0_1.1
  71.3 4.6 %collective-permute-done.18.rest_13_.refs_2_ = bf16[8,256,128]{2,1,0:T(8,128)(2,1)S(1)} collective-permute-done((bf16[8,256,128]{2,1,0:T(8,128)(2,1)S(1)}, bf16[8,256,128]{2,1,0:T(8,128)(2,1)S(1)}, u32[]{:S(2)}, u32[]{:S(2)}) %collective-permute-start.18) | collective-permute-done | bytes 524320 | tf_op jit(solution)/shard_map/ppermute | solution.py:254
  80.6 3.1 collective-permute-done.15.rest_9_
  83.7 2.4 collective-permute-done.16.rest_10_
  86.1 2.8 collective-permute-done.17.rest_11_
  88.9 4.6 %copy-done = bf16[3,8,4,256,256]{4,3,2,1,0:T(8,128)(2,1)S(1)} copy-done((bf16[3,8,4,256,256]{4,3,2,1,0:T(8,128)(2,1)S(1)}, bf16[3,8,4,256,256]{4,3,2,1,0:T(8,128)(2,1)}, u32[]{:S(2)}) %copy-start) | copy-done | bytes 12582936
  97.9 6.3 %level_1_0.1 = (bf16[8,256,128]{2,1,0:T(8,128)(2,1)S(1)}, bf16[4,8,256,256]{3,2,1,0:T(8,128)(2,1)}) custom-call(s32[32]{0:T(128)S(1)} %get-tuple-element.225.tbl, bf16[3,8,4,256,256]{4,3,2,1,0:T(8,128)(2,1)S(1)} %copy-done, bf16[4,8,256,256]{3,2,1,0:T(8,128)(2,1)S(1)} %copy-done.4, ...), custom_call_target="tpu_custom_call", output_to_operand_aliasing={{1}: (16, {})} | custom-call | flops 671088640 | bytes 10000000 | tf_op jit(solution)/shard_map/level_1_0/pallas_call | solution.py:154
  108.6 2.3 pick_0_1_1.1
  111.9 2.4 collective-permute-done.19.rest_1_
  114.5 4.5 %collective-permute-done.30.refs_3_.refs_5_ = bf16[8,256,128]{2,1,0:T(8,128)(2,1)S(1)} collective-permute-done((bf16[8,256,128]{2,1,0:T(8,128)(2,1)S(1)}, bf16[8,256,128]{2,1,0:T(8,128)(2,1)S(1)}, u32[]{:S(2)}, u32[]{:S(2)}) %collective-permute-start.30) | collective-permute-done | bytes 524320 | tf_op jit(solution)/shard_map/ppermute | solution.py:254
  122.0 3.6 %collective-permute-done.23.rest_5_ = bf16[4,256,128]{2,1,0:T(8,128)(2,1)S(1)} collective-permute-done((bf16[4,256,128]{2,1,0:T(8,128)(2,1)S(1)}, bf16[4,256,128]{2,1,0:T(8,128)(2,1)S(1)}, u32[]{:S(2)}, u32[]{:S(2)}) %collective-permute-start.23) | collective-permute-done | bytes 262176 | tf_op jit(solution)/shard_map/ppermute | solution.py:261
  126.8 4.8 %collective-permute-done.24.rest_6_ = bf16[4,256,128]{2,1,0:T(8,128)(2,1)S(1)} collective-permute-done((bf16[4,256,128]{2,1,0:T(8,128)(2,1)S(1)}, bf16[4,256,128]{2,1,0:T(8,128)(2,1)S(1)}, u32[]{:S(2)}, u32[]{:S(2)}) %collective-permute-start.24) | collective-permute-done | bytes 262176 | tf_op jit(solution)/shard_map/ppermute | solution.py:261
  134.3 2.8 collective-permute-start.36
  137.1 5.3 %collective-permute-done.28.rest_10_ = bf16[4,256,128]{2,1,0:T(8,128)(2,1)S(1)} collective-permute-done((bf16[4,256,128]{2,1,0:T(8,128)(2,1)S(1)}, bf16[4,256,128]{2,1,0:T(8,128)(2,1)S(1)}, u32[]{:S(2)}, u32[]{:S(2)}) %collective-permute-start.28) | collective-permute-done | bytes 262176 | tf_op jit(solution)/shard_map/ppermute | solution.py:268
  142.4 5.4 %level_1_1.1 = (bf16[8,256,128]{2,1,0:T(8,128)(2,1)S(1)}, bf16[4,8,256,256]{3,2,1,0:T(8,128)(2,1)}) custom-call(s32[32]{0:T(128)S(1)} %get-tuple-element.225.tbl, bf16[3,8,4,256,256]{4,3,2,1,0:T(8,128)(2,1)S(1)} %copy-done.1, bf16[4,8,256,256]{3,2,1,0:T(8,128)(2,1)S(1)} %copy-done.4, ...), custom_call_target="tpu_custom_call", output_to_operand_aliasing={{1}: (16, {})} | custom-call | flops 671088640 | bytes 10000000 | tf_op jit(solution)/shard_map/level_1_1/pallas_call | solution.py:154
  147.7 2.9 collective-permute-start.32
  157.3 3.5 %collective-permute-done.33.rest_1_ = bf16[4,256,128]{2,1,0:T(8,128)(2,1)S(1)} collective-permute-done((bf16[4,256,128]{2,1,0:T(8,128)(2,1)S(1)}, bf16[4,256,128]{2,1,0:T(8,128)(2,1)S(1)}, u32[]{:S(2)}, u32[]{:S(2)}) %collective-permute-start.33) | collective-permute-done | bytes 262176 | tf_op jit(solution)/shard_map/ppermute | solution.py:261
  162.4 3.9 %collective-permute-done.34.rest_2_ = bf16[4,256,128]{2,1,0:T(8,128)(2,1)S(1)} collective-permute-done((bf16[4,256,128]{2,1,0:T(8,128)(2,1)S(1)}, bf16[4,256,128]{2,1,0:T(8,128)(2,1)S(1)}, u32[]{:S(2)}, u32[]{:S(2)}) %collective-permute-start.34) | collective-permute-done | bytes 262176 | tf_op jit(solution)/shard_map/ppermute | solution.py:261
  167.6 3.9 %collective-permute-done.37.rest_5_ = bf16[4,256,128]{2,1,0:T(8,128)(2,1)S(1)} collective-permute-done((bf16[4,256,128]{2,1,0:T(8,128)(2,1)S(1)}, bf16[4,256,128]{2,1,0:T(8,128)(2,1)S(1)}, u32[]{:S(2)}, u32[]{:S(2)}) %collective-permute-start.37) | collective-permute-done | bytes 262176 | tf_op jit(solution)/shard_map/ppermute | solution.py:261
  172.8 4.8 %collective-permute-done.38.rest_6_ = bf16[4,256,128]{2,1,0:T(8,128)(2,1)S(1)} collective-permute-done((bf16[4,256,128]{2,1,0:T(8,128)(2,1)S(1)}, bf16[4,256,128]{2,1,0:T(8,128)(2,1)S(1)}, u32[]{:S(2)}, u32[]{:S(2)}) %collective-permute-start.38) | collective-permute-done | bytes 262176 | tf_op jit(solution)/shard_map/ppermute | solution.py:261
  180.3 8.1 %collective-permute-done.42.rest_10_ = bf16[4,256,128]{2,1,0:T(8,128)(2,1)S(1)} collective-permute-done((bf16[4,256,128]{2,1,0:T(8,128)(2,1)S(1)}, bf16[4,256,128]{2,1,0:T(8,128)(2,1)S(1)}, u32[]{:S(2)}, u32[]{:S(2)}) %collective-permute-start.42) | collective-permute-done | bytes 262176 | tf_op jit(solution)/shard_map/ppermute | solution.py:268
  188.4 5.3 %level_2_0.1 = (bf16[8,256,128]{2,1,0:T(8,128)(2,1)S(1)}, bf16[4,8,256,256]{3,2,1,0:T(8,128)(2,1)}) custom-call(s32[32]{0:T(128)S(1)} %get-tuple-element.224.tbl, bf16[3,8,4,256,256]{4,3,2,1,0:T(8,128)(2,1)S(1)} %copy-done.1, bf16[4,8,256,256]{3,2,1,0:T(8,128)(2,1)S(1)} %copy-done.4, ...), custom_call_target="tpu_custom_call", output_to_operand_aliasing={{1}: (16, {})} | custom-call | flops 671088640 | bytes 10000000 | tf_op jit(solution)/shard_map/level_2_0/pallas_call | solution.py:154
  198.3 2.3 pick_1_1_1.1
  201.1 2.9 collective-permute-done.45.rest_1_
  204.0 6.0 %collective-permute-done.46.rest_2_ = bf16[4,256,128]{2,1,0:T(8,128)(2,1)S(1)} collective-permute-done((bf16[4,256,128]{2,1,0:T(8,128)(2,1)S(1)}, bf16[4,256,128]{2,1,0:T(8,128)(2,1)S(1)}, u32[]{:S(2)}, u32[]{:S(2)}) %collective-permute-start.46) | collective-permute-done | bytes 262176 | tf_op jit(solution)/shard_map/ppermute | solution.py:261
  216.1 5.0 %collective-permute-done.50.rest_6_ = bf16[4,256,128]{2,1,0:T(8,128)(2,1)S(1)} collective-permute-done((bf16[4,256,128]{2,1,0:T(8,128)(2,1)S(1)}, bf16[4,256,128]{2,1,0:T(8,128)(2,1)S(1)}, u32[]{:S(2)}, u32[]{:S(2)}) %collective-permute-start.50) | collective-permute-done | bytes 262176 | tf_op jit(solution)/shard_map/ppermute | solution.py:261
  223.8 7.9 %collective-permute-done.54.rest_10_ = bf16[4,256,128]{2,1,0:T(8,128)(2,1)S(1)} collective-permute-done((bf16[4,256,128]{2,1,0:T(8,128)(2,1)S(1)}, bf16[4,256,128]{2,1,0:T(8,128)(2,1)S(1)}, u32[]{:S(2)}, u32[]{:S(2)}) %collective-permute-start.54) | collective-permute-done | bytes 262176 | tf_op jit(solution)/shard_map/ppermute | solution.py:268
  231.7 5.4 %level_2_1.1 = (bf16[8,256,128]{2,1,0:T(8,128)(2,1)S(1)}, bf16[4,8,256,256]{3,2,1,0:T(8,128)(2,1)}) custom-call(s32[32]{0:T(128)S(1)} %get-tuple-element.224.tbl, bf16[3,8,4,256,256]{4,3,2,1,0:T(8,128)(2,1)S(1)} %copy-done.1, bf16[4,8,256,256]{3,2,1,0:T(8,128)(2,1)S(1)} %copy-done.4, ...), custom_call_target="tpu_custom_call", output_to_operand_aliasing={{1}: (16, {})} | custom-call | flops 671088640 | bytes 10000000 | tf_op jit(solution)/shard_map/level_2_1/pallas_call | solution.py:154
  237.7 15.1 %collective-permute-done.58.refs_5_.refs_9_ = bf16[8,256,128]{2,1,0:T(8,128)(2,1)S(1)} collective-permute-done((bf16[8,256,128]{2,1,0:T(8,128)(2,1)S(1)}, bf16[8,256,128]{2,1,0:T(8,128)(2,1)S(1)}, u32[]{:S(2)}, u32[]{:S(2)}) %collective-permute-start.58) | collective-permute-done | bytes 524320 | tf_op jit(solution)/shard_map/ppermute | solution.py:254
  257.4 6.7 %collective-permute-done.62.refs_11_ = bf16[8,256,128]{2,1,0:T(8,128)(2,1)S(1)} collective-permute-done((bf16[8,256,128]{2,1,0:T(8,128)(2,1)S(1)}, bf16[8,256,128]{2,1,0:T(8,128)(2,1)S(1)}, u32[]{:S(2)}, u32[]{:S(2)}) %collective-permute-start.62) | collective-permute-done | bytes 524320 | tf_op jit(solution)/shard_map/ppermute | solution.py:254
  268.1 2.5 collective-permute-start.65
  270.6 4.4 %collective-permute-done.70.rest_13_.refs_10_ = bf16[8,256,128]{2,1,0:T(8,128)(2,1)S(1)} collective-permute-done((bf16[8,256,128]{2,1,0:T(8,128)(2,1)S(1)}, bf16[8,256,128]{2,1,0:T(8,128)(2,1)S(1)}, u32[]{:S(2)}, u32[]{:S(2)}) %collective-permute-start.70) | collective-permute-done | bytes 524320 | tf_op jit(solution)/shard_map/ppermute | solution.py:254
  284.3 6.4 %collective-permute-done.68.rest_10_ = bf16[4,256,128]{2,1,0:T(8,128)(2,1)S(1)} collective-permute-done((bf16[4,256,128]{2,1,0:T(8,128)(2,1)S(1)}, bf16[4,256,128]{2,1,0:T(8,128)(2,1)S(1)}, u32[]{:S(2)}, u32[]{:S(2)}) %collective-permute-start.68) | collective-permute-done | bytes 262176 | tf_op jit(solution)/shard_map/ppermute | solution.py:268
  290.7 5.4 %level_3_0.1 = (bf16[8,256,128]{2,1,0:T(8,128)(2,1)S(1)}, bf16[4,8,256,256]{3,2,1,0:T(8,128)(2,1)}) custom-call(s32[32]{0:T(128)S(1)} %get-tuple-element.226.tbl, bf16[3,8,4,256,256]{4,3,2,1,0:T(8,128)(2,1)S(1)} %copy-done.1, bf16[4,8,256,256]{3,2,1,0:T(8,128)(2,1)S(1)} %copy-done.5, ...), custom_call_target="tpu_custom_call", output_to_operand_aliasing={{1}: (16, {})} | custom-call | flops 671088640 | bytes 10000000 | tf_op jit(solution)/shard_map/level_3_0/pallas_call | solution.py:154
  309.2 4.0 %collective-permute-done.73.rest_3_ = bf16[4,256,128]{2,1,0:T(8,128)(2,1)S(1)} collective-permute-done((bf16[4,256,128]{2,1,0:T(8,128)(2,1)S(1)}, bf16[4,256,128]{2,1,0:T(8,128)(2,1)S(1)}, u32[]{:S(2)}, u32[]{:S(2)}) %collective-permute-start.73) | collective-permute-done | bytes 262176 | tf_op jit(solution)/shard_map/ppermute | solution.py:261
  314.5 2.7 collective-permute-done.75.rest_5_
  320.4 4.0 %collective-permute-done.77.rest_7_ = bf16[4,256,128]{2,1,0:T(8,128)(2,1)S(1)} collective-permute-done((bf16[4,256,128]{2,1,0:T(8,128)(2,1)S(1)}, bf16[4,256,128]{2,1,0:T(8,128)(2,1)S(1)}, u32[]{:S(2)}, u32[]{:S(2)}) %collective-permute-start.77) | collective-permute-done | bytes 262176 | tf_op jit(solution)/shard_map/ppermute | solution.py:261
  326.1 4.0 %collective-permute-done.81.rest_11_ = bf16[4,256,128]{2,1,0:T(8,128)(2,1)S(1)} collective-permute-done((bf16[4,256,128]{2,1,0:T(8,128)(2,1)S(1)}, bf16[4,256,128]{2,1,0:T(8,128)(2,1)S(1)}, u32[]{:S(2)}, u32[]{:S(2)}) %collective-permute-start.81) | collective-permute-done | bytes 262176 | tf_op jit(solution)/shard_map/ppermute | solution.py:268
  330.1 5.4 %level_3_1.1 = (bf16[8,256,128]{2,1,0:T(8,128)(2,1)}, bf16[4,8,256,256]{3,2,1,0:T(8,128)(2,1)}) custom-call(s32[32]{0:T(128)S(1)} %get-tuple-element.226.tbl, bf16[3,8,4,256,256]{4,3,2,1,0:T(8,128)(2,1)S(1)} %copy-done.1, bf16[4,8,256,256]{3,2,1,0:T(8,128)(2,1)S(1)} %copy-done.5, ...), custom_call_target="tpu_custom_call", output_to_operand_aliasing={{1}: (16, {})} | custom-call | flops 671088640 | bytes 10000000 | tf_op jit(solution)/shard_map/level_3_1/pallas_call | solution.py:154
  (230 shorter events, 120.2 us)
Async XLA Ops:
  0.9 13.3 %collective-permute-start = (s32[3,32]{1,0:T(4,128)S(1)}, s32[3,32]{1,0:T(4,128)S(1)}, u32[]{:S(2)}, u32[]{:S(2)}) collective-permute-start(s32[3,32]{1,0:T(4,128)S(1)} %reshape.537), channel_id=1, source_target_pairs={{16,0},{17,1},{18,2},{19,3},{20,4},{21,5},{22,6},{23,7},{24,8},{25... | collective-permute-start | bytes 1160 | tf_op jit(solution)/shard_map/ppermute | solution.py:199
  10.7 16.5 %collective-permute-start.4 = (bf16[8,256,128]{2,1,0:T(8,128)(2,1)S(1)}, bf16[8,256,128]{2,1,0:T(8,128)(2,1)S(1)}, u32[]{:S(2)}, u32[]{:S(2)}) collective-permute-start(bf16[8,256,128]{2,1,0:T(8,128)(2,1)S(1)} %get-tuple-element.93.refs_0_), channel_id=1, source_target_pairs={{0,4},{1,5},{2,6},{3,7},{4,8},{5,9},{6,10},{7,11},{8,12},{9,13},{1... | collective-permute-start | bytes 1572872 | tf_op jit(solution)/shard_map/ppermute | solution.py:254
  27.2 15.0 %collective-permute-start.9 = (bf16[8,256,128]{2,1,0:T(8,128)(2,1)S(1)}, bf16[8,256,128]{2,1,0:T(8,128)(2,1)S(1)}, u32[]{:S(2)}, u32[]{:S(2)}) collective-permute-start(bf16[8,256,128]{2,1,0:T(8,128)(2,1)S(1)} %collective-permute-done.4.refs_3_.refs_1_), channel_id=1, source_target_pairs={{0,4},{1,5},{2,6},{3,7},{4,8},{5,9},{6,10},{7,11},{8,12},{9,13},{1... | collective-permute-start | bytes 1572872 | tf_op jit(solution)/shard_map/ppermute | solution.py:254
  35.7 19.0 %collective-permute-start.5 = (bf16[8,256,128]{2,1,0:T(8,128)(2,1)S(1)}, bf16[8,256,128]{2,1,0:T(8,128)(2,1)S(1)}, u32[]{:S(2)}, u32[]{:S(2)}) collective-permute-start(bf16[8,256,128]{2,1,0:T(8,128)(2,1)S(1)} %get-tuple-element.94.refs_2_.refs_4_.refs_0_), channel_id=1, source_target_pairs={{0,4},{1,5},{2,6},{3,7},{4,8},{5,9},{6,10},{7,11},{8,12},{9,13},{1... | collective-permute-start | bytes 1572872 | tf_op jit(solution)/shard_map/ppermute | solution.py:254
  42.2 22.5 %collective-permute-start.10 = (bf16[8,256,128]{2,1,0:T(8,128)(2,1)S(1)}, bf16[8,256,128]{2,1,0:T(8,128)(2,1)S(1)}, u32[]{:S(2)}, u32[]{:S(2)}) collective-permute-start(bf16[8,256,128]{2,1,0:T(8,128)(2,1)S(1)} %collective-permute-done.9.refs_2_), channel_id=1, source_target_pairs={{0,4},{1,5},{2,6},{3,7},{4,8},{5,9},{6,10},{7,11},{8,12},{9,13},{1... | collective-permute-start | bytes 1572872 | tf_op jit(solution)/shard_map/ppermute | solution.py:254
  45.1 23.0 %collective-permute-start.6 = (bf16[4,256,128]{2,1,0:T(8,128)(2,1)}, bf16[4,256,128]{2,1,0:T(8,128)(2,1)}, u32[]{:S(2)}, u32[]{:S(2)}) collective-permute-start(bf16[4,256,128]{2,1,0:T(8,128)(2,1)} %get-tuple-element.96), channel_id=1, source_target_pairs={{0,1},{1,0},{2,3},{3,2},{4,5},{5,4},{6,7},{7,6},{8,9},{9,8},{10,11... | collective-permute-start | bytes 786440 | tf_op jit(solution)/shard_map/ppermute | solution.py:261
  54.7 21.1 %collective-permute-start.18 = (bf16[8,256,128]{2,1,0:T(8,128)(2,1)S(1)}, bf16[8,256,128]{2,1,0:T(8,128)(2,1)S(1)}, u32[]{:S(2)}, u32[]{:S(2)}) collective-permute-start(bf16[8,256,128]{2,1,0:T(8,128)(2,1)S(1)} %collective-permute-done.5.refs_1_), channel_id=1, source_target_pairs={{0,4},{1,5},{2,6},{3,7},{4,8},{5,9},{6,10},{7,11},{8,12},{9,13},{1... | collective-permute-start | bytes 1572872 | tf_op jit(solution)/shard_map/ppermute | solution.py:254
  54.8 14.6 %collective-permute-start.7 = (bf16[4,256,128]{2,1,0:T(8,128)(2,1)}, bf16[4,256,128]{2,1,0:T(8,128)(2,1)S(1)}, u32[]{:S(2)}, u32[]{:S(2)}) collective-permute-start(bf16[4,256,128]{2,1,0:T(8,128)(2,1)} %copy-done.10), channel_id=1, source_target_pairs={{0,2},{1,3},{2,0},{3,1},{4,6},{5,7},{6,4},{7,5},{8,10},{9,11},{10,... | collective-permute-start | bytes 786440 | tf_op jit(solution)/shard_map/ppermute | solution.py:261
  56.3 13.7 %collective-permute-start.8 = (bf16[4,256,128]{2,1,0:T(8,128)(2,1)}, bf16[4,256,128]{2,1,0:T(8,128)(2,1)S(1)}, u32[]{:S(2)}, u32[]{:S(2)}) collective-permute-start(bf16[4,256,128]{2,1,0:T(8,128)(2,1)} %copy-done.9), channel_id=1, source_target_pairs={{0,3},{1,2},{2,1},{3,0},{4,7},{5,6},{6,5},{7,4},{8,11},{9,10},{10,... | collective-permute-start | bytes 786440 | tf_op jit(solution)/shard_map/ppermute | solution.py:261
  80.5 28.1 %collective-permute-start.22 = (bf16[8,256,128]{2,1,0:T(8,128)(2,1)S(1)}, bf16[8,256,128]{2,1,0:T(8,128)(2,1)S(1)}, u32[]{:S(2)}, u32[]{:S(2)}) collective-permute-start(bf16[8,256,128]{2,1,0:T(8,128)(2,1)S(1)} %collective-permute-done.18.rest_13_.refs_2_), channel_id=1, source_target_pairs={{0,4},{1,5},{2,6},{3,7},{4,8},{5,9},{6,10},{7,11},{8,12},{9,13},{1... | collective-permute-start | bytes 1572872 | tf_op jit(solution)/shard_map/ppermute | solution.py:254
  104.2 14.8 %collective-permute-start.30 = (bf16[8,256,128]{2,1,0:T(8,128)(2,1)S(1)}, bf16[8,256,128]{2,1,0:T(8,128)(2,1)S(1)}, u32[]{:S(2)}, u32[]{:S(2)}) collective-permute-start(bf16[8,256,128]{2,1,0:T(8,128)(2,1)S(1)} %get-tuple-element.108.refs_2_.refs_4_), channel_id=1, source_target_pairs={{0,4},{1,5},{2,6},{3,7},{4,8},{5,9},{6,10},{7,11},{8,12},{9,13},{1... | collective-permute-start | bytes 1572872 | tf_op jit(solution)/shard_map/ppermute | solution.py:254
  107.1 13.5 %collective-permute-start.20 = (bf16[4,256,128]{2,1,0:T(8,128)(2,1)S(1)}, bf16[4,256,128]{2,1,0:T(8,128)(2,1)S(1)}, u32[]{:S(2)}, u32[]{:S(2)}) collective-permute-start(bf16[4,256,128]{2,1,0:T(8,128)(2,1)S(1)} %get-tuple-element.111), channel_id=1, source_target_pairs={{0,2},{1,3},{2,0},{3,1},{4,6},{5,7},{6,4},{7,5},{8,10},{9,11},{10,... | collective-permute-start | bytes 786440 | tf_op jit(solution)/shard_map/ppermute | solution.py:261
  107.5 13.2 %collective-permute-start.21 = (bf16[4,256,128]{2,1,0:T(8,128)(2,1)S(1)}, bf16[4,256,128]{2,1,0:T(8,128)(2,1)S(1)}, u32[]{:S(2)}, u32[]{:S(2)}) collective-permute-start(bf16[4,256,128]{2,1,0:T(8,128)(2,1)S(1)} %get-tuple-element.112), channel_id=1, source_target_pairs={{0,3},{1,2},{2,1},{3,0},{4,7},{5,6},{6,5},{7,4},{8,11},{9,10},{10,... | collective-permute-start | bytes 786440 | tf_op jit(solution)/shard_map/ppermute | solution.py:261
  110.9 14.6 %collective-permute-start.23 = (bf16[4,256,128]{2,1,0:T(8,128)(2,1)S(1)}, bf16[4,256,128]{2,1,0:T(8,128)(2,1)S(1)}, u32[]{:S(2)}, u32[]{:S(2)}) collective-permute-start(bf16[4,256,128]{2,1,0:T(8,128)(2,1)S(1)} %get-tuple-element.114), channel_id=1, source_target_pairs={{0,1},{1,0},{2,3},{3,2},{4,5},{5,4},{6,7},{7,6},{8,9},{9,8},{10,11... | collective-permute-start | bytes 786440 | tf_op jit(solution)/shard_map/ppermute | solution.py:261
  114.2 17.3 %collective-permute-start.24 = (bf16[4,256,128]{2,1,0:T(8,128)(2,1)S(1)}, bf16[4,256,128]{2,1,0:T(8,128)(2,1)S(1)}, u32[]{:S(2)}, u32[]{:S(2)}) collective-permute-start(bf16[4,256,128]{2,1,0:T(8,128)(2,1)S(1)} %get-tuple-element.115), channel_id=1, source_target_pairs={{0,2},{1,3},{2,0},{3,1},{4,6},{5,7},{6,4},{7,5},{8,10},{9,11},{10,... | collective-permute-start | bytes 786440 | tf_op jit(solution)/shard_map/ppermute | solution.py:261
  119.0 15.3 %collective-permute-start.31 = (bf16[8,256,128]{2,1,0:T(8,128)(2,1)S(1)}, bf16[8,256,128]{2,1,0:T(8,128)(2,1)S(1)}, u32[]{:S(2)}, u32[]{:S(2)}) collective-permute-start(bf16[8,256,128]{2,1,0:T(8,128)(2,1)S(1)} %collective-permute-done.30.refs_3_.refs_5_), channel_id=1, source_target_pairs={{0,4},{1,5},{2,6},{3,7},{4,8},{5,9},{6,10},{7,11},{8,12},{9,13},{1... | collective-permute-start | bytes 1572872 | tf_op jit(solution)/shard_map/ppermute | solution.py:254
  120.7 16.4 %collective-permute-start.26 = (bf16[4,256,128]{2,1,0:T(8,128)(2,1)S(1)}, bf16[4,256,128]{2,1,0:T(8,128)(2,1)S(1)}, u32[]{:S(2)}, u32[]{:S(2)}) collective-permute-start(bf16[4,256,128]{2,1,0:T(8,128)(2,1)S(1)} %get-tuple-element.117), channel_id=1, source_target_pairs={{0,16},{1,17},{2,18},{3,19},{4,20},{5,21},{6,22},{7,23},{8,24},{9,... | collective-permute-start | bytes 786440 | tf_op jit(solution)/shard_map/ppermute | solution.py:268
  134.3 20.8 %collective-permute-start.36 = (bf16[8,256,128]{2,1,0:T(8,128)(2,1)S(1)}, bf16[8,256,128]{2,1,0:T(8,128)(2,1)S(1)}, u32[]{:S(2)}, u32[]{:S(2)}) collective-permute-start(bf16[8,256,128]{2,1,0:T(8,128)(2,1)S(1)} %collective-permute-done.31.rest_13_.refs_6_), channel_id=1, source_target_pairs={{0,4},{1,5},{2,6},{3,7},{4,8},{5,9},{6,10},{7,11},{8,12},{9,13},{1... | collective-permute-start | bytes 1572872 | tf_op jit(solution)/shard_map/ppermute | solution.py:254
  147.7 14.6 %collective-permute-start.32 = (bf16[8,256,128]{2,1,0:T(8,128)(2,1)S(1)}, bf16[8,256,128]{2,1,0:T(8,128)(2,1)S(1)}, u32[]{:S(2)}, u32[]{:S(2)}) collective-permute-start(bf16[8,256,128]{2,1,0:T(8,128)(2,1)S(1)} %get-tuple-element.122.refs_4_.refs_8_.refs_2_), channel_id=1, source_target_pairs={{0,4},{1,5},{2,6},{3,7},{4,8},{5,9},{6,10},{7,11},{8,12},{9,13},{1... | collective-permute-start | bytes 1572872 | tf_op jit(solution)/shard_map/ppermute | solution.py:254
  152.4 13.9 %collective-permute-start.34 = (bf16[4,256,128]{2,1,0:T(8,128)(2,1)S(1)}, bf16[4,256,128]{2,1,0:T(8,128)(2,1)S(1)}, u32[]{:S(2)}, u32[]{:S(2)}) collective-permute-start(bf16[4,256,128]{2,1,0:T(8,128)(2,1)S(1)} %get-tuple-element.125), channel_id=1, source_target_pairs={{0,2},{1,3},{2,0},{3,1},{4,6},{5,7},{6,4},{7,5},{8,10},{9,11},{10,... | collective-permute-start | bytes 786440 | tf_op jit(solution)/shard_map/ppermute | solution.py:261
  153.4 13.0 %collective-permute-start.35 = (bf16[4,256,128]{2,1,0:T(8,128)(2,1)S(1)}, bf16[4,256,128]{2,1,0:T(8,128)(2,1)S(1)}, u32[]{:S(2)}, u32[]{:S(2)}) collective-permute-start(bf16[4,256,128]{2,1,0:T(8,128)(2,1)S(1)} %get-tuple-element.126), channel_id=1, source_target_pairs={{0,3},{1,2},{2,1},{3,0},{4,7},{5,6},{6,5},{7,4},{8,11},{9,10},{10,... | collective-permute-start | bytes 786440 | tf_op jit(solution)/shard_map/ppermute | solution.py:261
  157.2 14.3 %collective-permute-start.37 = (bf16[4,256,128]{2,1,0:T(8,128)(2,1)S(1)}, bf16[4,256,128]{2,1,0:T(8,128)(2,1)S(1)}, u32[]{:S(2)}, u32[]{:S(2)}) collective-permute-start(bf16[4,256,128]{2,1,0:T(8,128)(2,1)S(1)} %get-tuple-element.128), channel_id=1, source_target_pairs={{0,1},{1,0},{2,3},{3,2},{4,5},{5,4},{6,7},{7,6},{8,9},{9,8},{10,11... | collective-permute-start | bytes 786440 | tf_op jit(solution)/shard_map/ppermute | solution.py:261
  160.8 16.8 %collective-permute-start.38 = (bf16[4,256,128]{2,1,0:T(8,128)(2,1)S(1)}, bf16[4,256,128]{2,1,0:T(8,128)(2,1)S(1)}, u32[]{:S(2)}, u32[]{:S(2)}) collective-permute-start(bf16[4,256,128]{2,1,0:T(8,128)(2,1)S(1)} %get-tuple-element.129), channel_id=1, source_target_pairs={{0,2},{1,3},{2,0},{3,1},{4,6},{5,7},{6,4},{7,5},{8,10},{9,11},{10,... | collective-permute-start | bytes 786440 | tf_op jit(solution)/shard_map/ppermute | solution.py:261
  162.3 17.9 %collective-permute-start.44 = (bf16[8,256,128]{2,1,0:T(8,128)(2,1)S(1)}, bf16[8,256,128]{2,1,0:T(8,128)(2,1)S(1)}, u32[]{:S(2)}, u32[]{:S(2)}) collective-permute-start(bf16[8,256,128]{2,1,0:T(8,128)(2,1)S(1)} %collective-permute-done.32.refs_3_.refs_5_), channel_id=1, source_target_pairs={{0,4},{1,5},{2,6},{3,7},{4,8},{5,9},{6,10},{7,11},{8,12},{9,13},{1... | collective-permute-start | bytes 1572872 | tf_op jit(solution)/shard_map/ppermute | solution.py:254
  166.3 12.6 %collective-permute-start.39 = (bf16[4,256,128]{2,1,0:T(8,128)(2,1)S(1)}, bf16[4,256,128]{2,1,0:T(8,128)(2,1)S(1)}, u32[]{:S(2)}, u32[]{:S(2)}) collective-permute-start(bf16[4,256,128]{2,1,0:T(8,128)(2,1)S(1)} %get-tuple-element.130), channel_id=1, source_target_pairs={{0,3},{1,2},{2,1},{3,0},{4,7},{5,6},{6,5},{7,4},{8,11},{9,10},{10,... | collective-permute-start | bytes 786440 | tf_op jit(solution)/shard_map/ppermute | solution.py:261
  166.4 14.0 %collective-permute-start.40 = (bf16[4,256,128]{2,1,0:T(8,128)(2,1)S(1)}, bf16[4,256,128]{2,1,0:T(8,128)(2,1)S(1)}, u32[]{:S(2)}, u32[]{:S(2)}) collective-permute-start(bf16[4,256,128]{2,1,0:T(8,128)(2,1)S(1)} %get-tuple-element.131), channel_id=1, source_target_pairs={{0,16},{1,17},{2,18},{3,19},{4,20},{5,21},{6,22},{7,23},{8,24},{9,... | collective-permute-start | bytes 786440 | tf_op jit(solution)/shard_map/ppermute | solution.py:268
  180.2 18.0 %collective-permute-start.48 = (bf16[8,256,128]{2,1,0:T(8,128)(2,1)S(1)}, bf16[8,256,128]{2,1,0:T(8,128)(2,1)S(1)}, u32[]{:S(2)}, u32[]{:S(2)}) collective-permute-start(bf16[8,256,128]{2,1,0:T(8,128)(2,1)S(1)} %collective-permute-done.44.rest_13_.refs_6_), channel_id=1, source_target_pairs={{0,4},{1,5},{2,6},{3,7},{4,8},{5,9},{6,10},{7,11},{8,12},{9,13},{1... | collective-permute-start | bytes 1572872 | tf_op jit(solution)/shard_map/ppermute | solution.py:254
  193.8 16.2 %collective-permute-start.56 = (bf16[8,256,128]{2,1,0:T(8,128)(2,1)S(1)}, bf16[8,256,128]{2,1,0:T(8,128)(2,1)S(1)}, u32[]{:S(2)}, u32[]{:S(2)}) collective-permute-start(bf16[8,256,128]{2,1,0:T(8,128)(2,1)S(1)} %get-tuple-element.136.refs_4_.refs_8_), channel_id=1, source_target_pairs={{0,4},{1,5},{2,6},{3,7},{4,8},{5,9},{6,10},{7,11},{8,12},{9,13},{1... | collective-permute-start | bytes 1572872 | tf_op jit(solution)/shard_map/ppermute | solution.py:254
  196.1 13.9 %collective-permute-start.46 = (bf16[4,256,128]{2,1,0:T(8,128)(2,1)S(1)}, bf16[4,256,128]{2,1,0:T(8,128)(2,1)S(1)}, u32[]{:S(2)}, u32[]{:S(2)}) collective-permute-start(bf16[4,256,128]{2,1,0:T(8,128)(2,1)S(1)} %get-tuple-element.139), channel_id=1, source_target_pairs={{0,2},{1,3},{2,0},{3,1},{4,6},{5,7},{6,4},{7,5},{8,10},{9,11},{10,... | collective-permute-start | bytes 786440 | tf_op jit(solution)/shard_map/ppermute | solution.py:261
  197.1 14.7 %collective-permute-start.47 = (bf16[4,256,128]{2,1,0:T(8,128)(2,1)S(1)}, bf16[4,256,128]{2,1,0:T(8,128)(2,1)S(1)}, u32[]{:S(2)}, u32[]{:S(2)}) collective-permute-start(bf16[4,256,128]{2,1,0:T(8,128)(2,1)S(1)} %get-tuple-element.140), channel_id=1, source_target_pairs={{0,3},{1,2},{2,1},{3,0},{4,7},{5,6},{6,5},{7,4},{8,11},{9,10},{10,... | collective-permute-start | bytes 786440 | tf_op jit(solution)/shard_map/ppermute | solution.py:261
  200.6 14.3 %collective-permute-start.49 = (bf16[4,256,128]{2,1,0:T(8,128)(2,1)S(1)}, bf16[4,256,128]{2,1,0:T(8,128)(2,1)S(1)}, u32[]{:S(2)}, u32[]{:S(2)}) collective-permute-start(bf16[4,256,128]{2,1,0:T(8,128)(2,1)S(1)} %get-tuple-element.142), channel_id=1, source_target_pairs={{0,1},{1,0},{2,3},{3,2},{4,5},{5,4},{6,7},{7,6},{8,9},{9,8},{10,11... | collective-permute-start | bytes 786440 | tf_op jit(solution)/shard_map/ppermute | solution.py:261
  204.0 17.2 %collective-permute-start.50 = (bf16[4,256,128]{2,1,0:T(8,128)(2,1)S(1)}, bf16[4,256,128]{2,1,0:T(8,128)(2,1)S(1)}, u32[]{:S(2)}, u32[]{:S(2)}) collective-permute-start(bf16[4,256,128]{2,1,0:T(8,128)(2,1)S(1)} %get-tuple-element.143), channel_id=1, source_target_pairs={{0,2},{1,3},{2,0},{3,1},{4,6},{5,7},{6,4},{7,5},{8,10},{9,11},{10,... | collective-permute-start | bytes 786440 | tf_op jit(solution)/shard_map/ppermute | solution.py:261
  209.9 12.5 %collective-permute-start.51 = (bf16[4,256,128]{2,1,0:T(8,128)(2,1)S(1)}, bf16[4,256,128]{2,1,0:T(8,128)(2,1)S(1)}, u32[]{:S(2)}, u32[]{:S(2)}) collective-permute-start(bf16[4,256,128]{2,1,0:T(8,128)(2,1)S(1)} %get-tuple-element.144), channel_id=1, source_target_pairs={{0,3},{1,2},{2,1},{3,0},{4,7},{5,6},{6,5},{7,4},{8,11},{9,10},{10,... | collective-permute-start | bytes 786440 | tf_op jit(solution)/shard_map/ppermute | solution.py:261
  209.9 21.7 %collective-permute-start.57 = (bf16[8,256,128]{2,1,0:T(8,128)(2,1)S(1)}, bf16[8,256,128]{2,1,0:T(8,128)(2,1)S(1)}, u32[]{:S(2)}, u32[]{:S(2)}) collective-permute-start(bf16[8,256,128]{2,1,0:T(8,128)(2,1)S(1)} %collective-permute-done.56.refs_5_.refs_9_), channel_id=1, source_target_pairs={{0,4},{1,5},{2,6},{3,7},{4,8},{5,9},{6,10},{7,11},{8,12},{9,13},{1... | collective-permute-start | bytes 1572872 | tf_op jit(solution)/shard_map/ppermute | solution.py:254
  237.0 15.8 %collective-permute-start.58 = (bf16[8,256,128]{2,1,0:T(8,128)(2,1)S(1)}, bf16[8,256,128]{2,1,0:T(8,128)(2,1)S(1)}, u32[]{:S(2)}, u32[]{:S(2)}) collective-permute-start(bf16[8,256,128]{2,1,0:T(8,128)(2,1)S(1)} %get-tuple-element.150.refs_6_.refs_12_.refs_4_.refs_8_), channel_id=1, source_target_pairs={{0,4},{1,5},{2,6},{3,7},{4,8},{5,9},{6,10},{7,11},{8,12},{9,13},{1... | collective-permute-start | bytes 1572872 | tf_op jit(solution)/shard_map/ppermute | solution.py:254
  237.6 26.5 %collective-permute-start.62 = (bf16[8,256,128]{2,1,0:T(8,128)(2,1)S(1)}, bf16[8,256,128]{2,1,0:T(8,128)(2,1)S(1)}, u32[]{:S(2)}, u32[]{:S(2)}) collective-permute-start(bf16[8,256,128]{2,1,0:T(8,128)(2,1)S(1)} %collective-permute-done.57.rest_13_.refs_10_), channel_id=1, source_target_pairs={{0,4},{1,5},{2,6},{3,7},{4,8},{5,9},{6,10},{7,11},{8,12},{9,13},{1... | collective-permute-start | bytes 1572872 | tf_op jit(solution)/shard_map/ppermute | solution.py:254
  252.8 22.1 %collective-permute-start.70 = (bf16[8,256,128]{2,1,0:T(8,128)(2,1)S(1)}, bf16[8,256,128]{2,1,0:T(8,128)(2,1)S(1)}, u32[]{:S(2)}, u32[]{:S(2)}) collective-permute-start(bf16[8,256,128]{2,1,0:T(8,128)(2,1)S(1)} %collective-permute-done.58.refs_5_.refs_9_), channel_id=1, source_target_pairs={{0,4},{1,5},{2,6},{3,7},{4,8},{5,9},{6,10},{7,11},{8,12},{9,13},{1... | collective-permute-start | bytes 1572872 | tf_op jit(solution)/shard_map/ppermute | solution.py:254
  254.9 13.2 %collective-permute-start.60 = (bf16[4,256,128]{2,1,0:T(8,128)(2,1)S(1)}, bf16[4,256,128]{2,1,0:T(8,128)(2,1)S(1)}, u32[]{:S(2)}, u32[]{:S(2)}) collective-permute-start(bf16[4,256,128]{2,1,0:T(8,128)(2,1)S(1)} %get-tuple-element.153), channel_id=1, source_target_pairs={{0,2},{1,3},{2,0},{3,1},{4,6},{5,7},{6,4},{7,5},{8,10},{9,11},{10,... | collective-permute-start | bytes 786440 | tf_op jit(solution)/shard_map/ppermute | solution.py:261
  256.3 18.7 %collective-permute-start.61 = (bf16[4,256,128]{2,1,0:T(8,128)(2,1)S(1)}, bf16[4,256,128]{2,1,0:T(8,128)(2,1)S(1)}, u32[]{:S(2)}, u32[]{:S(2)}) collective-permute-start(bf16[4,256,128]{2,1,0:T(8,128)(2,1)S(1)} %get-tuple-element.154), channel_id=1, source_target_pairs={{0,3},{1,2},{2,1},{3,0},{4,7},{5,6},{6,5},{7,4},{8,11},{9,10},{10,... | collective-permute-start | bytes 786440 | tf_op jit(solution)/shard_map/ppermute | solution.py:261
  266.7 12.8 %collective-permute-start.64 = (bf16[4,256,128]{2,1,0:T(8,128)(2,1)S(1)}, bf16[4,256,128]{2,1,0:T(8,128)(2,1)S(1)}, u32[]{:S(2)}, u32[]{:S(2)}) collective-permute-start(bf16[4,256,128]{2,1,0:T(8,128)(2,1)S(1)} %get-tuple-element.157), channel_id=1, source_target_pairs={{0,2},{1,3},{2,0},{3,1},{4,6},{5,7},{6,4},{7,5},{8,10},{9,11},{10,... | collective-permute-start | bytes 786440 | tf_op jit(solution)/shard_map/ppermute | solution.py:261
  268.1 12.7 %collective-permute-start.65 = (bf16[4,256,128]{2,1,0:T(8,128)(2,1)S(1)}, bf16[4,256,128]{2,1,0:T(8,128)(2,1)S(1)}, u32[]{:S(2)}, u32[]{:S(2)}) collective-permute-start(bf16[4,256,128]{2,1,0:T(8,128)(2,1)S(1)} %get-tuple-element.158), channel_id=1, source_target_pairs={{0,3},{1,2},{2,1},{3,0},{4,7},{5,6},{6,5},{7,4},{8,11},{9,10},{10,... | collective-permute-start | bytes 786440 | tf_op jit(solution)/shard_map/ppermute | solution.py:261
  275.0 25.9 %collective-permute-start.74 = (bf16[8,256,128]{2,1,0:T(8,128)(2,1)S(1)}, bf16[8,256,128]{2,1,0:T(8,128)(2,1)S(1)}, u32[]{:S(2)}, u32[]{:S(2)}) collective-permute-start(bf16[8,256,128]{2,1,0:T(8,128)(2,1)S(1)} %collective-permute-done.70.rest_13_.refs_10_), channel_id=1, source_target_pairs={{0,4},{1,5},{2,6},{3,7},{4,8},{5,9},{6,10},{7,11},{8,12},{9,13},{1... | collective-permute-start | bytes 1572872 | tf_op jit(solution)/shard_map/ppermute | solution.py:254
  299.8 13.4 %collective-permute-start.73 = (bf16[4,256,128]{2,1,0:T(8,128)(2,1)S(1)}, bf16[4,256,128]{2,1,0:T(8,128)(2,1)S(1)}, u32[]{:S(2)}, u32[]{:S(2)}) collective-permute-start(bf16[4,256,128]{2,1,0:T(8,128)(2,1)S(1)} %get-tuple-element.168), channel_id=1, source_target_pairs={{0,3},{1,2},{2,1},{3,0},{4,7},{5,6},{6,5},{7,4},{8,11},{9,10},{10,... | collective-permute-start | bytes 786440 | tf_op jit(solution)/shard_map/ppermute | solution.py:261
  303.0 14.2 %collective-permute-start.75 = (bf16[4,256,128]{2,1,0:T(8,128)(2,1)S(1)}, bf16[4,256,128]{2,1,0:T(8,128)(2,1)S(1)}, u32[]{:S(2)}, u32[]{:S(2)}) collective-permute-start(bf16[4,256,128]{2,1,0:T(8,128)(2,1)S(1)} %get-tuple-element.170), channel_id=1, source_target_pairs={{0,1},{1,0},{2,3},{3,2},{4,5},{5,4},{6,7},{7,6},{8,9},{9,8},{10,11... | collective-permute-start | bytes 786440 | tf_op jit(solution)/shard_map/ppermute | solution.py:261
  303.4 15.8 %collective-permute-start.76 = (bf16[4,256,128]{2,1,0:T(8,128)(2,1)S(1)}, bf16[4,256,128]{2,1,0:T(8,128)(2,1)S(1)}, u32[]{:S(2)}, u32[]{:S(2)}) collective-permute-start(bf16[4,256,128]{2,1,0:T(8,128)(2,1)S(1)} %get-tuple-element.171), channel_id=1, source_target_pairs={{0,2},{1,3},{2,0},{3,1},{4,6},{5,7},{6,4},{7,5},{8,10},{9,11},{10,... | collective-permute-start | bytes 786440 | tf_op jit(solution)/shard_map/ppermute | solution.py:261
  305.9 18.5 %collective-permute-start.77 = (bf16[4,256,128]{2,1,0:T(8,128)(2,1)S(1)}, bf16[4,256,128]{2,1,0:T(8,128)(2,1)S(1)}, u32[]{:S(2)}, u32[]{:S(2)}) collective-permute-start(bf16[4,256,128]{2,1,0:T(8,128)(2,1)S(1)} %get-tuple-element.172), channel_id=1, source_target_pairs={{0,3},{1,2},{2,1},{3,0},{4,7},{5,6},{6,5},{7,4},{8,11},{9,10},{10,... | collective-permute-start | bytes 786440 | tf_op jit(solution)/shard_map/ppermute | solution.py:261
  307.9 16.6 %collective-permute-start.78 = (bf16[4,256,128]{2,1,0:T(8,128)(2,1)S(1)}, bf16[4,256,128]{2,1,0:T(8,128)(2,1)S(1)}, u32[]{:S(2)}, u32[]{:S(2)}) collective-permute-start(bf16[4,256,128]{2,1,0:T(8,128)(2,1)S(1)} %get-tuple-element.173), channel_id=1, source_target_pairs={{0,16},{1,17},{2,18},{3,19},{4,20},{5,21},{6,22},{7,23},{8,24},{9,... | collective-permute-start | bytes 786440 | tf_op jit(solution)/shard_map/ppermute | solution.py:268
  313.2 12.5 %collective-permute-start.79 = (bf16[4,256,128]{2,1,0:T(8,128)(2,1)S(1)}, bf16[4,256,128]{2,1,0:T(8,128)(2,1)S(1)}, u32[]{:S(2)}, u32[]{:S(2)}) collective-permute-start(bf16[4,256,128]{2,1,0:T(8,128)(2,1)S(1)} %get-tuple-element.174), channel_id=1, source_target_pairs={{0,17},{1,16},{2,19},{3,18},{4,21},{5,20},{6,23},{7,22},{8,25},{9,... | collective-permute-start | bytes 786440 | tf_op jit(solution)/shard_map/ppermute | solution.py:268
  (45 other events, 413.1 us)

commit v3 on v2

--- a/solution.py
+++ b/solution.py
@@ -19,41 +19,99 @@
     return pltpu.CompilerParams(vmem_limit_bytes=mib * 1024 * 1024)
 
 
-def first_level(chol, noise, out, half, after=()):
+def level_blocks(places, factors, chol, noise, got, out, section, half, after=()):
     depth, blocks, rows, _ = chol.shape
+    slots = factors.shape[2]
     width = noise.shape[3] // HALVES
+    sizes = [array.shape[0] for array in got]
+    starts = [sum(sizes[:i]) for i in range(len(sizes))]
+    n_got, first = len(sizes), section == 0
+    carried = [] if out is None else [out]
+    n_in = 3 + (not first) + n_got
+    columns = pl.ds(half * width, width)
 
     def body(*refs):
-        lower, draws, latest, full = refs[0], refs[1], refs[-2], refs[-1]
-        value = jnp.dot(lower[0, 0], draws[0, 0], preferred_element_type=jnp.float32)
-        value = value.astype(jnp.bfloat16)
-        latest[0] = value
-        full[0, 0] = value
-
-    carried = [] if out is None else [out, *after]
+        tbl, lower_all, draws_all = refs[:3]
+        arrived = refs[n_in - n_got : n_in]
+        latest, full, lower, draws, sems, *rest = refs[n_in + len(carried) + len(after) :]
+        if not first:
+            mats_all, (mats, held, got_sems) = refs[3], rest
+
+        def fetches(b):
+            moves = [
+                pltpu.make_async_copy(lower_all.at[section, b], lower.at[b], sems.at[0, b]),
+                pltpu.make_async_copy(
+                    draws_all.at[section, b, :, columns], draws.at[b], sems.at[1, b]
+                ),
+            ]
+            if not first:
+                moves.append(
+                    pltpu.make_async_copy(mats_all.at[section - 1, b], mats.at[b], sems.at[2, b])
+                )
+            return moves
+
+        def gather(i):
+            return pltpu.make_async_copy(
+                arrived[i], held.at[pl.ds(starts[i], sizes[i])], got_sems.at[i]
+            )
+
+        def store(b):
+            return pltpu.make_async_copy(
+                latest.at[b], full.at[section, b, :, columns], sems.at[3, b]
+            )
+
+        for move in fetches(0):
+            move.start()
+        for i in range(n_got):
+            gather(i).start()
+        for b in range(1, blocks):
+            for move in fetches(b):
+                move.start()
+        for i in range(n_got):
+            gather(i).wait()
+        for b in range(blocks):
+            for move in fetches(b):
+                move.wait()
+            total = jnp.dot(lower[b], draws[b], preferred_element_type=jnp.float32)
+            if not first:
+                for j in range(slots):
+                    place = tbl[b * slots + j]
+                    parent = held[jnp.maximum(place, 0)]
+                    parent = jnp.where(place >= 0, parent, jnp.zeros_like(parent))
+                    total += jnp.dot(mats[b, j], parent, preferred_element_type=jnp.float32)
+            latest[b] = total.astype(jnp.bfloat16)
+            store(b).start()
+        for b in range(blocks):
+            store(b).wait()
+
+    scratch = [
+        pltpu.VMEM((blocks, rows, rows), jnp.bfloat16),
+        pltpu.VMEM((blocks, rows, width), jnp.bfloat16),
+        pltpu.SemaphoreType.DMA((4, blocks)),
+    ]
+    if not first:
+        scratch += [
+            pltpu.VMEM((blocks, slots, rows, rows), jnp.bfloat16),
+            pltpu.VMEM((sum(sizes), rows, width), jnp.bfloat16),
+            pltpu.SemaphoreType.DMA((n_got,)),
+        ]
     return pl.pallas_call(
         body,
-        grid=(blocks,),
-        in_specs=[
-            pl.BlockSpec((1, 1, rows, rows), lambda b: (0, b, 0, 0)),
-            pl.BlockSpec((1, 1, rows, width), lambda b: (0, b, 0, half)),
-        ]
-        + [ANY] * len(carried),
-        out_specs=[
-            pl.BlockSpec((1, rows, width), lambda b: (b, 0, 0)),
-            pl.BlockSpec((1, 1, rows, width), lambda b: (0, b, 0, half)),
-        ],
+        in_specs=[pl.BlockSpec(memory_space=pltpu.SMEM)]
+        + [ANY] * (n_in - 1 + len(carried) + len(after)),
+        out_specs=[pl.BlockSpec(memory_space=pltpu.VMEM), ANY],
         out_shape=[
             jax.ShapeDtypeStruct((blocks, rows, width), jnp.bfloat16),
             jax.ShapeDtypeStruct(noise.shape, jnp.bfloat16),
         ],
-        input_output_aliases={2: 1} if carried else {},
-        compiler_params=params(8),
+        scratch_shapes=scratch,
+        input_output_aliases={n_in: 1} if carried else {},
+        compiler_params=params(56 if first else 48),
         cost_estimate=pl.CostEstimate(
-            flops=2 * blocks * rows * rows * width, bytes_accessed=4_000_000, transcendentals=0
+            flops=2 * blocks * rows * rows * width, bytes_accessed=8_000_000, transcendentals=0
         ),
-        name=f"first_{half}",
-    )(chol, noise, *carried)
+        name=f"level_{section}_{half}",
+    )(places, chol, noise, *([] if first else [factors]), *got, *carried, *after)
 
 
 def pick(table, held, group, name, after=()):
@@ -110,78 +168,6 @@
         name=name,
     )(table, *flat, *after)
     return out[:n_same], out[n_same:]
-
-
-def next_level(places, factors, chol, noise, got, out, section, half, after=()):
-    depth, blocks, rows, _ = chol.shape
-    slots = factors.shape[2]
-    width = noise.shape[3] // HALVES
-    sizes = [ref.shape[0] for ref in got]
-    starts = [sum(sizes[:i]) for i in range(len(sizes))]
-
-    def body(tbl, mats, lower, draws, *rest):
-        got = rest[: len(sizes)]
-        latest, full, held, sems = rest[len(sizes) + 1 + len(after) :]
-        block = pl.program_id(0)
-
-        def fetch(i):
-            return pltpu.make_async_copy(
-                got[i], held.at[pl.ds(starts[i], sizes[i])], sems.at[i]
-            )
-
-        @pl.when(block == 0)
-        def _():
-            for i in range(len(sizes)):
-                fetch(i).start()
-
-        total = jnp.dot(lower[0, 0], draws[0, 0], preferred_element_type=jnp.float32)
-
-        @pl.when(block == 0)
-        def _():
-            for i in range(len(sizes)):
-                fetch(i).wait()
-
-        for j in range(slots):
-            place = tbl[block * slots + j]
-            parent = held[jnp.maximum(place, 0)]
-            parent = jnp.where(place >= 0, parent, jnp.zeros_like(parent))
-            total += jnp.dot(mats[0, 0, j], parent, preferred_element_type=jnp.float32)
-        value = total.astype(jnp.bfloat16)
-        latest[0] = value
-        full[0, 0] = value
-
-    n_got = len(sizes)
-    return pl.pallas_call(
-        body,
-        grid=(blocks,),
-        in_specs=[
-            pl.BlockSpec(memory_space=pltpu.SMEM),
-            pl.BlockSpec((1, 1, slots, rows, rows), lambda b: (section - 1, b, 0, 0, 0)),
-            pl.BlockSpec((1, 1, rows, rows), lambda b: (section, b, 0, 0)),
-            pl.BlockSpec((1, 1, rows, width), lambda b: (section, b, 0, half)),
-        ]
-        + [ANY] * (n_got + 1 + len(after)),
-        out_specs=[
-            pl.BlockSpec((1, rows, width), lambda b: (b, 0, 0)),
-            pl.BlockSpec((1, 1, rows, width), lambda b: (section, b, 0, half)),
-        ],
-        out_shape=[
-            jax.ShapeDtypeStruct((blocks, rows, width), jnp.bfloat16),
-            jax.ShapeDtypeStruct(noise.shape, jnp.bfloat16),
-        ],
-        scratch_shapes=[
-            pltpu.VMEM((sum(sizes), rows, width), jnp.bfloat16),
-            pltpu.SemaphoreType.DMA((n_got,)),
-        ],
-        input_output_aliases={4 + n_got: 1},
-        compiler_params=params(12),
-        cost_estimate=pl.CostEstimate(
-            flops=2 * (slots + 1) * blocks * rows * rows * width,
-            bytes_accessed=10_000_000,
-            transcendentals=0,
-        ),
-        name=f"level_{section}_{half}",
-    )(places, factors, chol, noise, *got, out, *after)
 
 
 def ranks(active, lane):
@@ -290,21 +276,19 @@
             got += swap_plane(same, prior, peer_count, tile_count)
         return got
 
-    lead, out = first_level(chol, noise, None, 0)
+    args = factors, chol, noise
+    lead, out = level_blocks(places[0], *args, [], None, 0, 0)
     ring = spread(lead, 0)
-    lag, out = first_level(chol, noise, out, 1, [ring[1]])
+    lag, out = level_blocks(places[0], *args, [], out, 0, 1, [ring[1]])
     got = swap(0, 0, [lag])
     ring = spread(lag, 1)
     for section in range(1, depth):
         more = section + 1 < depth
-        lead, out = next_level(
-            places[section - 1], factors, chol, noise, got, out, section, 0, [ring[2]]
-        )
+        at = places[section - 1]
+        lead, out = level_blocks(at, *args, got, out, section, 0, [ring[2]])
         lag_got = swap(section - 1, 1, [lead])
         ring = spread(lead, 0) if more else None
-        lag, out = next_level(
-            places[section - 1], factors, chol, noise, lag_got, out, section, 1, [ring[2]] if more else ()
-        )
+        lag, out = level_blocks(at, *args, lag_got, out, section, 1, [ring[2]] if more else ())
         if more:
             got = swap(section, 0, [lag])
             ring = spread(lag, 1)

time: 338 us -> 331 us (0.979)
  local copies, waits for them, and re-layouts: 30.1 us -> 10.4 us
  starting transfers between devices: 77.5 us -> 87.5 us
  Pallas kernels: 63.5 us -> 68.2 us
    unnamed x39 -> x37, local copies, waits for them, and re-layouts: 25.8 us -> 6.02 us
    ppermute x36, waiting for transfers between devices: 58.7 us -> 45.8 us  [swap_plane(): got.append(lax.ppermute(same[k], 'lvl', across(k, peer_count)))]
    ppermute x18, waiting for transfers between devices: 55.7 us -> 66.7 us  [ring_z(): held.append(lax.ppermute(held[-1], 'lvl', links))]
    ppermute x36, starting transfers between devices: 29.5 us -> 37.4 us  [swap_plane(): got.append(lax.ppermute(same[k], 'lvl', across(k, peer_count)))]
    pallas_call x8, Pallas kernels: 40.1 us -> 45.2 us  [level_blocks(): pl.pallas_call(body, in_specs=[pl.BlockSpec(memory_space=pltpu.SMEM)] + [...]
    ppermute x24, waiting for transfers between devices: 43.7 us -> 47.9 us  [swap_plane(): got.append(lax.ppermute(prior[k], ('tile', 'lvl'), links))]
  transfers between devices with their start and end apart: 82 -> 82, of which waited for: 43 -> 40; matrix products, arithmetic and copies ran while one was open for 4% -> 2% of each run, Pallas kernels for 16% -> 17%
where the time goes in v3:
time: 331 us; the launch traced here: 329 us
  waiting for transfers between devices  160 us (48%)
  starting transfers between devices  87.5 us (26%)
  Pallas kernels  68.2 us (21%)
  local copies, waits for them, and re-layouts  10.4 us (3%)
    ppermute x18, waiting for transfers between devices, ring_z(): held.append(lax.ppermute(held[-1], 'lvl', links))  66.7 us
    ppermute x24, waiting for transfers between devices, swap_plane(): got.append(lax.ppermute(prior[k], ('tile', 'lvl'), links))  47.9 us
    ppermute x36, waiting for transfers between devices, swap_plane(): got.append(lax.ppermute(same[k], 'lvl', across(k, peer_count)))  45.8 us
    pallas_call x8, Pallas kernels, level_blocks(): pl.pallas_call(body, in_specs=[pl.BlockSpec(memory_space=pltpu.SMEM)] + [...  45.2 us
    ppermute x36, starting transfers between devices, swap_plane(): got.append(lax.ppermute(same[k], 'lvl', across(k, peer_count)))  37.4 us
    ppermute x24, starting transfers between devices, swap_plane(): got.append(lax.ppermute(prior[k], ('tile', 'lvl'), links))  31.3 us
    pallas_call x12, Pallas kernels, pick(): pl.pallas_call(body, in_specs=[pl.BlockSpec(memory_space=pltpu.SMEM)] + [...  23 us
    ppermute x18, starting transfers between devices, ring_z(): held.append(lax.ppermute(held[-1], 'lvl', links))  12.8 us
  transfers between devices with their start and end apart: 82, of which 40 were waited for; matrix products, arithmetic and copies ran while one was open for 2% of the time, Pallas kernels for 17%

profile of v3, /device:TPU:1, one launch (start us, length us, event | category | flops | bytes accessed | tf_op | source)
XLA Modules:
  0.0 329.2 jit_solution(3565876723342794957)
XLA Ops:
  3.9 3.7 %collective-permute-start.3 = (s32[2,3,32]{2,1,0:T(4,128)S(1)}, s32[2,3,32]{2,1,0:T(4,128)S(1)}, u32[]{:S(2)}, u32[]{:S(2)}) collective-permute-start(s32[2,3,32]{2,1,0:T(4,128)S(1)} %get-tuple-element.217), channel_id=1, source_target_pairs={{0,3},{1,2},{2,1},{3,0},{4,7},{5,6},{6,5},{7,4},{8,11},{9,10},{10,... | collective-permute-start | bytes 2312 | tf_op jit(solution)/shard_map/ppermute | solution.py:192
  7.9 4.9 %level_0_0.1 = (bf16[8,256,128]{2,1,0:T(8,128)(2,1)}, bf16[4,8,256,256]{3,2,1,0:T(8,128)(2,1)}) custom-call(s32[32]{0:T(128)} %get-tuple-element.225.refs_0_, bf16[4,8,256,256]{3,2,1,0:T(8,128)(2,1)} %refs_1_.15, bf16[4,8,256,256]{3,2,1,0:T(8,128)(2,1)} %refs_2_.15), custom_call_target="tpu_custom_call" | custom-call | flops 134217728 | bytes 8000000 | tf_op jit(solution)/shard_map/level_0_0/pallas_call | solution.py:98
  15.2 12.7 %collective-permute-done.4.refs_4_.refs_1_ = bf16[8,256,128]{2,1,0:T(8,128)(2,1)S(1)} collective-permute-done((bf16[8,256,128]{2,1,0:T(8,128)(2,1)}, bf16[8,256,128]{2,1,0:T(8,128)(2,1)S(1)}, u32[]{:S(2)}, u32[]{:S(2)}) %collective-permute-start.4) | collective-permute-done | bytes 524320 | tf_op jit(solution)/shard_map/ppermute | solution.py:240
  28.7 5.0 %level_0_1.1 = (bf16[8,256,128]{2,1,0:T(8,128)(2,1)}, bf16[4,8,256,256]{3,2,1,0:T(8,128)(2,1)}) custom-call(s32[32]{0:T(128)} %get-tuple-element.225.refs_0_, bf16[4,8,256,256]{3,2,1,0:T(8,128)(2,1)} %refs_1_.15, bf16[4,8,256,256]{3,2,1,0:T(8,128)(2,1)} %refs_2_.15, ...), custom_call_target="tpu_custom_call", output_to_operand_aliasing={{1}: (3, {})} | custom-call | flops 134217728 | bytes 8000000 | tf_op jit(solution)/shard_map/level_0_1/pallas_call | solution.py:98
  35.8 5.8 %collective-permute-done.9.refs_2_ = bf16[8,256,128]{2,1,0:T(8,128)(2,1)S(1)} collective-permute-done((bf16[8,256,128]{2,1,0:T(8,128)(2,1)S(1)}, bf16[8,256,128]{2,1,0:T(8,128)(2,1)S(1)}, u32[]{:S(2)}, u32[]{:S(2)}) %collective-permute-start.9) | collective-permute-done | bytes 524320 | tf_op jit(solution)/shard_map/ppermute | solution.py:240
  46.7 6.2 %collective-permute-done.5.refs_1_ = bf16[8,256,128]{2,1,0:T(8,128)(2,1)S(1)} collective-permute-done((bf16[8,256,128]{2,1,0:T(8,128)(2,1)}, bf16[8,256,128]{2,1,0:T(8,128)(2,1)S(1)}, u32[]{:S(2)}, u32[]{:S(2)}) %collective-permute-start.5) | collective-permute-done | bytes 524320 | tf_op jit(solution)/shard_map/ppermute | solution.py:240
  56.7 7.3 %collective-permute-done.10.refs_3_ = bf16[8,256,128]{2,1,0:T(8,128)(2,1)S(1)} collective-permute-done((bf16[8,256,128]{2,1,0:T(8,128)(2,1)S(1)}, bf16[8,256,128]{2,1,0:T(8,128)(2,1)S(1)}, u32[]{:S(2)}, u32[]{:S(2)}) %collective-permute-start.10) | collective-permute-done | bytes 524320 | tf_op jit(solution)/shard_map/ppermute | solution.py:240
  71.9 3.4 %collective-permute-done.18.refs_17_.refs_2_ = bf16[8,256,128]{2,1,0:T(8,128)(2,1)S(1)} collective-permute-done((bf16[8,256,128]{2,1,0:T(8,128)(2,1)S(1)}, bf16[8,256,128]{2,1,0:T(8,128)(2,1)S(1)}, u32[]{:S(2)}, u32[]{:S(2)}) %collective-permute-start.18) | collective-permute-done | bytes 524320 | tf_op jit(solution)/shard_map/ppermute | solution.py:240
  79.3 5.5 %collective-permute-done.15.refs_13_ = bf16[4,256,128]{2,1,0:T(8,128)(2,1)S(1)} collective-permute-done((bf16[4,256,128]{2,1,0:T(8,128)(2,1)S(1)}, bf16[4,256,128]{2,1,0:T(8,128)(2,1)S(1)}, u32[]{:S(2)}, u32[]{:S(2)}) %collective-permute-start.15) | collective-permute-done | bytes 262176 | tf_op jit(solution)/shard_map/ppermute | solution.py:254
  86.1 4.6 %collective-permute-done.17.refs_15_ = bf16[4,256,128]{2,1,0:T(8,128)(2,1)S(1)} collective-permute-done((bf16[4,256,128]{2,1,0:T(8,128)(2,1)S(1)}, bf16[4,256,128]{2,1,0:T(8,128)(2,1)S(1)}, u32[]{:S(2)}, u32[]{:S(2)}) %collective-permute-start.17) | collective-permute-done | bytes 262176 | tf_op jit(solution)/shard_map/ppermute | solution.py:254
  90.7 5.7 %level_1_0.1 = (bf16[8,256,128]{2,1,0:T(8,128)(2,1)S(1)}, bf16[4,8,256,256]{3,2,1,0:T(8,128)(2,1)}) custom-call(s32[32]{0:T(128)S(1)} %copy-done.8, bf16[4,8,256,256]{3,2,1,0:T(8,128)(2,1)} %refs_1_.15, bf16[4,8,256,256]{3,2,1,0:T(8,128)(2,1)} %refs_2_.15, bf16[3,8,4,256,256]{4,3,2,1,0:T(8,128)(2,1)} %refs_3_.11, ...), custom_call_target="tpu_custom_call", output_to_operand_aliasing={{1}: (16, {})} | custom-call | flops 134217728 | bytes 8000000 | tf_op jit(solution)/shard_map/level_1_0/pallas_call | solution.py:98
  103.8 2.6 collective-permute-done.19.refs_5_
  106.5 4.3 %collective-permute-done.30.refs_3_.refs_5_ = bf16[8,256,128]{2,1,0:T(8,128)(2,1)S(1)} collective-permute-done((bf16[8,256,128]{2,1,0:T(8,128)(2,1)S(1)}, bf16[8,256,128]{2,1,0:T(8,128)(2,1)S(1)}, u32[]{:S(2)}, u32[]{:S(2)}) %collective-permute-start.30) | collective-permute-done | bytes 524320 | tf_op jit(solution)/shard_map/ppermute | solution.py:240
  113.3 4.1 %collective-permute-done.23.refs_9_ = bf16[4,256,128]{2,1,0:T(8,128)(2,1)S(1)} collective-permute-done((bf16[4,256,128]{2,1,0:T(8,128)(2,1)S(1)}, bf16[4,256,128]{2,1,0:T(8,128)(2,1)S(1)}, u32[]{:S(2)}, u32[]{:S(2)}) %collective-permute-start.23) | collective-permute-done | bytes 262176 | tf_op jit(solution)/shard_map/ppermute | solution.py:247
  118.7 3.4 %collective-permute-done.24.refs_10_ = bf16[4,256,128]{2,1,0:T(8,128)(2,1)S(1)} collective-permute-done((bf16[4,256,128]{2,1,0:T(8,128)(2,1)S(1)}, bf16[4,256,128]{2,1,0:T(8,128)(2,1)S(1)}, u32[]{:S(2)}, u32[]{:S(2)}) %collective-permute-start.24) | collective-permute-done | bytes 262176 | tf_op jit(solution)/shard_map/ppermute | solution.py:247
  126.4 3.4 %collective-permute-done.28.refs_14_ = bf16[4,256,128]{2,1,0:T(8,128)(2,1)S(1)} collective-permute-done((bf16[4,256,128]{2,1,0:T(8,128)(2,1)S(1)}, bf16[4,256,128]{2,1,0:T(8,128)(2,1)S(1)}, u32[]{:S(2)}, u32[]{:S(2)}) %collective-permute-start.28) | collective-permute-done | bytes 262176 | tf_op jit(solution)/shard_map/ppermute | solution.py:254
  129.8 2.8 collective-permute-done.29.refs_15_
  132.6 5.7 %level_1_1.1 = (bf16[8,256,128]{2,1,0:T(8,128)(2,1)S(1)}, bf16[4,8,256,256]{3,2,1,0:T(8,128)(2,1)}) custom-call(s32[32]{0:T(128)S(1)} %copy-done.8, bf16[4,8,256,256]{3,2,1,0:T(8,128)(2,1)} %refs_1_.15, bf16[4,8,256,256]{3,2,1,0:T(8,128)(2,1)} %refs_2_.15, bf16[3,8,4,256,256]{4,3,2,1,0:T(8,128)(2,1)} %refs_3_.11, ...), custom_call_target="tpu_custom_call", output_to_operand_aliasing={{1}: (16, {})} | custom-call | flops 134217728 | bytes 8000000 | tf_op jit(solution)/shard_map/level_1_1/pallas_call | solution.py:98
  143.8 2.2 pick_1_0_1.1
  148.1 2.9 collective-permute-start.38
  151.0 2.0 collective-permute-done.32.refs_3_.refs_5_
  153.0 2.3 collective-permute-done.34.refs_6_
  160.7 6.0 %collective-permute-done.38.refs_10_ = bf16[4,256,128]{2,1,0:T(8,128)(2,1)S(1)} collective-permute-done((bf16[4,256,128]{2,1,0:T(8,128)(2,1)S(1)}, bf16[4,256,128]{2,1,0:T(8,128)(2,1)S(1)}, u32[]{:S(2)}, u32[]{:S(2)}) %collective-permute-start.38) | collective-permute-done | bytes 262176 | tf_op jit(solution)/shard_map/ppermute | solution.py:247
  169.4 8.1 %collective-permute-done.42.refs_14_ = bf16[4,256,128]{2,1,0:T(8,128)(2,1)S(1)} collective-permute-done((bf16[4,256,128]{2,1,0:T(8,128)(2,1)S(1)}, bf16[4,256,128]{2,1,0:T(8,128)(2,1)S(1)}, u32[]{:S(2)}, u32[]{:S(2)}) %collective-permute-start.42) | collective-permute-done | bytes 262176 | tf_op jit(solution)/shard_map/ppermute | solution.py:254
  177.5 5.7 %level_2_0.1 = (bf16[8,256,128]{2,1,0:T(8,128)(2,1)S(1)}, bf16[4,8,256,256]{3,2,1,0:T(8,128)(2,1)}) custom-call(s32[32]{0:T(128)S(1)} %get-tuple-element.224.refs_0_, bf16[4,8,256,256]{3,2,1,0:T(8,128)(2,1)} %refs_1_.15, bf16[4,8,256,256]{3,2,1,0:T(8,128)(2,1)} %refs_2_.15, bf16[3,8,4,256,256]{4,3,2,1,0:T(8,128)(2,1)} %refs_3_.11, ...), custom_call_target="tpu_custom_call", output_to_operand_aliasing={{1}: (16, {})} | custom-call | flops 134217728 | bytes 8000000 | tf_op jit(solution)/shard_map/level_2_0/pallas_call | solution.py:98
  187.8 2.2 pick_1_1_1.1
  192.7 2.2 collective-permute-start.50
  194.9 4.6 %collective-permute-done.46.refs_6_ = bf16[4,256,128]{2,1,0:T(8,128)(2,1)S(1)} collective-permute-done((bf16[4,256,128]{2,1,0:T(8,128)(2,1)S(1)}, bf16[4,256,128]{2,1,0:T(8,128)(2,1)S(1)}, u32[]{:S(2)}, u32[]{:S(2)}) %collective-permute-start.46) | collective-permute-done | bytes 262176 | tf_op jit(solution)/shard_map/ppermute | solution.py:247
  199.5 5.6 %collective-permute-start.57 = (bf16[8,256,128]{2,1,0:T(8,128)(2,1)S(1)}, bf16[8,256,128]{2,1,0:T(8,128)(2,1)S(1)}, u32[]{:S(2)}, u32[]{:S(2)}) collective-permute-start(bf16[8,256,128]{2,1,0:T(8,128)(2,1)S(1)} %collective-permute-done.56.refs_5_.refs_9_), channel_id=1, source_target_pairs={{0,4},{1,5},{2,6},{3,7},{4,8},{5,9},{6,10},{7,11},{8,12},{9,13},{1... | collective-permute-start | bytes 1572872 | tf_op jit(solution)/shard_map/ppermute | solution.py:240
  207.7 3.5 %collective-permute-done.50.refs_10_ = bf16[4,256,128]{2,1,0:T(8,128)(2,1)S(1)} collective-permute-done((bf16[4,256,128]{2,1,0:T(8,128)(2,1)S(1)}, bf16[4,256,128]{2,1,0:T(8,128)(2,1)S(1)}, u32[]{:S(2)}, u32[]{:S(2)}) %collective-permute-start.50) | collective-permute-done | bytes 262176 | tf_op jit(solution)/shard_map/ppermute | solution.py:247
  214.4 7.3 %collective-permute-done.54.refs_14_ = bf16[4,256,128]{2,1,0:T(8,128)(2,1)S(1)} collective-permute-done((bf16[4,256,128]{2,1,0:T(8,128)(2,1)S(1)}, bf16[4,256,128]{2,1,0:T(8,128)(2,1)S(1)}, u32[]{:S(2)}, u32[]{:S(2)}) %collective-permute-start.54) | collective-permute-done | bytes 262176 | tf_op jit(solution)/shard_map/ppermute | solution.py:254
  221.6 5.7 %level_2_1.1 = (bf16[8,256,128]{2,1,0:T(8,128)(2,1)S(1)}, bf16[4,8,256,256]{3,2,1,0:T(8,128)(2,1)}) custom-call(s32[32]{0:T(128)S(1)} %get-tuple-element.224.refs_0_, bf16[4,8,256,256]{3,2,1,0:T(8,128)(2,1)} %refs_1_.15, bf16[4,8,256,256]{3,2,1,0:T(8,128)(2,1)} %refs_2_.15, bf16[3,8,4,256,256]{4,3,2,1,0:T(8,128)(2,1)} %refs_3_.11, ...), custom_call_target="tpu_custom_call", output_to_operand_aliasing={{1}: (16, {})} | custom-call | flops 134217728 | bytes 8000000 | tf_op jit(solution)/shard_map/level_2_1/pallas_call | solution.py:98
  227.4 2.5 collective-permute-start.58
  230.8 12.1 %collective-permute-done.58.refs_5_.refs_9_ = bf16[8,256,128]{2,1,0:T(8,128)(2,1)S(1)} collective-permute-done((bf16[8,256,128]{2,1,0:T(8,128)(2,1)S(1)}, bf16[8,256,128]{2,1,0:T(8,128)(2,1)S(1)}, u32[]{:S(2)}, u32[]{:S(2)}) %collective-permute-start.58) | collective-permute-done | bytes 524320 | tf_op jit(solution)/shard_map/ppermute | solution.py:240
  248.7 5.4 %collective-permute-done.62.refs_11_ = bf16[8,256,128]{2,1,0:T(8,128)(2,1)S(1)} collective-permute-done((bf16[8,256,128]{2,1,0:T(8,128)(2,1)S(1)}, bf16[8,256,128]{2,1,0:T(8,128)(2,1)S(1)}, u32[]{:S(2)}, u32[]{:S(2)}) %collective-permute-start.62) | collective-permute-done | bytes 524320 | tf_op jit(solution)/shard_map/ppermute | solution.py:240
  254.1 2.5 pick_2_0_1.1
  259.5 5.8 %collective-permute-done.70.refs_17_.refs_10_ = bf16[8,256,128]{2,1,0:T(8,128)(2,1)S(1)} collective-permute-done((bf16[8,256,128]{2,1,0:T(8,128)(2,1)S(1)}, bf16[8,256,128]{2,1,0:T(8,128)(2,1)S(1)}, u32[]{:S(2)}, u32[]{:S(2)}) %collective-permute-start.70) | collective-permute-done | bytes 524320 | tf_op jit(solution)/shard_map/ppermute | solution.py:240
  268.9 3.0 collective-permute-done.64.refs_10_
  276.0 6.3 %collective-permute-done.68.refs_14_ = bf16[4,256,128]{2,1,0:T(8,128)(2,1)S(1)} collective-permute-done((bf16[4,256,128]{2,1,0:T(8,128)(2,1)S(1)}, bf16[4,256,128]{2,1,0:T(8,128)(2,1)S(1)}, u32[]{:S(2)}, u32[]{:S(2)}) %collective-permute-start.68) | collective-permute-done | bytes 262176 | tf_op jit(solution)/shard_map/ppermute | solution.py:254
  282.4 5.7 %level_3_0.1 = (bf16[8,256,128]{2,1,0:T(8,128)(2,1)S(1)}, bf16[4,8,256,256]{3,2,1,0:T(8,128)(2,1)}) custom-call(s32[32]{0:T(128)S(1)} %get-tuple-element.226.refs_0_, bf16[4,8,256,256]{3,2,1,0:T(8,128)(2,1)} %refs_1_.15, bf16[4,8,256,256]{3,2,1,0:T(8,128)(2,1)} %refs_2_.15, bf16[3,8,4,256,256]{4,3,2,1,0:T(8,128)(2,1)} %refs_3_.11, ...), custom_call_target="tpu_custom_call", output_to_operand_aliasing={{1}: (16, {})} | custom-call | flops 134217728 | bytes 8000000 | tf_op jit(solution)/shard_map/level_3_0/pallas_call | solution.py:98
  290.0 2.1 collective-permute-start.72
  292.6 2.5 pick_2_1_1.1
  298.0 2.2 collective-permute-start.77
  301.5 3.0 collective-permute-done.73.refs_7_
  305.8 3.5 %collective-permute-done.75.refs_9_ = bf16[4,256,128]{2,1,0:T(8,128)(2,1)S(1)} collective-permute-done((bf16[4,256,128]{2,1,0:T(8,128)(2,1)S(1)}, bf16[4,256,128]{2,1,0:T(8,128)(2,1)S(1)}, u32[]{:S(2)}, u32[]{:S(2)}) %collective-permute-start.75) | collective-permute-done | bytes 262176 | tf_op jit(solution)/shard_map/ppermute | solution.py:247
  312.2 3.6 %collective-permute-done.77.refs_11_ = bf16[4,256,128]{2,1,0:T(8,128)(2,1)S(1)} collective-permute-done((bf16[4,256,128]{2,1,0:T(8,128)(2,1)S(1)}, bf16[4,256,128]{2,1,0:T(8,128)(2,1)S(1)}, u32[]{:S(2)}, u32[]{:S(2)}) %collective-permute-start.77) | collective-permute-done | bytes 262176 | tf_op jit(solution)/shard_map/ppermute | solution.py:247
  318.4 4.1 %collective-permute-done.81.refs_15_ = bf16[4,256,128]{2,1,0:T(8,128)(2,1)S(1)} collective-permute-done((bf16[4,256,128]{2,1,0:T(8,128)(2,1)S(1)}, bf16[4,256,128]{2,1,0:T(8,128)(2,1)S(1)}, u32[]{:S(2)}, u32[]{:S(2)}) %collective-permute-start.81) | collective-permute-done | bytes 262176 | tf_op jit(solution)/shard_map/ppermute | solution.py:254
  322.4 6.6 %level_3_1.1 = (bf16[8,256,128]{2,1,0:T(8,128)(2,1)}, bf16[4,8,256,256]{3,2,1,0:T(8,128)(2,1)}) custom-call(s32[32]{0:T(128)S(1)} %get-tuple-element.226.refs_0_, bf16[4,8,256,256]{3,2,1,0:T(8,128)(2,1)} %refs_1_.15, bf16[4,8,256,256]{3,2,1,0:T(8,128)(2,1)} %refs_2_.15, bf16[3,8,4,256,256]{4,3,2,1,0:T(8,128)(2,1)} %refs_3_.11, ...), custom_call_target="tpu_custom_call", output_to_operand_aliasing={{1}: (16, {})} | custom-call | flops 134217728 | bytes 8000000 | tf_op jit(solution)/shard_map/level_3_1/pallas_call | solution.py:98
  (228 shorter events, 105.7 us)
Async XLA Ops:
  12.8 15.1 %collective-permute-start.4 = (bf16[8,256,128]{2,1,0:T(8,128)(2,1)}, bf16[8,256,128]{2,1,0:T(8,128)(2,1)S(1)}, u32[]{:S(2)}, u32[]{:S(2)}) collective-permute-start(bf16[8,256,128]{2,1,0:T(8,128)(2,1)} %get-tuple-element.93.refs_0_), channel_id=1, source_target_pairs={{0,4},{1,5},{2,6},{3,7},{4,8},{5,9},{6,10},{7,11},{8,12},{9,13},{1... | collective-permute-start | bytes 1572872 | tf_op jit(solution)/shard_map/ppermute | solution.py:240
  27.9 13.7 %collective-permute-start.9 = (bf16[8,256,128]{2,1,0:T(8,128)(2,1)S(1)}, bf16[8,256,128]{2,1,0:T(8,128)(2,1)S(1)}, u32[]{:S(2)}, u32[]{:S(2)}) collective-permute-start(bf16[8,256,128]{2,1,0:T(8,128)(2,1)S(1)} %collective-permute-done.4.refs_4_.refs_1_), channel_id=1, source_target_pairs={{0,4},{1,5},{2,6},{3,7},{4,8},{5,9},{6,10},{7,11},{8,12},{9,13},{1... | collective-permute-start | bytes 1572872 | tf_op jit(solution)/shard_map/ppermute | solution.py:240
  33.8 19.1 %collective-permute-start.5 = (bf16[8,256,128]{2,1,0:T(8,128)(2,1)}, bf16[8,256,128]{2,1,0:T(8,128)(2,1)S(1)}, u32[]{:S(2)}, u32[]{:S(2)}) collective-permute-start(bf16[8,256,128]{2,1,0:T(8,128)(2,1)} %get-tuple-element.94.refs_2_.refs_4_.refs_0_), channel_id=1, source_target_pairs={{0,4},{1,5},{2,6},{3,7},{4,8},{5,9},{6,10},{7,11},{8,12},{9,13},{1... | collective-permute-start | bytes 1572872 | tf_op jit(solution)/shard_map/ppermute | solution.py:240
  41.6 22.5 %collective-permute-start.10 = (bf16[8,256,128]{2,1,0:T(8,128)(2,1)S(1)}, bf16[8,256,128]{2,1,0:T(8,128)(2,1)S(1)}, u32[]{:S(2)}, u32[]{:S(2)}) collective-permute-start(bf16[8,256,128]{2,1,0:T(8,128)(2,1)S(1)} %collective-permute-done.9.refs_2_), channel_id=1, source_target_pairs={{0,4},{1,5},{2,6},{3,7},{4,8},{5,9},{6,10},{7,11},{8,12},{9,13},{1... | collective-permute-start | bytes 1572872 | tf_op jit(solution)/shard_map/ppermute | solution.py:240
  46.0 22.8 %collective-permute-start.6 = (bf16[4,256,128]{2,1,0:T(8,128)(2,1)}, bf16[4,256,128]{2,1,0:T(8,128)(2,1)S(1)}, u32[]{:S(2)}, u32[]{:S(2)}) collective-permute-start(bf16[4,256,128]{2,1,0:T(8,128)(2,1)} %get-tuple-element.96), channel_id=1, source_target_pairs={{0,1},{1,0},{2,3},{3,2},{4,5},{5,4},{6,7},{7,6},{8,9},{9,8},{10,11... | collective-permute-start | bytes 786440 | tf_op jit(solution)/shard_map/ppermute | solution.py:247
  52.9 22.5 %collective-permute-start.18 = (bf16[8,256,128]{2,1,0:T(8,128)(2,1)S(1)}, bf16[8,256,128]{2,1,0:T(8,128)(2,1)S(1)}, u32[]{:S(2)}, u32[]{:S(2)}) collective-permute-start(bf16[8,256,128]{2,1,0:T(8,128)(2,1)S(1)} %collective-permute-done.5.refs_1_), channel_id=1, source_target_pairs={{0,4},{1,5},{2,6},{3,7},{4,8},{5,9},{6,10},{7,11},{8,12},{9,13},{1... | collective-permute-start | bytes 1572872 | tf_op jit(solution)/shard_map/ppermute | solution.py:240
  54.8 15.3 %collective-permute-start.7 = (bf16[4,256,128]{2,1,0:T(8,128)(2,1)}, bf16[4,256,128]{2,1,0:T(8,128)(2,1)S(1)}, u32[]{:S(2)}, u32[]{:S(2)}) collective-permute-start(bf16[4,256,128]{2,1,0:T(8,128)(2,1)} %copy-done.9), channel_id=1, source_target_pairs={{0,2},{1,3},{2,0},{3,1},{4,6},{5,7},{6,4},{7,5},{8,10},{9,11},{10,... | collective-permute-start | bytes 786440 | tf_op jit(solution)/shard_map/ppermute | solution.py:247
  55.6 15.1 %collective-permute-start.8 = (bf16[4,256,128]{2,1,0:T(8,128)(2,1)S(1)}, bf16[4,256,128]{2,1,0:T(8,128)(2,1)S(1)}, u32[]{:S(2)}, u32[]{:S(2)}) collective-permute-start(bf16[4,256,128]{2,1,0:T(8,128)(2,1)S(1)} %get-tuple-element.98), channel_id=1, source_target_pairs={{0,3},{1,2},{2,1},{3,0},{4,7},{5,6},{6,5},{7,4},{8,11},{9,10},{10,... | collective-permute-start | bytes 786440 | tf_op jit(solution)/shard_map/ppermute | solution.py:247
  77.9 12.7 %collective-permute-start.17 = (bf16[4,256,128]{2,1,0:T(8,128)(2,1)S(1)}, bf16[4,256,128]{2,1,0:T(8,128)(2,1)S(1)}, u32[]{:S(2)}, u32[]{:S(2)}) collective-permute-start(bf16[4,256,128]{2,1,0:T(8,128)(2,1)S(1)} %get-tuple-element.106), channel_id=1, source_target_pairs={{0,19},{1,18},{2,17},{3,16},{4,23},{5,22},{6,21},{7,20},{8,27},{9,... | collective-permute-start | bytes 786440 | tf_op jit(solution)/shard_map/ppermute | solution.py:254
  79.3 21.5 %collective-permute-start.22 = (bf16[8,256,128]{2,1,0:T(8,128)(2,1)S(1)}, bf16[8,256,128]{2,1,0:T(8,128)(2,1)S(1)}, u32[]{:S(2)}, u32[]{:S(2)}) collective-permute-start(bf16[8,256,128]{2,1,0:T(8,128)(2,1)S(1)} %collective-permute-done.18.refs_17_.refs_2_), channel_id=1, source_target_pairs={{0,4},{1,5},{2,6},{3,7},{4,8},{5,9},{6,10},{7,11},{8,12},{9,13},{1... | collective-permute-start | bytes 1572872 | tf_op jit(solution)/shard_map/ppermute | solution.py:240
  96.4 14.3 %collective-permute-start.30 = (bf16[8,256,128]{2,1,0:T(8,128)(2,1)S(1)}, bf16[8,256,128]{2,1,0:T(8,128)(2,1)S(1)}, u32[]{:S(2)}, u32[]{:S(2)}) collective-permute-start(bf16[8,256,128]{2,1,0:T(8,128)(2,1)S(1)} %get-tuple-element.108.refs_2_.refs_4_), channel_id=1, source_target_pairs={{0,4},{1,5},{2,6},{3,7},{4,8},{5,9},{6,10},{7,11},{8,12},{9,13},{1... | collective-permute-start | bytes 1572872 | tf_op jit(solution)/shard_map/ppermute | solution.py:240
  99.3 12.7 %collective-permute-start.21 = (bf16[4,256,128]{2,1,0:T(8,128)(2,1)S(1)}, bf16[4,256,128]{2,1,0:T(8,128)(2,1)S(1)}, u32[]{:S(2)}, u32[]{:S(2)}) collective-permute-start(bf16[4,256,128]{2,1,0:T(8,128)(2,1)S(1)} %get-tuple-element.112), channel_id=1, source_target_pairs={{0,3},{1,2},{2,1},{3,0},{4,7},{5,6},{6,5},{7,4},{8,11},{9,10},{10,... | collective-permute-start | bytes 786440 | tf_op jit(solution)/shard_map/ppermute | solution.py:247
  102.5 14.9 %collective-permute-start.23 = (bf16[4,256,128]{2,1,0:T(8,128)(2,1)S(1)}, bf16[4,256,128]{2,1,0:T(8,128)(2,1)S(1)}, u32[]{:S(2)}, u32[]{:S(2)}) collective-permute-start(bf16[4,256,128]{2,1,0:T(8,128)(2,1)S(1)} %get-tuple-element.114), channel_id=1, source_target_pairs={{0,1},{1,0},{2,3},{3,2},{4,5},{5,4},{6,7},{7,6},{8,9},{9,8},{10,11... | collective-permute-start | bytes 786440 | tf_op jit(solution)/shard_map/ppermute | solution.py:247
  106.4 15.7 %collective-permute-start.24 = (bf16[4,256,128]{2,1,0:T(8,128)(2,1)S(1)}, bf16[4,256,128]{2,1,0:T(8,128)(2,1)S(1)}, u32[]{:S(2)}, u32[]{:S(2)}) collective-permute-start(bf16[4,256,128]{2,1,0:T(8,128)(2,1)S(1)} %get-tuple-element.115), channel_id=1, source_target_pairs={{0,2},{1,3},{2,0},{3,1},{4,6},{5,7},{6,4},{7,5},{8,10},{9,11},{10,... | collective-permute-start | bytes 786440 | tf_op jit(solution)/shard_map/ppermute | solution.py:247
  110.7 15.6 %collective-permute-start.31 = (bf16[8,256,128]{2,1,0:T(8,128)(2,1)S(1)}, bf16[8,256,128]{2,1,0:T(8,128)(2,1)S(1)}, u32[]{:S(2)}, u32[]{:S(2)}) collective-permute-start(bf16[8,256,128]{2,1,0:T(8,128)(2,1)S(1)} %collective-permute-done.30.refs_3_.refs_5_), channel_id=1, source_target_pairs={{0,4},{1,5},{2,6},{3,7},{4,8},{5,9},{6,10},{7,11},{8,12},{9,13},{1... | collective-permute-start | bytes 1572872 | tf_op jit(solution)/shard_map/ppermute | solution.py:240
  110.7 12.7 %collective-permute-start.25 = (bf16[4,256,128]{2,1,0:T(8,128)(2,1)S(1)}, bf16[4,256,128]{2,1,0:T(8,128)(2,1)S(1)}, u32[]{:S(2)}, u32[]{:S(2)}) collective-permute-start(bf16[4,256,128]{2,1,0:T(8,128)(2,1)S(1)} %get-tuple-element.116), channel_id=1, source_target_pairs={{0,3},{1,2},{2,1},{3,0},{4,7},{5,6},{6,5},{7,4},{8,11},{9,10},{10,... | collective-permute-start | bytes 786440 | tf_op jit(solution)/shard_map/ppermute | solution.py:247
  112.0 14.3 %collective-permute-start.26 = (bf16[4,256,128]{2,1,0:T(8,128)(2,1)S(1)}, bf16[4,256,128]{2,1,0:T(8,128)(2,1)S(1)}, u32[]{:S(2)}, u32[]{:S(2)}) collective-permute-start(bf16[4,256,128]{2,1,0:T(8,128)(2,1)S(1)} %get-tuple-element.117), channel_id=1, source_target_pairs={{0,16},{1,17},{2,18},{3,19},{4,20},{5,21},{6,22},{7,23},{8,24},{9,... | collective-permute-start | bytes 786440 | tf_op jit(solution)/shard_map/ppermute | solution.py:254
  126.4 17.4 %collective-permute-start.36 = (bf16[8,256,128]{2,1,0:T(8,128)(2,1)S(1)}, bf16[8,256,128]{2,1,0:T(8,128)(2,1)S(1)}, u32[]{:S(2)}, u32[]{:S(2)}) collective-permute-start(bf16[8,256,128]{2,1,0:T(8,128)(2,1)S(1)} %collective-permute-done.31.refs_17_.refs_6_), channel_id=1, source_target_pairs={{0,4},{1,5},{2,6},{3,7},{4,8},{5,9},{6,10},{7,11},{8,12},{9,13},{1... | collective-permute-start | bytes 1572872 | tf_op jit(solution)/shard_map/ppermute | solution.py:240
  138.4 14.6 %collective-permute-start.32 = (bf16[8,256,128]{2,1,0:T(8,128)(2,1)S(1)}, bf16[8,256,128]{2,1,0:T(8,128)(2,1)S(1)}, u32[]{:S(2)}, u32[]{:S(2)}) collective-permute-start(bf16[8,256,128]{2,1,0:T(8,128)(2,1)S(1)} %get-tuple-element.122.refs_4_.refs_8_.refs_2_), channel_id=1, source_target_pairs={{0,4},{1,5},{2,6},{3,7},{4,8},{5,9},{6,10},{7,11},{8,12},{9,13},{1... | collective-permute-start | bytes 1572872 | tf_op jit(solution)/shard_map/ppermute | solution.py:240
  142.0 13.3 %collective-permute-start.34 = (bf16[4,256,128]{2,1,0:T(8,128)(2,1)S(1)}, bf16[4,256,128]{2,1,0:T(8,128)(2,1)S(1)}, u32[]{:S(2)}, u32[]{:S(2)}) collective-permute-start(bf16[4,256,128]{2,1,0:T(8,128)(2,1)S(1)} %get-tuple-element.125), channel_id=1, source_target_pairs={{0,2},{1,3},{2,0},{3,1},{4,6},{5,7},{6,4},{7,5},{8,10},{9,11},{10,... | collective-permute-start | bytes 786440 | tf_op jit(solution)/shard_map/ppermute | solution.py:247
  142.7 14.2 %collective-permute-start.35 = (bf16[4,256,128]{2,1,0:T(8,128)(2,1)S(1)}, bf16[4,256,128]{2,1,0:T(8,128)(2,1)S(1)}, u32[]{:S(2)}, u32[]{:S(2)}) collective-permute-start(bf16[4,256,128]{2,1,0:T(8,128)(2,1)S(1)} %get-tuple-element.126), channel_id=1, source_target_pairs={{0,3},{1,2},{2,1},{3,0},{4,7},{5,6},{6,5},{7,4},{8,11},{9,10},{10,... | collective-permute-start | bytes 786440 | tf_op jit(solution)/shard_map/ppermute | solution.py:247
  146.0 13.4 %collective-permute-start.37 = (bf16[4,256,128]{2,1,0:T(8,128)(2,1)S(1)}, bf16[4,256,128]{2,1,0:T(8,128)(2,1)S(1)}, u32[]{:S(2)}, u32[]{:S(2)}) collective-permute-start(bf16[4,256,128]{2,1,0:T(8,128)(2,1)S(1)} %get-tuple-element.128), channel_id=1, source_target_pairs={{0,1},{1,0},{2,3},{3,2},{4,5},{5,4},{6,7},{7,6},{8,9},{9,8},{10,11... | collective-permute-start | bytes 786440 | tf_op jit(solution)/shard_map/ppermute | solution.py:247
  148.1 18.6 %collective-permute-start.38 = (bf16[4,256,128]{2,1,0:T(8,128)(2,1)S(1)}, bf16[4,256,128]{2,1,0:T(8,128)(2,1)S(1)}, u32[]{:S(2)}, u32[]{:S(2)}) collective-permute-start(bf16[4,256,128]{2,1,0:T(8,128)(2,1)S(1)} %get-tuple-element.129), channel_id=1, source_target_pairs={{0,2},{1,3},{2,0},{3,1},{4,6},{5,7},{6,4},{7,5},{8,10},{9,11},{10,... | collective-permute-start | bytes 786440 | tf_op jit(solution)/shard_map/ppermute | solution.py:247
  153.0 16.3 %collective-permute-start.44 = (bf16[8,256,128]{2,1,0:T(8,128)(2,1)S(1)}, bf16[8,256,128]{2,1,0:T(8,128)(2,1)S(1)}, u32[]{:S(2)}, u32[]{:S(2)}) collective-permute-start(bf16[8,256,128]{2,1,0:T(8,128)(2,1)S(1)} %collective-permute-done.32.refs_3_.refs_5_), channel_id=1, source_target_pairs={{0,4},{1,5},{2,6},{3,7},{4,8},{5,9},{6,10},{7,11},{8,12},{9,13},{1... | collective-permute-start | bytes 1572872 | tf_op jit(solution)/shard_map/ppermute | solution.py:240
  155.3 12.6 %collective-permute-start.39 = (bf16[4,256,128]{2,1,0:T(8,128)(2,1)S(1)}, bf16[4,256,128]{2,1,0:T(8,128)(2,1)S(1)}, u32[]{:S(2)}, u32[]{:S(2)}) collective-permute-start(bf16[4,256,128]{2,1,0:T(8,128)(2,1)S(1)} %get-tuple-element.130), channel_id=1, source_target_pairs={{0,3},{1,2},{2,1},{3,0},{4,7},{5,6},{6,5},{7,4},{8,11},{9,10},{10,... | collective-permute-start | bytes 786440 | tf_op jit(solution)/shard_map/ppermute | solution.py:247
  156.9 12.4 %collective-permute-start.40 = (bf16[4,256,128]{2,1,0:T(8,128)(2,1)S(1)}, bf16[4,256,128]{2,1,0:T(8,128)(2,1)S(1)}, u32[]{:S(2)}, u32[]{:S(2)}) collective-permute-start(bf16[4,256,128]{2,1,0:T(8,128)(2,1)S(1)} %get-tuple-element.131), channel_id=1, source_target_pairs={{0,16},{1,17},{2,18},{3,19},{4,20},{5,21},{6,22},{7,23},{8,24},{9,... | collective-permute-start | bytes 786440 | tf_op jit(solution)/shard_map/ppermute | solution.py:254
  169.3 18.5 %collective-permute-start.48 = (bf16[8,256,128]{2,1,0:T(8,128)(2,1)S(1)}, bf16[8,256,128]{2,1,0:T(8,128)(2,1)S(1)}, u32[]{:S(2)}, u32[]{:S(2)}) collective-permute-start(bf16[8,256,128]{2,1,0:T(8,128)(2,1)S(1)} %collective-permute-done.44.refs_17_.refs_6_), channel_id=1, source_target_pairs={{0,4},{1,5},{2,6},{3,7},{4,8},{5,9},{6,10},{7,11},{8,12},{9,13},{1... | collective-permute-start | bytes 1572872 | tf_op jit(solution)/shard_map/ppermute | solution.py:240
  183.2 16.3 %collective-permute-start.56 = (bf16[8,256,128]{2,1,0:T(8,128)(2,1)S(1)}, bf16[8,256,128]{2,1,0:T(8,128)(2,1)S(1)}, u32[]{:S(2)}, u32[]{:S(2)}) collective-permute-start(bf16[8,256,128]{2,1,0:T(8,128)(2,1)S(1)} %get-tuple-element.136.refs_4_.refs_8_), channel_id=1, source_target_pairs={{0,4},{1,5},{2,6},{3,7},{4,8},{5,9},{6,10},{7,11},{8,12},{9,13},{1... | collective-permute-start | bytes 1572872 | tf_op jit(solution)/shard_map/ppermute | solution.py:240
  186.4 13.1 %collective-permute-start.46 = (bf16[4,256,128]{2,1,0:T(8,128)(2,1)S(1)}, bf16[4,256,128]{2,1,0:T(8,128)(2,1)S(1)}, u32[]{:S(2)}, u32[]{:S(2)}) collective-permute-start(bf16[4,256,128]{2,1,0:T(8,128)(2,1)S(1)} %get-tuple-element.139), channel_id=1, source_target_pairs={{0,2},{1,3},{2,0},{3,1},{4,6},{5,7},{6,4},{7,5},{8,10},{9,11},{10,... | collective-permute-start | bytes 786440 | tf_op jit(solution)/shard_map/ppermute | solution.py:247
  187.8 17.3 %collective-permute-start.47 = (bf16[4,256,128]{2,1,0:T(8,128)(2,1)S(1)}, bf16[4,256,128]{2,1,0:T(8,128)(2,1)S(1)}, u32[]{:S(2)}, u32[]{:S(2)}) collective-permute-start(bf16[4,256,128]{2,1,0:T(8,128)(2,1)S(1)} %get-tuple-element.140), channel_id=1, source_target_pairs={{0,3},{1,2},{2,1},{3,0},{4,7},{5,6},{6,5},{7,4},{8,11},{9,10},{10,... | collective-permute-start | bytes 786440 | tf_op jit(solution)/shard_map/ppermute | solution.py:247
  190.0 16.4 %collective-permute-start.49 = (bf16[4,256,128]{2,1,0:T(8,128)(2,1)S(1)}, bf16[4,256,128]{2,1,0:T(8,128)(2,1)S(1)}, u32[]{:S(2)}, u32[]{:S(2)}) collective-permute-start(bf16[4,256,128]{2,1,0:T(8,128)(2,1)S(1)} %get-tuple-element.142), channel_id=1, source_target_pairs={{0,1},{1,0},{2,3},{3,2},{4,5},{5,4},{6,7},{7,6},{8,9},{9,8},{10,11... | collective-permute-start | bytes 786440 | tf_op jit(solution)/shard_map/ppermute | solution.py:247
  192.7 18.4 %collective-permute-start.50 = (bf16[4,256,128]{2,1,0:T(8,128)(2,1)S(1)}, bf16[4,256,128]{2,1,0:T(8,128)(2,1)S(1)}, u32[]{:S(2)}, u32[]{:S(2)}) collective-permute-start(bf16[4,256,128]{2,1,0:T(8,128)(2,1)S(1)} %get-tuple-element.143), channel_id=1, source_target_pairs={{0,2},{1,3},{2,0},{3,1},{4,6},{5,7},{6,4},{7,5},{8,10},{9,11},{10,... | collective-permute-start | bytes 786440 | tf_op jit(solution)/shard_map/ppermute | solution.py:247
  199.5 12.9 %collective-permute-start.51 = (bf16[4,256,128]{2,1,0:T(8,128)(2,1)S(1)}, bf16[4,256,128]{2,1,0:T(8,128)(2,1)S(1)}, u32[]{:S(2)}, u32[]{:S(2)}) collective-permute-start(bf16[4,256,128]{2,1,0:T(8,128)(2,1)S(1)} %get-tuple-element.144), channel_id=1, source_target_pairs={{0,3},{1,2},{2,1},{3,0},{4,7},{5,6},{6,5},{7,4},{8,11},{9,10},{10,... | collective-permute-start | bytes 786440 | tf_op jit(solution)/shard_map/ppermute | solution.py:247
  199.5 22.1 %collective-permute-start.57 = (bf16[8,256,128]{2,1,0:T(8,128)(2,1)S(1)}, bf16[8,256,128]{2,1,0:T(8,128)(2,1)S(1)}, u32[]{:S(2)}, u32[]{:S(2)}) collective-permute-start(bf16[8,256,128]{2,1,0:T(8,128)(2,1)S(1)} %collective-permute-done.56.refs_5_.refs_9_), channel_id=1, source_target_pairs={{0,4},{1,5},{2,6},{3,7},{4,8},{5,9},{6,10},{7,11},{8,12},{9,13},{1... | collective-permute-start | bytes 1572872 | tf_op jit(solution)/shard_map/ppermute | solution.py:240
  227.4 15.5 %collective-permute-start.58 = (bf16[8,256,128]{2,1,0:T(8,128)(2,1)S(1)}, bf16[8,256,128]{2,1,0:T(8,128)(2,1)S(1)}, u32[]{:S(2)}, u32[]{:S(2)}) collective-permute-start(bf16[8,256,128]{2,1,0:T(8,128)(2,1)S(1)} %get-tuple-element.150.refs_6_.refs_12_.refs_4_.refs_8_), channel_id=1, source_target_pairs={{0,4},{1,5},{2,6},{3,7},{4,8},{5,9},{6,10},{7,11},{8,12},{9,13},{1... | collective-permute-start | bytes 1572872 | tf_op jit(solution)/shard_map/ppermute | solution.py:240
  229.9 24.2 %collective-permute-start.62 = (bf16[8,256,128]{2,1,0:T(8,128)(2,1)S(1)}, bf16[8,256,128]{2,1,0:T(8,128)(2,1)S(1)}, u32[]{:S(2)}, u32[]{:S(2)}) collective-permute-start(bf16[8,256,128]{2,1,0:T(8,128)(2,1)S(1)} %collective-permute-done.57.refs_17_.refs_10_), channel_id=1, source_target_pairs={{0,4},{1,5},{2,6},{3,7},{4,8},{5,9},{6,10},{7,11},{8,12},{9,13},{1... | collective-permute-start | bytes 1572872 | tf_op jit(solution)/shard_map/ppermute | solution.py:240
  242.9 22.5 %collective-permute-start.70 = (bf16[8,256,128]{2,1,0:T(8,128)(2,1)S(1)}, bf16[8,256,128]{2,1,0:T(8,128)(2,1)S(1)}, u32[]{:S(2)}, u32[]{:S(2)}) collective-permute-start(bf16[8,256,128]{2,1,0:T(8,128)(2,1)S(1)} %collective-permute-done.58.refs_5_.refs_9_), channel_id=1, source_target_pairs={{0,4},{1,5},{2,6},{3,7},{4,8},{5,9},{6,10},{7,11},{8,12},{9,13},{1... | collective-permute-start | bytes 1572872 | tf_op jit(solution)/shard_map/ppermute | solution.py:240
  247.4 11.9 %collective-permute-start.60 = (bf16[4,256,128]{2,1,0:T(8,128)(2,1)S(1)}, bf16[4,256,128]{2,1,0:T(8,128)(2,1)S(1)}, u32[]{:S(2)}, u32[]{:S(2)}) collective-permute-start(bf16[4,256,128]{2,1,0:T(8,128)(2,1)S(1)} %get-tuple-element.153), channel_id=1, source_target_pairs={{0,2},{1,3},{2,0},{3,1},{4,6},{5,7},{6,4},{7,5},{8,10},{9,11},{10,... | collective-permute-start | bytes 786440 | tf_op jit(solution)/shard_map/ppermute | solution.py:247
  248.3 18.0 %collective-permute-start.61 = (bf16[4,256,128]{2,1,0:T(8,128)(2,1)S(1)}, bf16[4,256,128]{2,1,0:T(8,128)(2,1)S(1)}, u32[]{:S(2)}, u32[]{:S(2)}) collective-permute-start(bf16[4,256,128]{2,1,0:T(8,128)(2,1)S(1)} %get-tuple-element.154), channel_id=1, source_target_pairs={{0,3},{1,2},{2,1},{3,0},{4,7},{5,6},{6,5},{7,4},{8,11},{9,10},{10,... | collective-permute-start | bytes 786440 | tf_op jit(solution)/shard_map/ppermute | solution.py:247
  257.1 14.8 %collective-permute-start.64 = (bf16[4,256,128]{2,1,0:T(8,128)(2,1)S(1)}, bf16[4,256,128]{2,1,0:T(8,128)(2,1)S(1)}, u32[]{:S(2)}, u32[]{:S(2)}) collective-permute-start(bf16[4,256,128]{2,1,0:T(8,128)(2,1)S(1)} %get-tuple-element.157), channel_id=1, source_target_pairs={{0,2},{1,3},{2,0},{3,1},{4,6},{5,7},{6,4},{7,5},{8,10},{9,11},{10,... | collective-permute-start | bytes 786440 | tf_op jit(solution)/shard_map/ppermute | solution.py:247
  259.3 13.9 %collective-permute-start.65 = (bf16[4,256,128]{2,1,0:T(8,128)(2,1)S(1)}, bf16[4,256,128]{2,1,0:T(8,128)(2,1)S(1)}, u32[]{:S(2)}, u32[]{:S(2)}) collective-permute-start(bf16[4,256,128]{2,1,0:T(8,128)(2,1)S(1)} %get-tuple-element.158), channel_id=1, source_target_pairs={{0,3},{1,2},{2,1},{3,0},{4,7},{5,6},{6,5},{7,4},{8,11},{9,10},{10,... | collective-permute-start | bytes 786440 | tf_op jit(solution)/shard_map/ppermute | solution.py:247
  265.4 27.3 %collective-permute-start.74 = (bf16[8,256,128]{2,1,0:T(8,128)(2,1)S(1)}, bf16[8,256,128]{2,1,0:T(8,128)(2,1)S(1)}, u32[]{:S(2)}, u32[]{:S(2)}) collective-permute-start(bf16[8,256,128]{2,1,0:T(8,128)(2,1)S(1)} %collective-permute-done.70.refs_17_.refs_10_), channel_id=1, source_target_pairs={{0,4},{1,5},{2,6},{3,7},{4,8},{5,9},{6,10},{7,11},{8,12},{9,13},{1... | collective-permute-start | bytes 1572872 | tf_op jit(solution)/shard_map/ppermute | solution.py:240
  292.1 12.4 %collective-permute-start.73 = (bf16[4,256,128]{2,1,0:T(8,128)(2,1)S(1)}, bf16[4,256,128]{2,1,0:T(8,128)(2,1)S(1)}, u32[]{:S(2)}, u32[]{:S(2)}) collective-permute-start(bf16[4,256,128]{2,1,0:T(8,128)(2,1)S(1)} %get-tuple-element.168), channel_id=1, source_target_pairs={{0,3},{1,2},{2,1},{3,0},{4,7},{5,6},{6,5},{7,4},{8,11},{9,10},{10,... | collective-permute-start | bytes 786440 | tf_op jit(solution)/shard_map/ppermute | solution.py:247
  295.2 14.1 %collective-permute-start.75 = (bf16[4,256,128]{2,1,0:T(8,128)(2,1)S(1)}, bf16[4,256,128]{2,1,0:T(8,128)(2,1)S(1)}, u32[]{:S(2)}, u32[]{:S(2)}) collective-permute-start(bf16[4,256,128]{2,1,0:T(8,128)(2,1)S(1)} %get-tuple-element.170), channel_id=1, source_target_pairs={{0,1},{1,0},{2,3},{3,2},{4,5},{5,4},{6,7},{7,6},{8,9},{9,8},{10,11... | collective-permute-start | bytes 786440 | tf_op jit(solution)/shard_map/ppermute | solution.py:247
  295.7 14.9 %collective-permute-start.76 = (bf16[4,256,128]{2,1,0:T(8,128)(2,1)S(1)}, bf16[4,256,128]{2,1,0:T(8,128)(2,1)S(1)}, u32[]{:S(2)}, u32[]{:S(2)}) collective-permute-start(bf16[4,256,128]{2,1,0:T(8,128)(2,1)S(1)} %get-tuple-element.171), channel_id=1, source_target_pairs={{0,2},{1,3},{2,0},{3,1},{4,6},{5,7},{6,4},{7,5},{8,10},{9,11},{10,... | collective-permute-start | bytes 786440 | tf_op jit(solution)/shard_map/ppermute | solution.py:247
  298.0 17.7 %collective-permute-start.77 = (bf16[4,256,128]{2,1,0:T(8,128)(2,1)S(1)}, bf16[4,256,128]{2,1,0:T(8,128)(2,1)S(1)}, u32[]{:S(2)}, u32[]{:S(2)}) collective-permute-start(bf16[4,256,128]{2,1,0:T(8,128)(2,1)S(1)} %get-tuple-element.172), channel_id=1, source_target_pairs={{0,3},{1,2},{2,1},{3,0},{4,7},{5,6},{6,5},{7,4},{8,11},{9,10},{10,... | collective-permute-start | bytes 786440 | tf_op jit(solution)/shard_map/ppermute | solution.py:247
  300.2 15.5 %collective-permute-start.78 = (bf16[4,256,128]{2,1,0:T(8,128)(2,1)S(1)}, bf16[4,256,128]{2,1,0:T(8,128)(2,1)S(1)}, u32[]{:S(2)}, u32[]{:S(2)}) collective-permute-start(bf16[4,256,128]{2,1,0:T(8,128)(2,1)S(1)} %get-tuple-element.173), channel_id=1, source_target_pairs={{0,16},{1,17},{2,18},{3,19},{4,20},{5,21},{6,22},{7,23},{8,24},{9,... | collective-permute-start | bytes 786440 | tf_op jit(solution)/shard_map/ppermute | solution.py:254
  304.5 13.2 %collective-permute-start.79 = (bf16[4,256,128]{2,1,0:T(8,128)(2,1)S(1)}, bf16[4,256,128]{2,1,0:T(8,128)(2,1)S(1)}, u32[]{:S(2)}, u32[]{:S(2)}) collective-permute-start(bf16[4,256,128]{2,1,0:T(8,128)(2,1)S(1)} %get-tuple-element.174), channel_id=1, source_target_pairs={{0,17},{1,16},{2,19},{3,18},{4,21},{5,20},{6,23},{7,22},{8,25},{9,... | collective-permute-start | bytes 786440 | tf_op jit(solution)/shard_map/ppermute | solution.py:254
  (44 other events, 394.5 us)

commit v4 on v3

--- a/solution.py
+++ b/solution.py
@@ -67,12 +67,12 @@
         for b in range(1, blocks):
             for move in fetches(b):
                 move.start()
-        for i in range(n_got):
-            gather(i).wait()
         for b in range(blocks):
             for move in fetches(b):
                 move.wait()
             total = jnp.dot(lower[b], draws[b], preferred_element_type=jnp.float32)
+            for i in range(n_got if b == 0 else 0):
+                gather(i).wait()
             if not first:
                 for j in range(slots):
                     place = tbl[b * slots + j]

time: 331 us -> 331 us (level)
  no operation moved by 1% of the time
where the time goes in v4:
time: 331 us; the launch traced here: 329 us
  waiting for transfers between devices  159 us (48%)
  starting transfers between devices  89.6 us (27%)
  Pallas kernels  67.7 us (20%)
  local copies, waits for them, and re-layouts  10.4 us (3%)
    ppermute x18, waiting for transfers between devices, ring_z(): held.append(lax.ppermute(held[-1], 'lvl', links))  66.9 us
    ppermute x24, waiting for transfers between devices, swap_plane(): got.append(lax.ppermute(prior[k], ('tile', 'lvl'), links))  48 us
    pallas_call x8, Pallas kernels, level_blocks(): pl.pallas_call(body, in_specs=[pl.BlockSpec(memory_space=pltpu.SMEM)] + [...  45.3 us
    ppermute x36, waiting for transfers between devices, swap_plane(): got.append(lax.ppermute(same[k], 'lvl', across(k, peer_count)))  43.9 us
    ppermute x36, starting transfers between devices, swap_plane(): got.append(lax.ppermute(same[k], 'lvl', across(k, peer_count)))  39.3 us
    ppermute x24, starting transfers between devices, swap_plane(): got.append(lax.ppermute(prior[k], ('tile', 'lvl'), links))  31.3 us
    pallas_call x12, Pallas kernels, pick(): pl.pallas_call(body, in_specs=[pl.BlockSpec(memory_space=pltpu.SMEM)] + [...  22.4 us
    ppermute x18, starting transfers between devices, ring_z(): held.append(lax.ppermute(held[-1], 'lvl', links))  13 us
  transfers between devices with their start and end apart: 82, of which 40 were waited for; matrix products, arithmetic and copies ran while one was open for 2% of the time, Pallas kernels for 17%

profile of v4, /device:TPU:1, one launch (start us, length us, event | category | flops | bytes accessed | tf_op | source)
XLA Modules:
  0.0 329.3 jit_solution(9388050793845338215)
XLA Ops:
  3.9 3.7 %collective-permute-start.3 = (s32[2,3,32]{2,1,0:T(4,128)S(1)}, s32[2,3,32]{2,1,0:T(4,128)S(1)}, u32[]{:S(2)}, u32[]{:S(2)}) collective-permute-start(s32[2,3,32]{2,1,0:T(4,128)S(1)} %get-tuple-element.217), channel_id=1, source_target_pairs={{0,3},{1,2},{2,1},{3,0},{4,7},{5,6},{6,5},{7,4},{8,11},{9,10},{10,... | collective-permute-start | bytes 2312 | tf_op jit(solution)/shard_map/ppermute | solution.py:192
  7.9 4.9 %level_0_0.1 = (bf16[8,256,128]{2,1,0:T(8,128)(2,1)}, bf16[4,8,256,256]{3,2,1,0:T(8,128)(2,1)}) custom-call(s32[32]{0:T(128)} %get-tuple-element.225.refs_0_, bf16[4,8,256,256]{3,2,1,0:T(8,128)(2,1)} %refs_1_.15, bf16[4,8,256,256]{3,2,1,0:T(8,128)(2,1)} %refs_2_.15), custom_call_target="tpu_custom_call" | custom-call | flops 134217728 | bytes 8000000 | tf_op jit(solution)/shard_map/level_0_0/pallas_call | solution.py:98
  15.2 12.7 %collective-permute-done.4.refs_4_.refs_1_ = bf16[8,256,128]{2,1,0:T(8,128)(2,1)S(1)} collective-permute-done((bf16[8,256,128]{2,1,0:T(8,128)(2,1)}, bf16[8,256,128]{2,1,0:T(8,128)(2,1)S(1)}, u32[]{:S(2)}, u32[]{:S(2)}) %collective-permute-start.4) | collective-permute-done | bytes 524320 | tf_op jit(solution)/shard_map/ppermute | solution.py:240
  28.7 5.0 %level_0_1.1 = (bf16[8,256,128]{2,1,0:T(8,128)(2,1)}, bf16[4,8,256,256]{3,2,1,0:T(8,128)(2,1)}) custom-call(s32[32]{0:T(128)} %get-tuple-element.225.refs_0_, bf16[4,8,256,256]{3,2,1,0:T(8,128)(2,1)} %refs_1_.15, bf16[4,8,256,256]{3,2,1,0:T(8,128)(2,1)} %refs_2_.15, ...), custom_call_target="tpu_custom_call", output_to_operand_aliasing={{1}: (3, {})} | custom-call | flops 134217728 | bytes 8000000 | tf_op jit(solution)/shard_map/level_0_1/pallas_call | solution.py:98
  35.8 5.8 %collective-permute-done.9.refs_2_ = bf16[8,256,128]{2,1,0:T(8,128)(2,1)S(1)} collective-permute-done((bf16[8,256,128]{2,1,0:T(8,128)(2,1)S(1)}, bf16[8,256,128]{2,1,0:T(8,128)(2,1)S(1)}, u32[]{:S(2)}, u32[]{:S(2)}) %collective-permute-start.9) | collective-permute-done | bytes 524320 | tf_op jit(solution)/shard_map/ppermute | solution.py:240
  46.8 6.1 %collective-permute-done.5.refs_1_ = bf16[8,256,128]{2,1,0:T(8,128)(2,1)S(1)} collective-permute-done((bf16[8,256,128]{2,1,0:T(8,128)(2,1)}, bf16[8,256,128]{2,1,0:T(8,128)(2,1)S(1)}, u32[]{:S(2)}, u32[]{:S(2)}) %collective-permute-start.5) | collective-permute-done | bytes 524320 | tf_op jit(solution)/shard_map/ppermute | solution.py:240
  56.7 7.3 %collective-permute-done.10.refs_3_ = bf16[8,256,128]{2,1,0:T(8,128)(2,1)S(1)} collective-permute-done((bf16[8,256,128]{2,1,0:T(8,128)(2,1)S(1)}, bf16[8,256,128]{2,1,0:T(8,128)(2,1)S(1)}, u32[]{:S(2)}, u32[]{:S(2)}) %collective-permute-start.10) | collective-permute-done | bytes 524320 | tf_op jit(solution)/shard_map/ppermute | solution.py:240
  72.3 3.1 collective-permute-done.18.refs_17_.refs_2_
  79.3 5.7 %collective-permute-done.15.refs_13_ = bf16[4,256,128]{2,1,0:T(8,128)(2,1)S(1)} collective-permute-done((bf16[4,256,128]{2,1,0:T(8,128)(2,1)S(1)}, bf16[4,256,128]{2,1,0:T(8,128)(2,1)S(1)}, u32[]{:S(2)}, u32[]{:S(2)}) %collective-permute-start.15) | collective-permute-done | bytes 262176 | tf_op jit(solution)/shard_map/ppermute | solution.py:254
  86.3 4.3 %collective-permute-done.17.refs_15_ = bf16[4,256,128]{2,1,0:T(8,128)(2,1)S(1)} collective-permute-done((bf16[4,256,128]{2,1,0:T(8,128)(2,1)S(1)}, bf16[4,256,128]{2,1,0:T(8,128)(2,1)S(1)}, u32[]{:S(2)}, u32[]{:S(2)}) %collective-permute-start.17) | collective-permute-done | bytes 262176 | tf_op jit(solution)/shard_map/ppermute | solution.py:254
  90.7 5.8 %level_1_0.1 = (bf16[8,256,128]{2,1,0:T(8,128)(2,1)S(1)}, bf16[4,8,256,256]{3,2,1,0:T(8,128)(2,1)}) custom-call(s32[32]{0:T(128)S(1)} %copy-done.8, bf16[4,8,256,256]{3,2,1,0:T(8,128)(2,1)} %refs_1_.15, bf16[4,8,256,256]{3,2,1,0:T(8,128)(2,1)} %refs_2_.15, bf16[3,8,4,256,256]{4,3,2,1,0:T(8,128)(2,1)} %refs_3_.11, ...), custom_call_target="tpu_custom_call", output_to_operand_aliasing={{1}: (16, {})} | custom-call | flops 134217728 | bytes 8000000 | tf_op jit(solution)/shard_map/level_1_0/pallas_call | solution.py:98
  103.2 3.4 %collective-permute-done.19.refs_5_ = bf16[4,256,128]{2,1,0:T(8,128)(2,1)S(1)} collective-permute-done((bf16[4,256,128]{2,1,0:T(8,128)(2,1)S(1)}, bf16[4,256,128]{2,1,0:T(8,128)(2,1)S(1)}, u32[]{:S(2)}, u32[]{:S(2)}) %collective-permute-start.19) | collective-permute-done | bytes 262176 | tf_op jit(solution)/shard_map/ppermute | solution.py:247
  106.9 4.2 %collective-permute-done.30.refs_3_.refs_5_ = bf16[8,256,128]{2,1,0:T(8,128)(2,1)S(1)} collective-permute-done((bf16[8,256,128]{2,1,0:T(8,128)(2,1)S(1)}, bf16[8,256,128]{2,1,0:T(8,128)(2,1)S(1)}, u32[]{:S(2)}, u32[]{:S(2)}) %collective-permute-start.30) | collective-permute-done | bytes 524320 | tf_op jit(solution)/shard_map/ppermute | solution.py:240
  111.1 2.5 collective-permute-start.25
  114.9 2.9 collective-permute-done.23.refs_9_
  119.1 2.9 collective-permute-done.24.refs_10_
  126.5 3.1 collective-permute-done.28.refs_14_
  129.6 2.9 collective-permute-done.29.refs_15_
  132.6 5.8 %level_1_1.1 = (bf16[8,256,128]{2,1,0:T(8,128)(2,1)S(1)}, bf16[4,8,256,256]{3,2,1,0:T(8,128)(2,1)}) custom-call(s32[32]{0:T(128)S(1)} %copy-done.8, bf16[4,8,256,256]{3,2,1,0:T(8,128)(2,1)} %refs_1_.15, bf16[4,8,256,256]{3,2,1,0:T(8,128)(2,1)} %refs_2_.15, bf16[3,8,4,256,256]{4,3,2,1,0:T(8,128)(2,1)} %refs_3_.11, ...), custom_call_target="tpu_custom_call", output_to_operand_aliasing={{1}: (16, {})} | custom-call | flops 134217728 | bytes 8000000 | tf_op jit(solution)/shard_map/level_1_1/pallas_call | solution.py:98
  148.7 2.2 collective-permute-start.38
  150.9 2.9 collective-permute-done.32.refs_3_.refs_5_
  157.3 2.7 collective-permute-done.37.refs_9_
  161.2 5.9 %collective-permute-done.38.refs_10_ = bf16[4,256,128]{2,1,0:T(8,128)(2,1)S(1)} collective-permute-done((bf16[4,256,128]{2,1,0:T(8,128)(2,1)S(1)}, bf16[4,256,128]{2,1,0:T(8,128)(2,1)S(1)}, u32[]{:S(2)}, u32[]{:S(2)}) %collective-permute-start.38) | collective-permute-done | bytes 262176 | tf_op jit(solution)/shard_map/ppermute | solution.py:247
  170.7 7.2 %collective-permute-done.42.refs_14_ = bf16[4,256,128]{2,1,0:T(8,128)(2,1)S(1)} collective-permute-done((bf16[4,256,128]{2,1,0:T(8,128)(2,1)S(1)}, bf16[4,256,128]{2,1,0:T(8,128)(2,1)S(1)}, u32[]{:S(2)}, u32[]{:S(2)}) %collective-permute-start.42) | collective-permute-done | bytes 262176 | tf_op jit(solution)/shard_map/ppermute | solution.py:254
  177.9 5.8 %level_2_0.1 = (bf16[8,256,128]{2,1,0:T(8,128)(2,1)S(1)}, bf16[4,8,256,256]{3,2,1,0:T(8,128)(2,1)}) custom-call(s32[32]{0:T(128)S(1)} %get-tuple-element.224.refs_0_, bf16[4,8,256,256]{3,2,1,0:T(8,128)(2,1)} %refs_1_.15, bf16[4,8,256,256]{3,2,1,0:T(8,128)(2,1)} %refs_2_.15, bf16[3,8,4,256,256]{4,3,2,1,0:T(8,128)(2,1)} %refs_3_.11, ...), custom_call_target="tpu_custom_call", output_to_operand_aliasing={{1}: (16, {})} | custom-call | flops 134217728 | bytes 8000000 | tf_op jit(solution)/shard_map/level_2_0/pallas_call | solution.py:98
  191.3 3.4 %collective-permute-done.45.refs_5_ = bf16[4,256,128]{2,1,0:T(8,128)(2,1)S(1)} collective-permute-done((bf16[4,256,128]{2,1,0:T(8,128)(2,1)S(1)}, bf16[4,256,128]{2,1,0:T(8,128)(2,1)S(1)}, u32[]{:S(2)}, u32[]{:S(2)}) %collective-permute-start.45) | collective-permute-done | bytes 262176 | tf_op jit(solution)/shard_map/ppermute | solution.py:247
  195.3 6.7 %collective-permute-start.51 = (bf16[4,256,128]{2,1,0:T(8,128)(2,1)S(1)}, bf16[4,256,128]{2,1,0:T(8,128)(2,1)S(1)}, u32[]{:S(2)}, u32[]{:S(2)}) collective-permute-start(bf16[4,256,128]{2,1,0:T(8,128)(2,1)S(1)} %get-tuple-element.144), channel_id=1, source_target_pairs={{0,3},{1,2},{2,1},{3,0},{4,7},{5,6},{6,5},{7,4},{8,11},{9,10},{10,... | collective-permute-start | bytes 786440 | tf_op jit(solution)/shard_map/ppermute | solution.py:247
  202.0 3.3 %collective-permute-start.57 = (bf16[8,256,128]{2,1,0:T(8,128)(2,1)S(1)}, bf16[8,256,128]{2,1,0:T(8,128)(2,1)S(1)}, u32[]{:S(2)}, u32[]{:S(2)}) collective-permute-start(bf16[8,256,128]{2,1,0:T(8,128)(2,1)S(1)} %collective-permute-done.56.refs_5_.refs_9_), channel_id=1, source_target_pairs={{0,4},{1,5},{2,6},{3,7},{4,8},{5,9},{6,10},{7,11},{8,12},{9,13},{1... | collective-permute-start | bytes 1572872 | tf_op jit(solution)/shard_map/ppermute | solution.py:240
  209.2 2.6 collective-permute-done.51.refs_11_
  215.9 5.7 %collective-permute-done.55.refs_15_ = bf16[4,256,128]{2,1,0:T(8,128)(2,1)S(1)} collective-permute-done((bf16[4,256,128]{2,1,0:T(8,128)(2,1)S(1)}, bf16[4,256,128]{2,1,0:T(8,128)(2,1)S(1)}, u32[]{:S(2)}, u32[]{:S(2)}) %collective-permute-start.55) | collective-permute-done | bytes 262176 | tf_op jit(solution)/shard_map/ppermute | solution.py:254
  221.6 5.8 %level_2_1.1 = (bf16[8,256,128]{2,1,0:T(8,128)(2,1)S(1)}, bf16[4,8,256,256]{3,2,1,0:T(8,128)(2,1)}) custom-call(s32[32]{0:T(128)S(1)} %get-tuple-element.224.refs_0_, bf16[4,8,256,256]{3,2,1,0:T(8,128)(2,1)} %refs_1_.15, bf16[4,8,256,256]{3,2,1,0:T(8,128)(2,1)} %refs_2_.15, bf16[3,8,4,256,256]{4,3,2,1,0:T(8,128)(2,1)} %refs_3_.11, ...), custom_call_target="tpu_custom_call", output_to_operand_aliasing={{1}: (16, {})} | custom-call | flops 134217728 | bytes 8000000 | tf_op jit(solution)/shard_map/level_2_1/pallas_call | solution.py:98
  227.4 2.6 collective-permute-start.58
  231.0 12.1 %collective-permute-done.58.refs_5_.refs_9_ = bf16[8,256,128]{2,1,0:T(8,128)(2,1)S(1)} collective-permute-done((bf16[8,256,128]{2,1,0:T(8,128)(2,1)S(1)}, bf16[8,256,128]{2,1,0:T(8,128)(2,1)S(1)}, u32[]{:S(2)}, u32[]{:S(2)}) %collective-permute-start.58) | collective-permute-done | bytes 524320 | tf_op jit(solution)/shard_map/ppermute | solution.py:240
  245.5 2.2 collective-permute-start.59
  248.9 5.3 %collective-permute-done.62.refs_11_ = bf16[8,256,128]{2,1,0:T(8,128)(2,1)S(1)} collective-permute-done((bf16[8,256,128]{2,1,0:T(8,128)(2,1)S(1)}, bf16[8,256,128]{2,1,0:T(8,128)(2,1)S(1)}, u32[]{:S(2)}, u32[]{:S(2)}) %collective-permute-start.62) | collective-permute-done | bytes 524320 | tf_op jit(solution)/shard_map/ppermute | solution.py:240
  254.3 2.2 pick_2_0_1.1
  259.5 5.4 %collective-permute-done.70.refs_17_.refs_10_ = bf16[8,256,128]{2,1,0:T(8,128)(2,1)S(1)} collective-permute-done((bf16[8,256,128]{2,1,0:T(8,128)(2,1)S(1)}, bf16[8,256,128]{2,1,0:T(8,128)(2,1)S(1)}, u32[]{:S(2)}, u32[]{:S(2)}) %collective-permute-start.70) | collective-permute-done | bytes 524320 | tf_op jit(solution)/shard_map/ppermute | solution.py:240
  268.9 3.3 %collective-permute-done.64.refs_10_ = bf16[4,256,128]{2,1,0:T(8,128)(2,1)S(1)} collective-permute-done((bf16[4,256,128]{2,1,0:T(8,128)(2,1)S(1)}, bf16[4,256,128]{2,1,0:T(8,128)(2,1)S(1)}, u32[]{:S(2)}, u32[]{:S(2)}) %collective-permute-start.64) | collective-permute-done | bytes 262176 | tf_op jit(solution)/shard_map/ppermute | solution.py:247
  276.0 6.7 %collective-permute-done.68.refs_14_ = bf16[4,256,128]{2,1,0:T(8,128)(2,1)S(1)} collective-permute-done((bf16[4,256,128]{2,1,0:T(8,128)(2,1)S(1)}, bf16[4,256,128]{2,1,0:T(8,128)(2,1)S(1)}, u32[]{:S(2)}, u32[]{:S(2)}) %collective-permute-start.68) | collective-permute-done | bytes 262176 | tf_op jit(solution)/shard_map/ppermute | solution.py:254
  282.7 5.8 %level_3_0.1 = (bf16[8,256,128]{2,1,0:T(8,128)(2,1)S(1)}, bf16[4,8,256,256]{3,2,1,0:T(8,128)(2,1)}) custom-call(s32[32]{0:T(128)S(1)} %get-tuple-element.226.refs_0_, bf16[4,8,256,256]{3,2,1,0:T(8,128)(2,1)} %refs_1_.15, bf16[4,8,256,256]{3,2,1,0:T(8,128)(2,1)} %refs_2_.15, bf16[3,8,4,256,256]{4,3,2,1,0:T(8,128)(2,1)} %refs_3_.11, ...), custom_call_target="tpu_custom_call", output_to_operand_aliasing={{1}: (16, {})} | custom-call | flops 134217728 | bytes 8000000 | tf_op jit(solution)/shard_map/level_3_0/pallas_call | solution.py:98
  290.7 2.1 collective-permute-start.73
  292.8 2.2 pick_2_1_1.1
  295.8 2.3 collective-permute-done.71.refs_5_
  299.9 4.1 %collective-permute-done.73.refs_7_ = bf16[4,256,128]{2,1,0:T(8,128)(2,1)S(1)} collective-permute-done((bf16[4,256,128]{2,1,0:T(8,128)(2,1)S(1)}, bf16[4,256,128]{2,1,0:T(8,128)(2,1)S(1)}, u32[]{:S(2)}, u32[]{:S(2)}) %collective-permute-start.73) | collective-permute-done | bytes 262176 | tf_op jit(solution)/shard_map/ppermute | solution.py:247
  305.3 4.2 %collective-permute-done.75.refs_9_ = bf16[4,256,128]{2,1,0:T(8,128)(2,1)S(1)} collective-permute-done((bf16[4,256,128]{2,1,0:T(8,128)(2,1)S(1)}, bf16[4,256,128]{2,1,0:T(8,128)(2,1)S(1)}, u32[]{:S(2)}, u32[]{:S(2)}) %collective-permute-start.75) | collective-permute-done | bytes 262176 | tf_op jit(solution)/shard_map/ppermute | solution.py:247
  312.3 2.9 collective-permute-done.77.refs_11_
  318.0 4.5 %collective-permute-done.81.refs_15_ = bf16[4,256,128]{2,1,0:T(8,128)(2,1)S(1)} collective-permute-done((bf16[4,256,128]{2,1,0:T(8,128)(2,1)S(1)}, bf16[4,256,128]{2,1,0:T(8,128)(2,1)S(1)}, u32[]{:S(2)}, u32[]{:S(2)}) %collective-permute-start.81) | collective-permute-done | bytes 262176 | tf_op jit(solution)/shard_map/ppermute | solution.py:254
  322.5 6.6 %level_3_1.1 = (bf16[8,256,128]{2,1,0:T(8,128)(2,1)}, bf16[4,8,256,256]{3,2,1,0:T(8,128)(2,1)}) custom-call(s32[32]{0:T(128)S(1)} %get-tuple-element.226.refs_0_, bf16[4,8,256,256]{3,2,1,0:T(8,128)(2,1)} %refs_1_.15, bf16[4,8,256,256]{3,2,1,0:T(8,128)(2,1)} %refs_2_.15, bf16[3,8,4,256,256]{4,3,2,1,0:T(8,128)(2,1)} %refs_3_.11, ...), custom_call_target="tpu_custom_call", output_to_operand_aliasing={{1}: (16, {})} | custom-call | flops 134217728 | bytes 8000000 | tf_op jit(solution)/shard_map/level_3_1/pallas_call | solution.py:98
  (228 shorter events, 107.7 us)
Async XLA Ops:
  12.8 15.1 %collective-permute-start.4 = (bf16[8,256,128]{2,1,0:T(8,128)(2,1)}, bf16[8,256,128]{2,1,0:T(8,128)(2,1)S(1)}, u32[]{:S(2)}, u32[]{:S(2)}) collective-permute-start(bf16[8,256,128]{2,1,0:T(8,128)(2,1)} %get-tuple-element.93.refs_0_), channel_id=1, source_target_pairs={{0,4},{1,5},{2,6},{3,7},{4,8},{5,9},{6,10},{7,11},{8,12},{9,13},{1... | collective-permute-start | bytes 1572872 | tf_op jit(solution)/shard_map/ppermute | solution.py:240
  27.9 13.7 %collective-permute-start.9 = (bf16[8,256,128]{2,1,0:T(8,128)(2,1)S(1)}, bf16[8,256,128]{2,1,0:T(8,128)(2,1)S(1)}, u32[]{:S(2)}, u32[]{:S(2)}) collective-permute-start(bf16[8,256,128]{2,1,0:T(8,128)(2,1)S(1)} %collective-permute-done.4.refs_4_.refs_1_), channel_id=1, source_target_pairs={{0,4},{1,5},{2,6},{3,7},{4,8},{5,9},{6,10},{7,11},{8,12},{9,13},{1... | collective-permute-start | bytes 1572872 | tf_op jit(solution)/shard_map/ppermute | solution.py:240
  33.8 19.1 %collective-permute-start.5 = (bf16[8,256,128]{2,1,0:T(8,128)(2,1)}, bf16[8,256,128]{2,1,0:T(8,128)(2,1)S(1)}, u32[]{:S(2)}, u32[]{:S(2)}) collective-permute-start(bf16[8,256,128]{2,1,0:T(8,128)(2,1)} %get-tuple-element.94.refs_2_.refs_4_.refs_0_), channel_id=1, source_target_pairs={{0,4},{1,5},{2,6},{3,7},{4,8},{5,9},{6,10},{7,11},{8,12},{9,13},{1... | collective-permute-start | bytes 1572872 | tf_op jit(solution)/shard_map/ppermute | solution.py:240
  41.6 22.5 %collective-permute-start.10 = (bf16[8,256,128]{2,1,0:T(8,128)(2,1)S(1)}, bf16[8,256,128]{2,1,0:T(8,128)(2,1)S(1)}, u32[]{:S(2)}, u32[]{:S(2)}) collective-permute-start(bf16[8,256,128]{2,1,0:T(8,128)(2,1)S(1)} %collective-permute-done.9.refs_2_), channel_id=1, source_target_pairs={{0,4},{1,5},{2,6},{3,7},{4,8},{5,9},{6,10},{7,11},{8,12},{9,13},{1... | collective-permute-start | bytes 1572872 | tf_op jit(solution)/shard_map/ppermute | solution.py:240
  46.1 22.4 %collective-permute-start.6 = (bf16[4,256,128]{2,1,0:T(8,128)(2,1)}, bf16[4,256,128]{2,1,0:T(8,128)(2,1)S(1)}, u32[]{:S(2)}, u32[]{:S(2)}) collective-permute-start(bf16[4,256,128]{2,1,0:T(8,128)(2,1)} %get-tuple-element.96), channel_id=1, source_target_pairs={{0,1},{1,0},{2,3},{3,2},{4,5},{5,4},{6,7},{7,6},{8,9},{9,8},{10,11... | collective-permute-start | bytes 786440 | tf_op jit(solution)/shard_map/ppermute | solution.py:247
  52.9 22.5 %collective-permute-start.18 = (bf16[8,256,128]{2,1,0:T(8,128)(2,1)S(1)}, bf16[8,256,128]{2,1,0:T(8,128)(2,1)S(1)}, u32[]{:S(2)}, u32[]{:S(2)}) collective-permute-start(bf16[8,256,128]{2,1,0:T(8,128)(2,1)S(1)} %collective-permute-done.5.refs_1_), channel_id=1, source_target_pairs={{0,4},{1,5},{2,6},{3,7},{4,8},{5,9},{6,10},{7,11},{8,12},{9,13},{1... | collective-permute-start | bytes 1572872 | tf_op jit(solution)/shard_map/ppermute | solution.py:240
  54.8 15.5 %collective-permute-start.7 = (bf16[4,256,128]{2,1,0:T(8,128)(2,1)}, bf16[4,256,128]{2,1,0:T(8,128)(2,1)S(1)}, u32[]{:S(2)}, u32[]{:S(2)}) collective-permute-start(bf16[4,256,128]{2,1,0:T(8,128)(2,1)} %copy-done.9), channel_id=1, source_target_pairs={{0,2},{1,3},{2,0},{3,1},{4,6},{5,7},{6,4},{7,5},{8,10},{9,11},{10,... | collective-permute-start | bytes 786440 | tf_op jit(solution)/shard_map/ppermute | solution.py:247
  55.6 15.4 %collective-permute-start.8 = (bf16[4,256,128]{2,1,0:T(8,128)(2,1)S(1)}, bf16[4,256,128]{2,1,0:T(8,128)(2,1)S(1)}, u32[]{:S(2)}, u32[]{:S(2)}) collective-permute-start(bf16[4,256,128]{2,1,0:T(8,128)(2,1)S(1)} %get-tuple-element.98), channel_id=1, source_target_pairs={{0,3},{1,2},{2,1},{3,0},{4,7},{5,6},{6,5},{7,4},{8,11},{9,10},{10,... | collective-permute-start | bytes 786440 | tf_op jit(solution)/shard_map/ppermute | solution.py:247
  77.9 12.7 %collective-permute-start.17 = (bf16[4,256,128]{2,1,0:T(8,128)(2,1)S(1)}, bf16[4,256,128]{2,1,0:T(8,128)(2,1)S(1)}, u32[]{:S(2)}, u32[]{:S(2)}) collective-permute-start(bf16[4,256,128]{2,1,0:T(8,128)(2,1)S(1)} %get-tuple-element.106), channel_id=1, source_target_pairs={{0,19},{1,18},{2,17},{3,16},{4,23},{5,22},{6,21},{7,20},{8,27},{9,... | collective-permute-start | bytes 786440 | tf_op jit(solution)/shard_map/ppermute | solution.py:254
  79.3 21.6 %collective-permute-start.22 = (bf16[8,256,128]{2,1,0:T(8,128)(2,1)S(1)}, bf16[8,256,128]{2,1,0:T(8,128)(2,1)S(1)}, u32[]{:S(2)}, u32[]{:S(2)}) collective-permute-start(bf16[8,256,128]{2,1,0:T(8,128)(2,1)S(1)} %collective-permute-done.18.refs_17_.refs_2_), channel_id=1, source_target_pairs={{0,4},{1,5},{2,6},{3,7},{4,8},{5,9},{6,10},{7,11},{8,12},{9,13},{1... | collective-permute-start | bytes 1572872 | tf_op jit(solution)/shard_map/ppermute | solution.py:240
  96.4 14.7 %collective-permute-start.30 = (bf16[8,256,128]{2,1,0:T(8,128)(2,1)S(1)}, bf16[8,256,128]{2,1,0:T(8,128)(2,1)S(1)}, u32[]{:S(2)}, u32[]{:S(2)}) collective-permute-start(bf16[8,256,128]{2,1,0:T(8,128)(2,1)S(1)} %get-tuple-element.108.refs_2_.refs_4_), channel_id=1, source_target_pairs={{0,4},{1,5},{2,6},{3,7},{4,8},{5,9},{6,10},{7,11},{8,12},{9,13},{1... | collective-permute-start | bytes 1572872 | tf_op jit(solution)/shard_map/ppermute | solution.py:240
  98.9 12.2 %collective-permute-start.20 = (bf16[4,256,128]{2,1,0:T(8,128)(2,1)S(1)}, bf16[4,256,128]{2,1,0:T(8,128)(2,1)S(1)}, u32[]{:S(2)}, u32[]{:S(2)}) collective-permute-start(bf16[4,256,128]{2,1,0:T(8,128)(2,1)S(1)} %get-tuple-element.111), channel_id=1, source_target_pairs={{0,2},{1,3},{2,0},{3,1},{4,6},{5,7},{6,4},{7,5},{8,10},{9,11},{10,... | collective-permute-start | bytes 786440 | tf_op jit(solution)/shard_map/ppermute | solution.py:247
  100.1 13.6 %collective-permute-start.21 = (bf16[4,256,128]{2,1,0:T(8,128)(2,1)S(1)}, bf16[4,256,128]{2,1,0:T(8,128)(2,1)S(1)}, u32[]{:S(2)}, u32[]{:S(2)}) collective-permute-start(bf16[4,256,128]{2,1,0:T(8,128)(2,1)S(1)} %get-tuple-element.112), channel_id=1, source_target_pairs={{0,3},{1,2},{2,1},{3,0},{4,7},{5,6},{6,5},{7,4},{8,11},{9,10},{10,... | collective-permute-start | bytes 786440 | tf_op jit(solution)/shard_map/ppermute | solution.py:247
  102.9 14.9 %collective-permute-start.23 = (bf16[4,256,128]{2,1,0:T(8,128)(2,1)S(1)}, bf16[4,256,128]{2,1,0:T(8,128)(2,1)S(1)}, u32[]{:S(2)}, u32[]{:S(2)}) collective-permute-start(bf16[4,256,128]{2,1,0:T(8,128)(2,1)S(1)} %get-tuple-element.114), channel_id=1, source_target_pairs={{0,1},{1,0},{2,3},{3,2},{4,5},{5,4},{6,7},{7,6},{8,9},{9,8},{10,11... | collective-permute-start | bytes 786440 | tf_op jit(solution)/shard_map/ppermute | solution.py:247
  106.5 15.4 %collective-permute-start.24 = (bf16[4,256,128]{2,1,0:T(8,128)(2,1)S(1)}, bf16[4,256,128]{2,1,0:T(8,128)(2,1)S(1)}, u32[]{:S(2)}, u32[]{:S(2)}) collective-permute-start(bf16[4,256,128]{2,1,0:T(8,128)(2,1)S(1)} %get-tuple-element.115), channel_id=1, source_target_pairs={{0,2},{1,3},{2,0},{3,1},{4,6},{5,7},{6,4},{7,5},{8,10},{9,11},{10,... | collective-permute-start | bytes 786440 | tf_op jit(solution)/shard_map/ppermute | solution.py:247
  111.1 15.4 %collective-permute-start.31 = (bf16[8,256,128]{2,1,0:T(8,128)(2,1)S(1)}, bf16[8,256,128]{2,1,0:T(8,128)(2,1)S(1)}, u32[]{:S(2)}, u32[]{:S(2)}) collective-permute-start(bf16[8,256,128]{2,1,0:T(8,128)(2,1)S(1)} %collective-permute-done.30.refs_3_.refs_5_), channel_id=1, source_target_pairs={{0,4},{1,5},{2,6},{3,7},{4,8},{5,9},{6,10},{7,11},{8,12},{9,13},{1... | collective-permute-start | bytes 1572872 | tf_op jit(solution)/shard_map/ppermute | solution.py:240
  111.1 12.2 %collective-permute-start.25 = (bf16[4,256,128]{2,1,0:T(8,128)(2,1)S(1)}, bf16[4,256,128]{2,1,0:T(8,128)(2,1)S(1)}, u32[]{:S(2)}, u32[]{:S(2)}) collective-permute-start(bf16[4,256,128]{2,1,0:T(8,128)(2,1)S(1)} %get-tuple-element.116), channel_id=1, source_target_pairs={{0,3},{1,2},{2,1},{3,0},{4,7},{5,6},{6,5},{7,4},{8,11},{9,10},{10,... | collective-permute-start | bytes 786440 | tf_op jit(solution)/shard_map/ppermute | solution.py:247
  113.6 12.9 %collective-permute-start.26 = (bf16[4,256,128]{2,1,0:T(8,128)(2,1)S(1)}, bf16[4,256,128]{2,1,0:T(8,128)(2,1)S(1)}, u32[]{:S(2)}, u32[]{:S(2)}) collective-permute-start(bf16[4,256,128]{2,1,0:T(8,128)(2,1)S(1)} %get-tuple-element.117), channel_id=1, source_target_pairs={{0,16},{1,17},{2,18},{3,19},{4,20},{5,21},{6,22},{7,23},{8,24},{9,... | collective-permute-start | bytes 786440 | tf_op jit(solution)/shard_map/ppermute | solution.py:254
  126.5 17.2 %collective-permute-start.36 = (bf16[8,256,128]{2,1,0:T(8,128)(2,1)S(1)}, bf16[8,256,128]{2,1,0:T(8,128)(2,1)S(1)}, u32[]{:S(2)}, u32[]{:S(2)}) collective-permute-start(bf16[8,256,128]{2,1,0:T(8,128)(2,1)S(1)} %collective-permute-done.31.refs_17_.refs_6_), channel_id=1, source_target_pairs={{0,4},{1,5},{2,6},{3,7},{4,8},{5,9},{6,10},{7,11},{8,12},{9,13},{1... | collective-permute-start | bytes 1572872 | tf_op jit(solution)/shard_map/ppermute | solution.py:240
  138.3 15.4 %collective-permute-start.32 = (bf16[8,256,128]{2,1,0:T(8,128)(2,1)S(1)}, bf16[8,256,128]{2,1,0:T(8,128)(2,1)S(1)}, u32[]{:S(2)}, u32[]{:S(2)}) collective-permute-start(bf16[8,256,128]{2,1,0:T(8,128)(2,1)S(1)} %get-tuple-element.122.refs_4_.refs_8_.refs_2_), channel_id=1, source_target_pairs={{0,4},{1,5},{2,6},{3,7},{4,8},{5,9},{6,10},{7,11},{8,12},{9,13},{1... | collective-permute-start | bytes 1572872 | tf_op jit(solution)/shard_map/ppermute | solution.py:240
  142.2 13.3 %collective-permute-start.34 = (bf16[4,256,128]{2,1,0:T(8,128)(2,1)S(1)}, bf16[4,256,128]{2,1,0:T(8,128)(2,1)S(1)}, u32[]{:S(2)}, u32[]{:S(2)}) collective-permute-start(bf16[4,256,128]{2,1,0:T(8,128)(2,1)S(1)} %get-tuple-element.125), channel_id=1, source_target_pairs={{0,2},{1,3},{2,0},{3,1},{4,6},{5,7},{6,4},{7,5},{8,10},{9,11},{10,... | collective-permute-start | bytes 786440 | tf_op jit(solution)/shard_map/ppermute | solution.py:247
  143.1 12.9 %collective-permute-start.35 = (bf16[4,256,128]{2,1,0:T(8,128)(2,1)S(1)}, bf16[4,256,128]{2,1,0:T(8,128)(2,1)S(1)}, u32[]{:S(2)}, u32[]{:S(2)}) collective-permute-start(bf16[4,256,128]{2,1,0:T(8,128)(2,1)S(1)} %get-tuple-element.126), channel_id=1, source_target_pairs={{0,3},{1,2},{2,1},{3,0},{4,7},{5,6},{6,5},{7,4},{8,11},{9,10},{10,... | collective-permute-start | bytes 786440 | tf_op jit(solution)/shard_map/ppermute | solution.py:247
  145.7 14.2 %collective-permute-start.37 = (bf16[4,256,128]{2,1,0:T(8,128)(2,1)S(1)}, bf16[4,256,128]{2,1,0:T(8,128)(2,1)S(1)}, u32[]{:S(2)}, u32[]{:S(2)}) collective-permute-start(bf16[4,256,128]{2,1,0:T(8,128)(2,1)S(1)} %get-tuple-element.128), channel_id=1, source_target_pairs={{0,1},{1,0},{2,3},{3,2},{4,5},{5,4},{6,7},{7,6},{8,9},{9,8},{10,11... | collective-permute-start | bytes 786440 | tf_op jit(solution)/shard_map/ppermute | solution.py:247
  148.7 18.4 %collective-permute-start.38 = (bf16[4,256,128]{2,1,0:T(8,128)(2,1)S(1)}, bf16[4,256,128]{2,1,0:T(8,128)(2,1)S(1)}, u32[]{:S(2)}, u32[]{:S(2)}) collective-permute-start(bf16[4,256,128]{2,1,0:T(8,128)(2,1)S(1)} %get-tuple-element.129), channel_id=1, source_target_pairs={{0,2},{1,3},{2,0},{3,1},{4,6},{5,7},{6,4},{7,5},{8,10},{9,11},{10,... | collective-permute-start | bytes 786440 | tf_op jit(solution)/shard_map/ppermute | solution.py:247
  153.8 15.9 %collective-permute-start.44 = (bf16[8,256,128]{2,1,0:T(8,128)(2,1)S(1)}, bf16[8,256,128]{2,1,0:T(8,128)(2,1)S(1)}, u32[]{:S(2)}, u32[]{:S(2)}) collective-permute-start(bf16[8,256,128]{2,1,0:T(8,128)(2,1)S(1)} %collective-permute-done.32.refs_3_.refs_5_), channel_id=1, source_target_pairs={{0,4},{1,5},{2,6},{3,7},{4,8},{5,9},{6,10},{7,11},{8,12},{9,13},{1... | collective-permute-start | bytes 1572872 | tf_op jit(solution)/shard_map/ppermute | solution.py:240
  155.4 12.9 %collective-permute-start.39 = (bf16[4,256,128]{2,1,0:T(8,128)(2,1)S(1)}, bf16[4,256,128]{2,1,0:T(8,128)(2,1)S(1)}, u32[]{:S(2)}, u32[]{:S(2)}) collective-permute-start(bf16[4,256,128]{2,1,0:T(8,128)(2,1)S(1)} %get-tuple-element.130), channel_id=1, source_target_pairs={{0,3},{1,2},{2,1},{3,0},{4,7},{5,6},{6,5},{7,4},{8,11},{9,10},{10,... | collective-permute-start | bytes 786440 | tf_op jit(solution)/shard_map/ppermute | solution.py:247
  156.0 14.7 %collective-permute-start.40 = (bf16[4,256,128]{2,1,0:T(8,128)(2,1)S(1)}, bf16[4,256,128]{2,1,0:T(8,128)(2,1)S(1)}, u32[]{:S(2)}, u32[]{:S(2)}) collective-permute-start(bf16[4,256,128]{2,1,0:T(8,128)(2,1)S(1)} %get-tuple-element.131), channel_id=1, source_target_pairs={{0,16},{1,17},{2,18},{3,19},{4,20},{5,21},{6,22},{7,23},{8,24},{9,... | collective-permute-start | bytes 786440 | tf_op jit(solution)/shard_map/ppermute | solution.py:254
  169.7 19.4 %collective-permute-start.48 = (bf16[8,256,128]{2,1,0:T(8,128)(2,1)S(1)}, bf16[8,256,128]{2,1,0:T(8,128)(2,1)S(1)}, u32[]{:S(2)}, u32[]{:S(2)}) collective-permute-start(bf16[8,256,128]{2,1,0:T(8,128)(2,1)S(1)} %collective-permute-done.44.refs_17_.refs_6_), channel_id=1, source_target_pairs={{0,4},{1,5},{2,6},{3,7},{4,8},{5,9},{6,10},{7,11},{8,12},{9,13},{1... | collective-permute-start | bytes 1572872 | tf_op jit(solution)/shard_map/ppermute | solution.py:240
  183.7 18.3 %collective-permute-start.56 = (bf16[8,256,128]{2,1,0:T(8,128)(2,1)S(1)}, bf16[8,256,128]{2,1,0:T(8,128)(2,1)S(1)}, u32[]{:S(2)}, u32[]{:S(2)}) collective-permute-start(bf16[8,256,128]{2,1,0:T(8,128)(2,1)S(1)} %get-tuple-element.136.refs_4_.refs_8_), channel_id=1, source_target_pairs={{0,4},{1,5},{2,6},{3,7},{4,8},{5,9},{6,10},{7,11},{8,12},{9,13},{1... | collective-permute-start | bytes 1572872 | tf_op jit(solution)/shard_map/ppermute | solution.py:240
  187.4 18.0 %collective-permute-start.47 = (bf16[4,256,128]{2,1,0:T(8,128)(2,1)S(1)}, bf16[4,256,128]{2,1,0:T(8,128)(2,1)S(1)}, u32[]{:S(2)}, u32[]{:S(2)}) collective-permute-start(bf16[4,256,128]{2,1,0:T(8,128)(2,1)S(1)} %get-tuple-element.140), channel_id=1, source_target_pairs={{0,3},{1,2},{2,1},{3,0},{4,7},{5,6},{6,5},{7,4},{8,11},{9,10},{10,... | collective-permute-start | bytes 786440 | tf_op jit(solution)/shard_map/ppermute | solution.py:247
  191.1 15.5 %collective-permute-start.49 = (bf16[4,256,128]{2,1,0:T(8,128)(2,1)S(1)}, bf16[4,256,128]{2,1,0:T(8,128)(2,1)S(1)}, u32[]{:S(2)}, u32[]{:S(2)}) collective-permute-start(bf16[4,256,128]{2,1,0:T(8,128)(2,1)S(1)} %get-tuple-element.142), channel_id=1, source_target_pairs={{0,1},{1,0},{2,3},{3,2},{4,5},{5,4},{6,7},{7,6},{8,9},{9,8},{10,11... | collective-permute-start | bytes 786440 | tf_op jit(solution)/shard_map/ppermute | solution.py:247
  194.7 13.2 %collective-permute-start.50 = (bf16[4,256,128]{2,1,0:T(8,128)(2,1)S(1)}, bf16[4,256,128]{2,1,0:T(8,128)(2,1)S(1)}, u32[]{:S(2)}, u32[]{:S(2)}) collective-permute-start(bf16[4,256,128]{2,1,0:T(8,128)(2,1)S(1)} %get-tuple-element.143), channel_id=1, source_target_pairs={{0,2},{1,3},{2,0},{3,1},{4,6},{5,7},{6,4},{7,5},{8,10},{9,11},{10,... | collective-permute-start | bytes 786440 | tf_op jit(solution)/shard_map/ppermute | solution.py:247
  195.3 16.5 %collective-permute-start.51 = (bf16[4,256,128]{2,1,0:T(8,128)(2,1)S(1)}, bf16[4,256,128]{2,1,0:T(8,128)(2,1)S(1)}, u32[]{:S(2)}, u32[]{:S(2)}) collective-permute-start(bf16[4,256,128]{2,1,0:T(8,128)(2,1)S(1)} %get-tuple-element.144), channel_id=1, source_target_pairs={{0,3},{1,2},{2,1},{3,0},{4,7},{5,6},{6,5},{7,4},{8,11},{9,10},{10,... | collective-permute-start | bytes 786440 | tf_op jit(solution)/shard_map/ppermute | solution.py:247
  202.0 19.6 %collective-permute-start.57 = (bf16[8,256,128]{2,1,0:T(8,128)(2,1)S(1)}, bf16[8,256,128]{2,1,0:T(8,128)(2,1)S(1)}, u32[]{:S(2)}, u32[]{:S(2)}) collective-permute-start(bf16[8,256,128]{2,1,0:T(8,128)(2,1)S(1)} %collective-permute-done.56.refs_5_.refs_9_), channel_id=1, source_target_pairs={{0,4},{1,5},{2,6},{3,7},{4,8},{5,9},{6,10},{7,11},{8,12},{9,13},{1... | collective-permute-start | bytes 1572872 | tf_op jit(solution)/shard_map/ppermute | solution.py:240
  227.4 15.7 %collective-permute-start.58 = (bf16[8,256,128]{2,1,0:T(8,128)(2,1)S(1)}, bf16[8,256,128]{2,1,0:T(8,128)(2,1)S(1)}, u32[]{:S(2)}, u32[]{:S(2)}) collective-permute-start(bf16[8,256,128]{2,1,0:T(8,128)(2,1)S(1)} %get-tuple-element.150.refs_6_.refs_12_.refs_4_.refs_8_), channel_id=1, source_target_pairs={{0,4},{1,5},{2,6},{3,7},{4,8},{5,9},{6,10},{7,11},{8,12},{9,13},{1... | collective-permute-start | bytes 1572872 | tf_op jit(solution)/shard_map/ppermute | solution.py:240
  230.0 24.3 %collective-permute-start.62 = (bf16[8,256,128]{2,1,0:T(8,128)(2,1)S(1)}, bf16[8,256,128]{2,1,0:T(8,128)(2,1)S(1)}, u32[]{:S(2)}, u32[]{:S(2)}) collective-permute-start(bf16[8,256,128]{2,1,0:T(8,128)(2,1)S(1)} %collective-permute-done.57.refs_17_.refs_10_), channel_id=1, source_target_pairs={{0,4},{1,5},{2,6},{3,7},{4,8},{5,9},{6,10},{7,11},{8,12},{9,13},{1... | collective-permute-start | bytes 1572872 | tf_op jit(solution)/shard_map/ppermute | solution.py:240
  243.1 21.9 %collective-permute-start.70 = (bf16[8,256,128]{2,1,0:T(8,128)(2,1)S(1)}, bf16[8,256,128]{2,1,0:T(8,128)(2,1)S(1)}, u32[]{:S(2)}, u32[]{:S(2)}) collective-permute-start(bf16[8,256,128]{2,1,0:T(8,128)(2,1)S(1)} %collective-permute-done.58.refs_5_.refs_9_), channel_id=1, source_target_pairs={{0,4},{1,5},{2,6},{3,7},{4,8},{5,9},{6,10},{7,11},{8,12},{9,13},{1... | collective-permute-start | bytes 1572872 | tf_op jit(solution)/shard_map/ppermute | solution.py:240
  245.5 12.7 %collective-permute-start.59 = (bf16[4,256,128]{2,1,0:T(8,128)(2,1)S(1)}, bf16[4,256,128]{2,1,0:T(8,128)(2,1)S(1)}, u32[]{:S(2)}, u32[]{:S(2)}) collective-permute-start(bf16[4,256,128]{2,1,0:T(8,128)(2,1)S(1)} %get-tuple-element.152), channel_id=1, source_target_pairs={{0,1},{1,0},{2,3},{3,2},{4,5},{5,4},{6,7},{7,6},{8,9},{9,8},{10,11... | collective-permute-start | bytes 786440 | tf_op jit(solution)/shard_map/ppermute | solution.py:247
  248.1 18.2 %collective-permute-start.61 = (bf16[4,256,128]{2,1,0:T(8,128)(2,1)S(1)}, bf16[4,256,128]{2,1,0:T(8,128)(2,1)S(1)}, u32[]{:S(2)}, u32[]{:S(2)}) collective-permute-start(bf16[4,256,128]{2,1,0:T(8,128)(2,1)S(1)} %get-tuple-element.154), channel_id=1, source_target_pairs={{0,3},{1,2},{2,1},{3,0},{4,7},{5,6},{6,5},{7,4},{8,11},{9,10},{10,... | collective-permute-start | bytes 786440 | tf_op jit(solution)/shard_map/ppermute | solution.py:247
  258.3 13.9 %collective-permute-start.64 = (bf16[4,256,128]{2,1,0:T(8,128)(2,1)S(1)}, bf16[4,256,128]{2,1,0:T(8,128)(2,1)S(1)}, u32[]{:S(2)}, u32[]{:S(2)}) collective-permute-start(bf16[4,256,128]{2,1,0:T(8,128)(2,1)S(1)} %get-tuple-element.157), channel_id=1, source_target_pairs={{0,2},{1,3},{2,0},{3,1},{4,6},{5,7},{6,4},{7,5},{8,10},{9,11},{10,... | collective-permute-start | bytes 786440 | tf_op jit(solution)/shard_map/ppermute | solution.py:247
  259.3 14.2 %collective-permute-start.65 = (bf16[4,256,128]{2,1,0:T(8,128)(2,1)S(1)}, bf16[4,256,128]{2,1,0:T(8,128)(2,1)S(1)}, u32[]{:S(2)}, u32[]{:S(2)}) collective-permute-start(bf16[4,256,128]{2,1,0:T(8,128)(2,1)S(1)} %get-tuple-element.158), channel_id=1, source_target_pairs={{0,3},{1,2},{2,1},{3,0},{4,7},{5,6},{6,5},{7,4},{8,11},{9,10},{10,... | collective-permute-start | bytes 786440 | tf_op jit(solution)/shard_map/ppermute | solution.py:247
  264.9 27.8 %collective-permute-start.74 = (bf16[8,256,128]{2,1,0:T(8,128)(2,1)S(1)}, bf16[8,256,128]{2,1,0:T(8,128)(2,1)S(1)}, u32[]{:S(2)}, u32[]{:S(2)}) collective-permute-start(bf16[8,256,128]{2,1,0:T(8,128)(2,1)S(1)} %collective-permute-done.70.refs_17_.refs_10_), channel_id=1, source_target_pairs={{0,4},{1,5},{2,6},{3,7},{4,8},{5,9},{6,10},{7,11},{8,12},{9,13},{1... | collective-permute-start | bytes 1572872 | tf_op jit(solution)/shard_map/ppermute | solution.py:240
  290.7 13.3 %collective-permute-start.73 = (bf16[4,256,128]{2,1,0:T(8,128)(2,1)S(1)}, bf16[4,256,128]{2,1,0:T(8,128)(2,1)S(1)}, u32[]{:S(2)}, u32[]{:S(2)}) collective-permute-start(bf16[4,256,128]{2,1,0:T(8,128)(2,1)S(1)} %get-tuple-element.168), channel_id=1, source_target_pairs={{0,3},{1,2},{2,1},{3,0},{4,7},{5,6},{6,5},{7,4},{8,11},{9,10},{10,... | collective-permute-start | bytes 786440 | tf_op jit(solution)/shard_map/ppermute | solution.py:247
  295.0 14.4 %collective-permute-start.75 = (bf16[4,256,128]{2,1,0:T(8,128)(2,1)S(1)}, bf16[4,256,128]{2,1,0:T(8,128)(2,1)S(1)}, u32[]{:S(2)}, u32[]{:S(2)}) collective-permute-start(bf16[4,256,128]{2,1,0:T(8,128)(2,1)S(1)} %get-tuple-element.170), channel_id=1, source_target_pairs={{0,1},{1,0},{2,3},{3,2},{4,5},{5,4},{6,7},{7,6},{8,9},{9,8},{10,11... | collective-permute-start | bytes 786440 | tf_op jit(solution)/shard_map/ppermute | solution.py:247
  295.1 15.7 %collective-permute-start.76 = (bf16[4,256,128]{2,1,0:T(8,128)(2,1)S(1)}, bf16[4,256,128]{2,1,0:T(8,128)(2,1)S(1)}, u32[]{:S(2)}, u32[]{:S(2)}) collective-permute-start(bf16[4,256,128]{2,1,0:T(8,128)(2,1)S(1)} %get-tuple-element.171), channel_id=1, source_target_pairs={{0,2},{1,3},{2,0},{3,1},{4,6},{5,7},{6,4},{7,5},{8,10},{9,11},{10,... | collective-permute-start | bytes 786440 | tf_op jit(solution)/shard_map/ppermute | solution.py:247
  298.1 17.1 %collective-permute-start.77 = (bf16[4,256,128]{2,1,0:T(8,128)(2,1)S(1)}, bf16[4,256,128]{2,1,0:T(8,128)(2,1)S(1)}, u32[]{:S(2)}, u32[]{:S(2)}) collective-permute-start(bf16[4,256,128]{2,1,0:T(8,128)(2,1)S(1)} %get-tuple-element.172), channel_id=1, source_target_pairs={{0,3},{1,2},{2,1},{3,0},{4,7},{5,6},{6,5},{7,4},{8,11},{9,10},{10,... | collective-permute-start | bytes 786440 | tf_op jit(solution)/shard_map/ppermute | solution.py:247
  298.6 16.6 %collective-permute-start.78 = (bf16[4,256,128]{2,1,0:T(8,128)(2,1)S(1)}, bf16[4,256,128]{2,1,0:T(8,128)(2,1)S(1)}, u32[]{:S(2)}, u32[]{:S(2)}) collective-permute-start(bf16[4,256,128]{2,1,0:T(8,128)(2,1)S(1)} %get-tuple-element.173), channel_id=1, source_target_pairs={{0,16},{1,17},{2,18},{3,19},{4,20},{5,21},{6,22},{7,23},{8,24},{9,... | collective-permute-start | bytes 786440 | tf_op jit(solution)/shard_map/ppermute | solution.py:254
  304.0 13.0 %collective-permute-start.79 = (bf16[4,256,128]{2,1,0:T(8,128)(2,1)S(1)}, bf16[4,256,128]{2,1,0:T(8,128)(2,1)S(1)}, u32[]{:S(2)}, u32[]{:S(2)}) collective-permute-start(bf16[4,256,128]{2,1,0:T(8,128)(2,1)S(1)} %get-tuple-element.174), channel_id=1, source_target_pairs={{0,17},{1,16},{2,19},{3,18},{4,21},{5,20},{6,23},{7,22},{8,25},{9,... | collective-permute-start | bytes 786440 | tf_op jit(solution)/shard_map/ppermute | solution.py:254
  (44 other events, 389.0 us)

commit v5 on v3

--- a/solution.py
+++ b/solution.py
@@ -163,7 +163,7 @@
         out_shape=[jax.ShapeDtypeStruct((same_slots, rows, width), jnp.bfloat16)] * n_same
         + [jax.ShapeDtypeStruct((prior_slots, rows, width), jnp.bfloat16)] * n_prior,
         scratch_shapes=[pltpu.SemaphoreType.DMA((total,))],
-        compiler_params=params(4),
+        compiler_params=params(1),
         cost_estimate=pl.CostEstimate(flops=0, bytes_accessed=6_000_000, transcendentals=0),
         name=name,
     )(table, *flat, *after)

time: 331 us -> 331 us (level)
  waiting for transfers between devices: 160 us -> 167 us
  starting transfers between devices: 87.5 us -> 81.8 us
    ppermute x36, waiting for transfers between devices: 45.8 us -> 50 us  [swap_plane(): got.append(lax.ppermute(same[k], 'lvl', across(k, peer_count)))]
  transfers between devices with their start and end apart: 82 -> 82, of which waited for: 40 -> 39; matrix products, arithmetic and copies ran while one was open for 2% -> 2% of each run, Pallas kernels for 17% -> 17%
where the time goes in v5:
time: 331 us; the launch traced here: 330 us
  waiting for transfers between devices  167 us (50%)
  starting transfers between devices  81.8 us (25%)
  Pallas kernels  68.6 us (21%)
  local copies, waits for them, and re-layouts  10.4 us (3%)
    ppermute x18, waiting for transfers between devices, ring_z(): held.append(lax.ppermute(held[-1], 'lvl', links))  67 us
    ppermute x36, waiting for transfers between devices, swap_plane(): got.append(lax.ppermute(same[k], 'lvl', across(k, peer_count)))  50 us
    ppermute x24, waiting for transfers between devices, swap_plane(): got.append(lax.ppermute(prior[k], ('tile', 'lvl'), links))  49.9 us
    pallas_call x8, Pallas kernels, level_blocks(): pl.pallas_call(body, in_specs=[pl.BlockSpec(memory_space=pltpu.SMEM)] + [...  45.2 us
    ppermute x36, starting transfers between devices, swap_plane(): got.append(lax.ppermute(same[k], 'lvl', across(k, peer_count)))  34.8 us
    ppermute x24, starting transfers between devices, swap_plane(): got.append(lax.ppermute(prior[k], ('tile', 'lvl'), links))  31.3 us
    pallas_call x12, Pallas kernels, pick(): pl.pallas_call(body, in_specs=[pl.BlockSpec(memory_space=pltpu.SMEM)] + [...  23.4 us
    ppermute x18, starting transfers between devices, ring_z(): held.append(lax.ppermute(held[-1], 'lvl', links))  9.63 us
  transfers between devices with their start and end apart: 82, of which 39 were waited for; matrix products, arithmetic and copies ran while one was open for 2% of the time, Pallas kernels for 17%

profile of v5, /device:TPU:1, one launch (start us, length us, event | category | flops | bytes accessed | tf_op | source)
XLA Modules:
  0.0 330.4 jit_solution(16842127544497478203)
XLA Ops:
  3.9 3.7 %collective-permute-start.3 = (s32[2,3,32]{2,1,0:T(4,128)S(1)}, s32[2,3,32]{2,1,0:T(4,128)S(1)}, u32[]{:S(2)}, u32[]{:S(2)}) collective-permute-start(s32[2,3,32]{2,1,0:T(4,128)S(1)} %get-tuple-element.217), channel_id=1, source_target_pairs={{0,3},{1,2},{2,1},{3,0},{4,7},{5,6},{6,5},{7,4},{8,11},{9,10},{10,... | collective-permute-start | bytes 2312 | tf_op jit(solution)/shard_map/ppermute | solution.py:192
  7.9 4.9 %level_0_0.1 = (bf16[8,256,128]{2,1,0:T(8,128)(2,1)}, bf16[4,8,256,256]{3,2,1,0:T(8,128)(2,1)}) custom-call(s32[32]{0:T(128)} %get-tuple-element.225.refs_0_, bf16[4,8,256,256]{3,2,1,0:T(8,128)(2,1)} %refs_1_.15, bf16[4,8,256,256]{3,2,1,0:T(8,128)(2,1)} %refs_2_.15), custom_call_target="tpu_custom_call" | custom-call | flops 134217728 | bytes 8000000 | tf_op jit(solution)/shard_map/level_0_0/pallas_call | solution.py:98
  15.2 12.7 %collective-permute-done.4.refs_4_.refs_1_ = bf16[8,256,128]{2,1,0:T(8,128)(2,1)S(1)} collective-permute-done((bf16[8,256,128]{2,1,0:T(8,128)(2,1)}, bf16[8,256,128]{2,1,0:T(8,128)(2,1)S(1)}, u32[]{:S(2)}, u32[]{:S(2)}) %collective-permute-start.4) | collective-permute-done | bytes 524320 | tf_op jit(solution)/shard_map/ppermute | solution.py:240
  28.7 5.0 %level_0_1.1 = (bf16[8,256,128]{2,1,0:T(8,128)(2,1)}, bf16[4,8,256,256]{3,2,1,0:T(8,128)(2,1)}) custom-call(s32[32]{0:T(128)} %get-tuple-element.225.refs_0_, bf16[4,8,256,256]{3,2,1,0:T(8,128)(2,1)} %refs_1_.15, bf16[4,8,256,256]{3,2,1,0:T(8,128)(2,1)} %refs_2_.15, ...), custom_call_target="tpu_custom_call", output_to_operand_aliasing={{1}: (3, {})} | custom-call | flops 134217728 | bytes 8000000 | tf_op jit(solution)/shard_map/level_0_1/pallas_call | solution.py:98
  35.8 5.8 %collective-permute-done.9.refs_2_ = bf16[8,256,128]{2,1,0:T(8,128)(2,1)S(1)} collective-permute-done((bf16[8,256,128]{2,1,0:T(8,128)(2,1)S(1)}, bf16[8,256,128]{2,1,0:T(8,128)(2,1)S(1)}, u32[]{:S(2)}, u32[]{:S(2)}) %collective-permute-start.9) | collective-permute-done | bytes 524320 | tf_op jit(solution)/shard_map/ppermute | solution.py:240
  46.7 6.2 %collective-permute-done.5.refs_1_ = bf16[8,256,128]{2,1,0:T(8,128)(2,1)S(1)} collective-permute-done((bf16[8,256,128]{2,1,0:T(8,128)(2,1)}, bf16[8,256,128]{2,1,0:T(8,128)(2,1)S(1)}, u32[]{:S(2)}, u32[]{:S(2)}) %collective-permute-start.5) | collective-permute-done | bytes 524320 | tf_op jit(solution)/shard_map/ppermute | solution.py:240
  56.7 7.3 %collective-permute-done.10.refs_3_ = bf16[8,256,128]{2,1,0:T(8,128)(2,1)S(1)} collective-permute-done((bf16[8,256,128]{2,1,0:T(8,128)(2,1)S(1)}, bf16[8,256,128]{2,1,0:T(8,128)(2,1)S(1)}, u32[]{:S(2)}, u32[]{:S(2)}) %collective-permute-start.10) | collective-permute-done | bytes 524320 | tf_op jit(solution)/shard_map/ppermute | solution.py:240
  66.2 2.1 pick_0_0_1.1
  72.3 3.1 collective-permute-done.18.refs_17_.refs_2_
  79.3 5.5 %collective-permute-done.15.refs_13_ = bf16[4,256,128]{2,1,0:T(8,128)(2,1)S(1)} collective-permute-done((bf16[4,256,128]{2,1,0:T(8,128)(2,1)S(1)}, bf16[4,256,128]{2,1,0:T(8,128)(2,1)S(1)}, u32[]{:S(2)}, u32[]{:S(2)}) %collective-permute-start.15) | collective-permute-done | bytes 262176 | tf_op jit(solution)/shard_map/ppermute | solution.py:254
  86.4 4.6 %collective-permute-done.17.refs_15_ = bf16[4,256,128]{2,1,0:T(8,128)(2,1)S(1)} collective-permute-done((bf16[4,256,128]{2,1,0:T(8,128)(2,1)S(1)}, bf16[4,256,128]{2,1,0:T(8,128)(2,1)S(1)}, u32[]{:S(2)}, u32[]{:S(2)}) %collective-permute-start.17) | collective-permute-done | bytes 262176 | tf_op jit(solution)/shard_map/ppermute | solution.py:254
  91.0 5.7 %level_1_0.1 = (bf16[8,256,128]{2,1,0:T(8,128)(2,1)S(1)}, bf16[4,8,256,256]{3,2,1,0:T(8,128)(2,1)}) custom-call(s32[32]{0:T(128)S(1)} %copy-done.8, bf16[4,8,256,256]{3,2,1,0:T(8,128)(2,1)} %refs_1_.15, bf16[4,8,256,256]{3,2,1,0:T(8,128)(2,1)} %refs_2_.15, bf16[3,8,4,256,256]{4,3,2,1,0:T(8,128)(2,1)} %refs_3_.11, ...), custom_call_target="tpu_custom_call", output_to_operand_aliasing={{1}: (16, {})} | custom-call | flops 134217728 | bytes 8000000 | tf_op jit(solution)/shard_map/level_1_0/pallas_call | solution.py:98
  99.0 2.1 collective-permute-start.21
  101.1 2.1 pick_0_1_1.1
  103.6 3.3 collective-permute-done.19.refs_5_
  106.8 2.8 collective-permute-done.30.refs_3_.refs_5_
  110.7 2.5 collective-permute-start.25
  116.8 5.7 %collective-permute-done.24.refs_10_ = bf16[4,256,128]{2,1,0:T(8,128)(2,1)S(1)} collective-permute-done((bf16[4,256,128]{2,1,0:T(8,128)(2,1)S(1)}, bf16[4,256,128]{2,1,0:T(8,128)(2,1)S(1)}, u32[]{:S(2)}, u32[]{:S(2)}) %collective-permute-start.24) | collective-permute-done | bytes 262176 | tf_op jit(solution)/shard_map/ppermute | solution.py:247
  125.3 7.6 %collective-permute-done.28.refs_14_ = bf16[4,256,128]{2,1,0:T(8,128)(2,1)S(1)} collective-permute-done((bf16[4,256,128]{2,1,0:T(8,128)(2,1)S(1)}, bf16[4,256,128]{2,1,0:T(8,128)(2,1)S(1)}, u32[]{:S(2)}, u32[]{:S(2)}) %collective-permute-start.28) | collective-permute-done | bytes 262176 | tf_op jit(solution)/shard_map/ppermute | solution.py:254
  133.0 5.7 %level_1_1.1 = (bf16[8,256,128]{2,1,0:T(8,128)(2,1)S(1)}, bf16[4,8,256,256]{3,2,1,0:T(8,128)(2,1)}) custom-call(s32[32]{0:T(128)S(1)} %copy-done.8, bf16[4,8,256,256]{3,2,1,0:T(8,128)(2,1)} %refs_1_.15, bf16[4,8,256,256]{3,2,1,0:T(8,128)(2,1)} %refs_2_.15, bf16[3,8,4,256,256]{4,3,2,1,0:T(8,128)(2,1)} %refs_3_.11, ...), custom_call_target="tpu_custom_call", output_to_operand_aliasing={{1}: (16, {})} | custom-call | flops 134217728 | bytes 8000000 | tf_op jit(solution)/shard_map/level_1_1/pallas_call | solution.py:98
  141.5 2.0 collective-permute-start.34
  143.7 2.0 pick_1_0_1.1
  148.5 2.3 collective-permute-start.38
  150.9 4.3 %collective-permute-done.32.refs_3_.refs_5_ = bf16[8,256,128]{2,1,0:T(8,128)(2,1)S(1)} collective-permute-done((bf16[8,256,128]{2,1,0:T(8,128)(2,1)S(1)}, bf16[8,256,128]{2,1,0:T(8,128)(2,1)S(1)}, u32[]{:S(2)}, u32[]{:S(2)}) %collective-permute-start.32) | collective-permute-done | bytes 524320 | tf_op jit(solution)/shard_map/ppermute | solution.py:240
  157.7 2.1 collective-permute-done.37.refs_9_
  161.1 6.1 %collective-permute-done.38.refs_10_ = bf16[4,256,128]{2,1,0:T(8,128)(2,1)S(1)} collective-permute-done((bf16[4,256,128]{2,1,0:T(8,128)(2,1)S(1)}, bf16[4,256,128]{2,1,0:T(8,128)(2,1)S(1)}, u32[]{:S(2)}, u32[]{:S(2)}) %collective-permute-start.38) | collective-permute-done | bytes 262176 | tf_op jit(solution)/shard_map/ppermute | solution.py:247
  170.3 7.7 %collective-permute-done.42.refs_14_ = bf16[4,256,128]{2,1,0:T(8,128)(2,1)S(1)} collective-permute-done((bf16[4,256,128]{2,1,0:T(8,128)(2,1)S(1)}, bf16[4,256,128]{2,1,0:T(8,128)(2,1)S(1)}, u32[]{:S(2)}, u32[]{:S(2)}) %collective-permute-start.42) | collective-permute-done | bytes 262176 | tf_op jit(solution)/shard_map/ppermute | solution.py:254
  178.0 5.7 %level_2_0.1 = (bf16[8,256,128]{2,1,0:T(8,128)(2,1)S(1)}, bf16[4,8,256,256]{3,2,1,0:T(8,128)(2,1)}) custom-call(s32[32]{0:T(128)S(1)} %get-tuple-element.224.refs_0_, bf16[4,8,256,256]{3,2,1,0:T(8,128)(2,1)} %refs_1_.15, bf16[4,8,256,256]{3,2,1,0:T(8,128)(2,1)} %refs_2_.15, bf16[3,8,4,256,256]{4,3,2,1,0:T(8,128)(2,1)} %refs_3_.11, ...), custom_call_target="tpu_custom_call", output_to_operand_aliasing={{1}: (16, {})} | custom-call | flops 134217728 | bytes 8000000 | tf_op jit(solution)/shard_map/level_2_0/pallas_call | solution.py:98
  188.8 2.0 pick_1_1_1.1
  191.8 2.7 collective-permute-done.45.refs_5_
  194.9 6.0 %collective-permute-done.46.refs_6_ = bf16[4,256,128]{2,1,0:T(8,128)(2,1)S(1)} collective-permute-done((bf16[4,256,128]{2,1,0:T(8,128)(2,1)S(1)}, bf16[4,256,128]{2,1,0:T(8,128)(2,1)S(1)}, u32[]{:S(2)}, u32[]{:S(2)}) %collective-permute-start.46) | collective-permute-done | bytes 262176 | tf_op jit(solution)/shard_map/ppermute | solution.py:247
  201.4 2.3 collective-permute-start.57
  206.9 5.1 %collective-permute-done.50.refs_10_ = bf16[4,256,128]{2,1,0:T(8,128)(2,1)S(1)} collective-permute-done((bf16[4,256,128]{2,1,0:T(8,128)(2,1)S(1)}, bf16[4,256,128]{2,1,0:T(8,128)(2,1)S(1)}, u32[]{:S(2)}, u32[]{:S(2)}) %collective-permute-start.50) | collective-permute-done | bytes 262176 | tf_op jit(solution)/shard_map/ppermute | solution.py:247
  214.9 7.6 %collective-permute-done.54.refs_14_ = bf16[4,256,128]{2,1,0:T(8,128)(2,1)S(1)} collective-permute-done((bf16[4,256,128]{2,1,0:T(8,128)(2,1)S(1)}, bf16[4,256,128]{2,1,0:T(8,128)(2,1)S(1)}, u32[]{:S(2)}, u32[]{:S(2)}) %collective-permute-start.54) | collective-permute-done | bytes 262176 | tf_op jit(solution)/shard_map/ppermute | solution.py:254
  222.5 5.7 %level_2_1.1 = (bf16[8,256,128]{2,1,0:T(8,128)(2,1)S(1)}, bf16[4,8,256,256]{3,2,1,0:T(8,128)(2,1)}) custom-call(s32[32]{0:T(128)S(1)} %get-tuple-element.224.refs_0_, bf16[4,8,256,256]{3,2,1,0:T(8,128)(2,1)} %refs_1_.15, bf16[4,8,256,256]{3,2,1,0:T(8,128)(2,1)} %refs_2_.15, bf16[3,8,4,256,256]{4,3,2,1,0:T(8,128)(2,1)} %refs_3_.11, ...), custom_call_target="tpu_custom_call", output_to_operand_aliasing={{1}: (16, {})} | custom-call | flops 134217728 | bytes 8000000 | tf_op jit(solution)/shard_map/level_2_1/pallas_call | solution.py:98
  228.3 2.5 collective-permute-start.58
  231.0 13.0 %collective-permute-done.58.refs_5_.refs_9_ = bf16[8,256,128]{2,1,0:T(8,128)(2,1)S(1)} collective-permute-done((bf16[8,256,128]{2,1,0:T(8,128)(2,1)S(1)}, bf16[8,256,128]{2,1,0:T(8,128)(2,1)S(1)}, u32[]{:S(2)}, u32[]{:S(2)}) %collective-permute-start.58) | collective-permute-done | bytes 524320 | tf_op jit(solution)/shard_map/ppermute | solution.py:240
  249.3 6.0 %collective-permute-done.62.refs_11_ = bf16[8,256,128]{2,1,0:T(8,128)(2,1)S(1)} collective-permute-done((bf16[8,256,128]{2,1,0:T(8,128)(2,1)S(1)}, bf16[8,256,128]{2,1,0:T(8,128)(2,1)S(1)}, u32[]{:S(2)}, u32[]{:S(2)}) %collective-permute-start.62) | collective-permute-done | bytes 524320 | tf_op jit(solution)/shard_map/ppermute | solution.py:240
  255.2 2.4 pick_2_0_1.1
  260.3 5.6 %collective-permute-done.70.refs_17_.refs_10_ = bf16[8,256,128]{2,1,0:T(8,128)(2,1)S(1)} collective-permute-done((bf16[8,256,128]{2,1,0:T(8,128)(2,1)S(1)}, bf16[8,256,128]{2,1,0:T(8,128)(2,1)S(1)}, u32[]{:S(2)}, u32[]{:S(2)}) %collective-permute-start.70) | collective-permute-done | bytes 524320 | tf_op jit(solution)/shard_map/ppermute | solution.py:240
  272.6 3.7 %collective-permute-done.67.refs_13_ = bf16[4,256,128]{2,1,0:T(8,128)(2,1)S(1)} collective-permute-done((bf16[4,256,128]{2,1,0:T(8,128)(2,1)S(1)}, bf16[4,256,128]{2,1,0:T(8,128)(2,1)S(1)}, u32[]{:S(2)}, u32[]{:S(2)}) %collective-permute-start.67) | collective-permute-done | bytes 262176 | tf_op jit(solution)/shard_map/ppermute | solution.py:254
  277.6 3.3 collective-permute-done.69.refs_15_
  280.9 5.7 %level_3_0.1 = (bf16[8,256,128]{2,1,0:T(8,128)(2,1)S(1)}, bf16[4,8,256,256]{3,2,1,0:T(8,128)(2,1)}) custom-call(s32[32]{0:T(128)S(1)} %get-tuple-element.226.refs_0_, bf16[4,8,256,256]{3,2,1,0:T(8,128)(2,1)} %refs_1_.15, bf16[4,8,256,256]{3,2,1,0:T(8,128)(2,1)} %refs_2_.15, bf16[3,8,4,256,256]{4,3,2,1,0:T(8,128)(2,1)} %refs_3_.11, ...), custom_call_target="tpu_custom_call", output_to_operand_aliasing={{1}: (16, {})} | custom-call | flops 134217728 | bytes 8000000 | tf_op jit(solution)/shard_map/level_3_0/pallas_call | solution.py:98
  291.2 2.4 pick_2_1_1.1
  298.7 5.2 %collective-permute-done.72.refs_6_ = bf16[4,256,128]{2,1,0:T(8,128)(2,1)S(1)} collective-permute-done((bf16[4,256,128]{2,1,0:T(8,128)(2,1)S(1)}, bf16[4,256,128]{2,1,0:T(8,128)(2,1)S(1)}, u32[]{:S(2)}, u32[]{:S(2)}) %collective-permute-start.72) | collective-permute-done | bytes 262176 | tf_op jit(solution)/shard_map/ppermute | solution.py:247
  309.4 5.7 %collective-permute-done.76.refs_10_ = bf16[4,256,128]{2,1,0:T(8,128)(2,1)S(1)} collective-permute-done((bf16[4,256,128]{2,1,0:T(8,128)(2,1)S(1)}, bf16[4,256,128]{2,1,0:T(8,128)(2,1)S(1)}, u32[]{:S(2)}, u32[]{:S(2)}) %collective-permute-start.76) | collective-permute-done | bytes 262176 | tf_op jit(solution)/shard_map/ppermute | solution.py:247
  317.6 6.1 %collective-permute-done.81.refs_15_ = bf16[4,256,128]{2,1,0:T(8,128)(2,1)S(1)} collective-permute-done((bf16[4,256,128]{2,1,0:T(8,128)(2,1)S(1)}, bf16[4,256,128]{2,1,0:T(8,128)(2,1)S(1)}, u32[]{:S(2)}, u32[]{:S(2)}) %collective-permute-start.81) | collective-permute-done | bytes 262176 | tf_op jit(solution)/shard_map/ppermute | solution.py:254
  323.7 6.6 %level_3_1.1 = (bf16[8,256,128]{2,1,0:T(8,128)(2,1)}, bf16[4,8,256,256]{3,2,1,0:T(8,128)(2,1)}) custom-call(s32[32]{0:T(128)S(1)} %get-tuple-element.226.refs_0_, bf16[4,8,256,256]{3,2,1,0:T(8,128)(2,1)} %refs_1_.15, bf16[4,8,256,256]{3,2,1,0:T(8,128)(2,1)} %refs_2_.15, bf16[3,8,4,256,256]{4,3,2,1,0:T(8,128)(2,1)} %refs_3_.11, ...), custom_call_target="tpu_custom_call", output_to_operand_aliasing={{1}: (16, {})} | custom-call | flops 134217728 | bytes 8000000 | tf_op jit(solution)/shard_map/level_3_1/pallas_call | solution.py:98
  (228 shorter events, 99.1 us)
Async XLA Ops:
  12.8 15.1 %collective-permute-start.4 = (bf16[8,256,128]{2,1,0:T(8,128)(2,1)}, bf16[8,256,128]{2,1,0:T(8,128)(2,1)S(1)}, u32[]{:S(2)}, u32[]{:S(2)}) collective-permute-start(bf16[8,256,128]{2,1,0:T(8,128)(2,1)} %get-tuple-element.93.refs_0_), channel_id=1, source_target_pairs={{0,4},{1,5},{2,6},{3,7},{4,8},{5,9},{6,10},{7,11},{8,12},{9,13},{1... | collective-permute-start | bytes 1572872 | tf_op jit(solution)/shard_map/ppermute | solution.py:240
  27.9 13.7 %collective-permute-start.9 = (bf16[8,256,128]{2,1,0:T(8,128)(2,1)S(1)}, bf16[8,256,128]{2,1,0:T(8,128)(2,1)S(1)}, u32[]{:S(2)}, u32[]{:S(2)}) collective-permute-start(bf16[8,256,128]{2,1,0:T(8,128)(2,1)S(1)} %collective-permute-done.4.refs_4_.refs_1_), channel_id=1, source_target_pairs={{0,4},{1,5},{2,6},{3,7},{4,8},{5,9},{6,10},{7,11},{8,12},{9,13},{1... | collective-permute-start | bytes 1572872 | tf_op jit(solution)/shard_map/ppermute | solution.py:240
  33.8 19.1 %collective-permute-start.5 = (bf16[8,256,128]{2,1,0:T(8,128)(2,1)}, bf16[8,256,128]{2,1,0:T(8,128)(2,1)S(1)}, u32[]{:S(2)}, u32[]{:S(2)}) collective-permute-start(bf16[8,256,128]{2,1,0:T(8,128)(2,1)} %get-tuple-element.94.refs_2_.refs_4_.refs_0_), channel_id=1, source_target_pairs={{0,4},{1,5},{2,6},{3,7},{4,8},{5,9},{6,10},{7,11},{8,12},{9,13},{1... | collective-permute-start | bytes 1572872 | tf_op jit(solution)/shard_map/ppermute | solution.py:240
  41.6 22.5 %collective-permute-start.10 = (bf16[8,256,128]{2,1,0:T(8,128)(2,1)S(1)}, bf16[8,256,128]{2,1,0:T(8,128)(2,1)S(1)}, u32[]{:S(2)}, u32[]{:S(2)}) collective-permute-start(bf16[8,256,128]{2,1,0:T(8,128)(2,1)S(1)} %collective-permute-done.9.refs_2_), channel_id=1, source_target_pairs={{0,4},{1,5},{2,6},{3,7},{4,8},{5,9},{6,10},{7,11},{8,12},{9,13},{1... | collective-permute-start | bytes 1572872 | tf_op jit(solution)/shard_map/ppermute | solution.py:240
  46.0 22.8 %collective-permute-start.6 = (bf16[4,256,128]{2,1,0:T(8,128)(2,1)}, bf16[4,256,128]{2,1,0:T(8,128)(2,1)S(1)}, u32[]{:S(2)}, u32[]{:S(2)}) collective-permute-start(bf16[4,256,128]{2,1,0:T(8,128)(2,1)} %get-tuple-element.96), channel_id=1, source_target_pairs={{0,1},{1,0},{2,3},{3,2},{4,5},{5,4},{6,7},{7,6},{8,9},{9,8},{10,11... | collective-permute-start | bytes 786440 | tf_op jit(solution)/shard_map/ppermute | solution.py:247
  52.9 22.5 %collective-permute-start.18 = (bf16[8,256,128]{2,1,0:T(8,128)(2,1)S(1)}, bf16[8,256,128]{2,1,0:T(8,128)(2,1)S(1)}, u32[]{:S(2)}, u32[]{:S(2)}) collective-permute-start(bf16[8,256,128]{2,1,0:T(8,128)(2,1)S(1)} %collective-permute-done.5.refs_1_), channel_id=1, source_target_pairs={{0,4},{1,5},{2,6},{3,7},{4,8},{5,9},{6,10},{7,11},{8,12},{9,13},{1... | collective-permute-start | bytes 1572872 | tf_op jit(solution)/shard_map/ppermute | solution.py:240
  54.8 15.5 %collective-permute-start.7 = (bf16[4,256,128]{2,1,0:T(8,128)(2,1)}, bf16[4,256,128]{2,1,0:T(8,128)(2,1)S(1)}, u32[]{:S(2)}, u32[]{:S(2)}) collective-permute-start(bf16[4,256,128]{2,1,0:T(8,128)(2,1)} %copy-done.9), channel_id=1, source_target_pairs={{0,2},{1,3},{2,0},{3,1},{4,6},{5,7},{6,4},{7,5},{8,10},{9,11},{10,... | collective-permute-start | bytes 786440 | tf_op jit(solution)/shard_map/ppermute | solution.py:247
  55.6 15.4 %collective-permute-start.8 = (bf16[4,256,128]{2,1,0:T(8,128)(2,1)S(1)}, bf16[4,256,128]{2,1,0:T(8,128)(2,1)S(1)}, u32[]{:S(2)}, u32[]{:S(2)}) collective-permute-start(bf16[4,256,128]{2,1,0:T(8,128)(2,1)S(1)} %get-tuple-element.98), channel_id=1, source_target_pairs={{0,3},{1,2},{2,1},{3,0},{4,7},{5,6},{6,5},{7,4},{8,11},{9,10},{10,... | collective-permute-start | bytes 786440 | tf_op jit(solution)/shard_map/ppermute | solution.py:247
  77.9 13.0 %collective-permute-start.17 = (bf16[4,256,128]{2,1,0:T(8,128)(2,1)S(1)}, bf16[4,256,128]{2,1,0:T(8,128)(2,1)S(1)}, u32[]{:S(2)}, u32[]{:S(2)}) collective-permute-start(bf16[4,256,128]{2,1,0:T(8,128)(2,1)S(1)} %get-tuple-element.106), channel_id=1, source_target_pairs={{0,19},{1,18},{2,17},{3,16},{4,23},{5,22},{6,21},{7,20},{8,27},{9,... | collective-permute-start | bytes 786440 | tf_op jit(solution)/shard_map/ppermute | solution.py:254
  79.3 21.8 %collective-permute-start.22 = (bf16[8,256,128]{2,1,0:T(8,128)(2,1)S(1)}, bf16[8,256,128]{2,1,0:T(8,128)(2,1)S(1)}, u32[]{:S(2)}, u32[]{:S(2)}) collective-permute-start(bf16[8,256,128]{2,1,0:T(8,128)(2,1)S(1)} %collective-permute-done.18.refs_17_.refs_2_), channel_id=1, source_target_pairs={{0,4},{1,5},{2,6},{3,7},{4,8},{5,9},{6,10},{7,11},{8,12},{9,13},{1... | collective-permute-start | bytes 1572872 | tf_op jit(solution)/shard_map/ppermute | solution.py:240
  96.7 12.9 %collective-permute-start.30 = (bf16[8,256,128]{2,1,0:T(8,128)(2,1)S(1)}, bf16[8,256,128]{2,1,0:T(8,128)(2,1)S(1)}, u32[]{:S(2)}, u32[]{:S(2)}) collective-permute-start(bf16[8,256,128]{2,1,0:T(8,128)(2,1)S(1)} %get-tuple-element.108.refs_2_.refs_4_), channel_id=1, source_target_pairs={{0,4},{1,5},{2,6},{3,7},{4,8},{5,9},{6,10},{7,11},{8,12},{9,13},{1... | collective-permute-start | bytes 1572872 | tf_op jit(solution)/shard_map/ppermute | solution.py:240
  99.0 14.2 %collective-permute-start.21 = (bf16[4,256,128]{2,1,0:T(8,128)(2,1)S(1)}, bf16[4,256,128]{2,1,0:T(8,128)(2,1)S(1)}, u32[]{:S(2)}, u32[]{:S(2)}) collective-permute-start(bf16[4,256,128]{2,1,0:T(8,128)(2,1)S(1)} %get-tuple-element.112), channel_id=1, source_target_pairs={{0,3},{1,2},{2,1},{3,0},{4,7},{5,6},{6,5},{7,4},{8,11},{9,10},{10,... | collective-permute-start | bytes 786440 | tf_op jit(solution)/shard_map/ppermute | solution.py:247
  103.2 12.3 %collective-permute-start.23 = (bf16[4,256,128]{2,1,0:T(8,128)(2,1)S(1)}, bf16[4,256,128]{2,1,0:T(8,128)(2,1)S(1)}, u32[]{:S(2)}, u32[]{:S(2)}) collective-permute-start(bf16[4,256,128]{2,1,0:T(8,128)(2,1)S(1)} %get-tuple-element.114), channel_id=1, source_target_pairs={{0,1},{1,0},{2,3},{3,2},{4,5},{5,4},{6,7},{7,6},{8,9},{9,8},{10,11... | collective-permute-start | bytes 786440 | tf_op jit(solution)/shard_map/ppermute | solution.py:247
  106.8 15.6 %collective-permute-start.24 = (bf16[4,256,128]{2,1,0:T(8,128)(2,1)S(1)}, bf16[4,256,128]{2,1,0:T(8,128)(2,1)S(1)}, u32[]{:S(2)}, u32[]{:S(2)}) collective-permute-start(bf16[4,256,128]{2,1,0:T(8,128)(2,1)S(1)} %get-tuple-element.115), channel_id=1, source_target_pairs={{0,2},{1,3},{2,0},{3,1},{4,6},{5,7},{6,4},{7,5},{8,10},{9,11},{10,... | collective-permute-start | bytes 786440 | tf_op jit(solution)/shard_map/ppermute | solution.py:247
  109.7 15.4 %collective-permute-start.31 = (bf16[8,256,128]{2,1,0:T(8,128)(2,1)S(1)}, bf16[8,256,128]{2,1,0:T(8,128)(2,1)S(1)}, u32[]{:S(2)}, u32[]{:S(2)}) collective-permute-start(bf16[8,256,128]{2,1,0:T(8,128)(2,1)S(1)} %collective-permute-done.30.refs_3_.refs_5_), channel_id=1, source_target_pairs={{0,4},{1,5},{2,6},{3,7},{4,8},{5,9},{6,10},{7,11},{8,12},{9,13},{1... | collective-permute-start | bytes 1572872 | tf_op jit(solution)/shard_map/ppermute | solution.py:240
  110.7 13.0 %collective-permute-start.25 = (bf16[4,256,128]{2,1,0:T(8,128)(2,1)S(1)}, bf16[4,256,128]{2,1,0:T(8,128)(2,1)S(1)}, u32[]{:S(2)}, u32[]{:S(2)}) collective-permute-start(bf16[4,256,128]{2,1,0:T(8,128)(2,1)S(1)} %get-tuple-element.116), channel_id=1, source_target_pairs={{0,3},{1,2},{2,1},{3,0},{4,7},{5,6},{6,5},{7,4},{8,11},{9,10},{10,... | collective-permute-start | bytes 786440 | tf_op jit(solution)/shard_map/ppermute | solution.py:247
  113.2 12.1 %collective-permute-start.26 = (bf16[4,256,128]{2,1,0:T(8,128)(2,1)S(1)}, bf16[4,256,128]{2,1,0:T(8,128)(2,1)S(1)}, u32[]{:S(2)}, u32[]{:S(2)}) collective-permute-start(bf16[4,256,128]{2,1,0:T(8,128)(2,1)S(1)} %get-tuple-element.117), channel_id=1, source_target_pairs={{0,16},{1,17},{2,18},{3,19},{4,20},{5,21},{6,22},{7,23},{8,24},{9,... | collective-permute-start | bytes 786440 | tf_op jit(solution)/shard_map/ppermute | solution.py:254
  125.1 18.6 %collective-permute-start.36 = (bf16[8,256,128]{2,1,0:T(8,128)(2,1)S(1)}, bf16[8,256,128]{2,1,0:T(8,128)(2,1)S(1)}, u32[]{:S(2)}, u32[]{:S(2)}) collective-permute-start(bf16[8,256,128]{2,1,0:T(8,128)(2,1)S(1)} %collective-permute-done.31.refs_17_.refs_6_), channel_id=1, source_target_pairs={{0,4},{1,5},{2,6},{3,7},{4,8},{5,9},{6,10},{7,11},{8,12},{9,13},{1... | collective-permute-start | bytes 1572872 | tf_op jit(solution)/shard_map/ppermute | solution.py:240
  138.7 16.4 %collective-permute-start.32 = (bf16[8,256,128]{2,1,0:T(8,128)(2,1)S(1)}, bf16[8,256,128]{2,1,0:T(8,128)(2,1)S(1)}, u32[]{:S(2)}, u32[]{:S(2)}) collective-permute-start(bf16[8,256,128]{2,1,0:T(8,128)(2,1)S(1)} %get-tuple-element.122.refs_4_.refs_8_.refs_2_), channel_id=1, source_target_pairs={{0,4},{1,5},{2,6},{3,7},{4,8},{5,9},{6,10},{7,11},{8,12},{9,13},{1... | collective-permute-start | bytes 1572872 | tf_op jit(solution)/shard_map/ppermute | solution.py:240
  141.5 14.2 %collective-permute-start.34 = (bf16[4,256,128]{2,1,0:T(8,128)(2,1)S(1)}, bf16[4,256,128]{2,1,0:T(8,128)(2,1)S(1)}, u32[]{:S(2)}, u32[]{:S(2)}) collective-permute-start(bf16[4,256,128]{2,1,0:T(8,128)(2,1)S(1)} %get-tuple-element.125), channel_id=1, source_target_pairs={{0,2},{1,3},{2,0},{3,1},{4,6},{5,7},{6,4},{7,5},{8,10},{9,11},{10,... | collective-permute-start | bytes 786440 | tf_op jit(solution)/shard_map/ppermute | solution.py:247
  143.5 12.9 %collective-permute-start.35 = (bf16[4,256,128]{2,1,0:T(8,128)(2,1)S(1)}, bf16[4,256,128]{2,1,0:T(8,128)(2,1)S(1)}, u32[]{:S(2)}, u32[]{:S(2)}) collective-permute-start(bf16[4,256,128]{2,1,0:T(8,128)(2,1)S(1)} %get-tuple-element.126), channel_id=1, source_target_pairs={{0,3},{1,2},{2,1},{3,0},{4,7},{5,6},{6,5},{7,4},{8,11},{9,10},{10,... | collective-permute-start | bytes 786440 | tf_op jit(solution)/shard_map/ppermute | solution.py:247
  145.7 14.1 %collective-permute-start.37 = (bf16[4,256,128]{2,1,0:T(8,128)(2,1)S(1)}, bf16[4,256,128]{2,1,0:T(8,128)(2,1)S(1)}, u32[]{:S(2)}, u32[]{:S(2)}) collective-permute-start(bf16[4,256,128]{2,1,0:T(8,128)(2,1)S(1)} %get-tuple-element.128), channel_id=1, source_target_pairs={{0,1},{1,0},{2,3},{3,2},{4,5},{5,4},{6,7},{7,6},{8,9},{9,8},{10,11... | collective-permute-start | bytes 786440 | tf_op jit(solution)/shard_map/ppermute | solution.py:247
  148.5 18.7 %collective-permute-start.38 = (bf16[4,256,128]{2,1,0:T(8,128)(2,1)S(1)}, bf16[4,256,128]{2,1,0:T(8,128)(2,1)S(1)}, u32[]{:S(2)}, u32[]{:S(2)}) collective-permute-start(bf16[4,256,128]{2,1,0:T(8,128)(2,1)S(1)} %get-tuple-element.129), channel_id=1, source_target_pairs={{0,2},{1,3},{2,0},{3,1},{4,6},{5,7},{6,4},{7,5},{8,10},{9,11},{10,... | collective-permute-start | bytes 786440 | tf_op jit(solution)/shard_map/ppermute | solution.py:247
  155.1 14.9 %collective-permute-start.44 = (bf16[8,256,128]{2,1,0:T(8,128)(2,1)S(1)}, bf16[8,256,128]{2,1,0:T(8,128)(2,1)S(1)}, u32[]{:S(2)}, u32[]{:S(2)}) collective-permute-start(bf16[8,256,128]{2,1,0:T(8,128)(2,1)S(1)} %collective-permute-done.32.refs_3_.refs_5_), channel_id=1, source_target_pairs={{0,4},{1,5},{2,6},{3,7},{4,8},{5,9},{6,10},{7,11},{8,12},{9,13},{1... | collective-permute-start | bytes 1572872 | tf_op jit(solution)/shard_map/ppermute | solution.py:240
  155.7 12.8 %collective-permute-start.39 = (bf16[4,256,128]{2,1,0:T(8,128)(2,1)S(1)}, bf16[4,256,128]{2,1,0:T(8,128)(2,1)S(1)}, u32[]{:S(2)}, u32[]{:S(2)}) collective-permute-start(bf16[4,256,128]{2,1,0:T(8,128)(2,1)S(1)} %get-tuple-element.130), channel_id=1, source_target_pairs={{0,3},{1,2},{2,1},{3,0},{4,7},{5,6},{6,5},{7,4},{8,11},{9,10},{10,... | collective-permute-start | bytes 786440 | tf_op jit(solution)/shard_map/ppermute | solution.py:247
  156.4 13.9 %collective-permute-start.40 = (bf16[4,256,128]{2,1,0:T(8,128)(2,1)S(1)}, bf16[4,256,128]{2,1,0:T(8,128)(2,1)S(1)}, u32[]{:S(2)}, u32[]{:S(2)}) collective-permute-start(bf16[4,256,128]{2,1,0:T(8,128)(2,1)S(1)} %get-tuple-element.131), channel_id=1, source_target_pairs={{0,16},{1,17},{2,18},{3,19},{4,20},{5,21},{6,22},{7,23},{8,24},{9,... | collective-permute-start | bytes 786440 | tf_op jit(solution)/shard_map/ppermute | solution.py:254
  170.1 18.8 %collective-permute-start.48 = (bf16[8,256,128]{2,1,0:T(8,128)(2,1)S(1)}, bf16[8,256,128]{2,1,0:T(8,128)(2,1)S(1)}, u32[]{:S(2)}, u32[]{:S(2)}) collective-permute-start(bf16[8,256,128]{2,1,0:T(8,128)(2,1)S(1)} %collective-permute-done.44.refs_17_.refs_6_), channel_id=1, source_target_pairs={{0,4},{1,5},{2,6},{3,7},{4,8},{5,9},{6,10},{7,11},{8,12},{9,13},{1... | collective-permute-start | bytes 1572872 | tf_op jit(solution)/shard_map/ppermute | solution.py:240
  183.7 17.7 %collective-permute-start.56 = (bf16[8,256,128]{2,1,0:T(8,128)(2,1)S(1)}, bf16[8,256,128]{2,1,0:T(8,128)(2,1)S(1)}, u32[]{:S(2)}, u32[]{:S(2)}) collective-permute-start(bf16[8,256,128]{2,1,0:T(8,128)(2,1)S(1)} %get-tuple-element.136.refs_4_.refs_8_), channel_id=1, source_target_pairs={{0,4},{1,5},{2,6},{3,7},{4,8},{5,9},{6,10},{7,11},{8,12},{9,13},{1... | collective-permute-start | bytes 1572872 | tf_op jit(solution)/shard_map/ppermute | solution.py:240
  187.0 13.9 %collective-permute-start.46 = (bf16[4,256,128]{2,1,0:T(8,128)(2,1)S(1)}, bf16[4,256,128]{2,1,0:T(8,128)(2,1)S(1)}, u32[]{:S(2)}, u32[]{:S(2)}) collective-permute-start(bf16[4,256,128]{2,1,0:T(8,128)(2,1)S(1)} %get-tuple-element.139), channel_id=1, source_target_pairs={{0,2},{1,3},{2,0},{3,1},{4,6},{5,7},{6,4},{7,5},{8,10},{9,11},{10,... | collective-permute-start | bytes 786440 | tf_op jit(solution)/shard_map/ppermute | solution.py:247
  188.0 15.7 %collective-permute-start.47 = (bf16[4,256,128]{2,1,0:T(8,128)(2,1)S(1)}, bf16[4,256,128]{2,1,0:T(8,128)(2,1)S(1)}, u32[]{:S(2)}, u32[]{:S(2)}) collective-permute-start(bf16[4,256,128]{2,1,0:T(8,128)(2,1)S(1)} %get-tuple-element.140), channel_id=1, source_target_pairs={{0,3},{1,2},{2,1},{3,0},{4,7},{5,6},{6,5},{7,4},{8,11},{9,10},{10,... | collective-permute-start | bytes 786440 | tf_op jit(solution)/shard_map/ppermute | solution.py:247
  190.8 14.8 %collective-permute-start.49 = (bf16[4,256,128]{2,1,0:T(8,128)(2,1)S(1)}, bf16[4,256,128]{2,1,0:T(8,128)(2,1)S(1)}, u32[]{:S(2)}, u32[]{:S(2)}) collective-permute-start(bf16[4,256,128]{2,1,0:T(8,128)(2,1)S(1)} %get-tuple-element.142), channel_id=1, source_target_pairs={{0,1},{1,0},{2,3},{3,2},{4,5},{5,4},{6,7},{7,6},{8,9},{9,8},{10,11... | collective-permute-start | bytes 786440 | tf_op jit(solution)/shard_map/ppermute | solution.py:247
  194.5 17.6 %collective-permute-start.50 = (bf16[4,256,128]{2,1,0:T(8,128)(2,1)S(1)}, bf16[4,256,128]{2,1,0:T(8,128)(2,1)S(1)}, u32[]{:S(2)}, u32[]{:S(2)}) collective-permute-start(bf16[4,256,128]{2,1,0:T(8,128)(2,1)S(1)} %get-tuple-element.143), channel_id=1, source_target_pairs={{0,2},{1,3},{2,0},{3,1},{4,6},{5,7},{6,4},{7,5},{8,10},{9,11},{10,... | collective-permute-start | bytes 786440 | tf_op jit(solution)/shard_map/ppermute | solution.py:247
  200.9 12.4 %collective-permute-start.51 = (bf16[4,256,128]{2,1,0:T(8,128)(2,1)S(1)}, bf16[4,256,128]{2,1,0:T(8,128)(2,1)S(1)}, u32[]{:S(2)}, u32[]{:S(2)}) collective-permute-start(bf16[4,256,128]{2,1,0:T(8,128)(2,1)S(1)} %get-tuple-element.144), channel_id=1, source_target_pairs={{0,3},{1,2},{2,1},{3,0},{4,7},{5,6},{6,5},{7,4},{8,11},{9,10},{10,... | collective-permute-start | bytes 786440 | tf_op jit(solution)/shard_map/ppermute | solution.py:247
  201.4 21.1 %collective-permute-start.57 = (bf16[8,256,128]{2,1,0:T(8,128)(2,1)S(1)}, bf16[8,256,128]{2,1,0:T(8,128)(2,1)S(1)}, u32[]{:S(2)}, u32[]{:S(2)}) collective-permute-start(bf16[8,256,128]{2,1,0:T(8,128)(2,1)S(1)} %collective-permute-done.56.refs_5_.refs_9_), channel_id=1, source_target_pairs={{0,4},{1,5},{2,6},{3,7},{4,8},{5,9},{6,10},{7,11},{8,12},{9,13},{1... | collective-permute-start | bytes 1572872 | tf_op jit(solution)/shard_map/ppermute | solution.py:240
  228.3 15.7 %collective-permute-start.58 = (bf16[8,256,128]{2,1,0:T(8,128)(2,1)S(1)}, bf16[8,256,128]{2,1,0:T(8,128)(2,1)S(1)}, u32[]{:S(2)}, u32[]{:S(2)}) collective-permute-start(bf16[8,256,128]{2,1,0:T(8,128)(2,1)S(1)} %get-tuple-element.150.refs_6_.refs_12_.refs_4_.refs_8_), channel_id=1, source_target_pairs={{0,4},{1,5},{2,6},{3,7},{4,8},{5,9},{6,10},{7,11},{8,12},{9,13},{1... | collective-permute-start | bytes 1572872 | tf_op jit(solution)/shard_map/ppermute | solution.py:240
  230.8 24.5 %collective-permute-start.62 = (bf16[8,256,128]{2,1,0:T(8,128)(2,1)S(1)}, bf16[8,256,128]{2,1,0:T(8,128)(2,1)S(1)}, u32[]{:S(2)}, u32[]{:S(2)}) collective-permute-start(bf16[8,256,128]{2,1,0:T(8,128)(2,1)S(1)} %collective-permute-done.57.refs_17_.refs_10_), channel_id=1, source_target_pairs={{0,4},{1,5},{2,6},{3,7},{4,8},{5,9},{6,10},{7,11},{8,12},{9,13},{1... | collective-permute-start | bytes 1572872 | tf_op jit(solution)/shard_map/ppermute | solution.py:240
  244.0 21.9 %collective-permute-start.70 = (bf16[8,256,128]{2,1,0:T(8,128)(2,1)S(1)}, bf16[8,256,128]{2,1,0:T(8,128)(2,1)S(1)}, u32[]{:S(2)}, u32[]{:S(2)}) collective-permute-start(bf16[8,256,128]{2,1,0:T(8,128)(2,1)S(1)} %collective-permute-done.58.refs_5_.refs_9_), channel_id=1, source_target_pairs={{0,4},{1,5},{2,6},{3,7},{4,8},{5,9},{6,10},{7,11},{8,12},{9,13},{1... | collective-permute-start | bytes 1572872 | tf_op jit(solution)/shard_map/ppermute | solution.py:240
  246.6 12.1 %collective-permute-start.60 = (bf16[4,256,128]{2,1,0:T(8,128)(2,1)S(1)}, bf16[4,256,128]{2,1,0:T(8,128)(2,1)S(1)}, u32[]{:S(2)}, u32[]{:S(2)}) collective-permute-start(bf16[4,256,128]{2,1,0:T(8,128)(2,1)S(1)} %get-tuple-element.153), channel_id=1, source_target_pairs={{0,2},{1,3},{2,0},{3,1},{4,6},{5,7},{6,4},{7,5},{8,10},{9,11},{10,... | collective-permute-start | bytes 786440 | tf_op jit(solution)/shard_map/ppermute | solution.py:247
  247.5 19.5 %collective-permute-start.61 = (bf16[4,256,128]{2,1,0:T(8,128)(2,1)S(1)}, bf16[4,256,128]{2,1,0:T(8,128)(2,1)S(1)}, u32[]{:S(2)}, u32[]{:S(2)}) collective-permute-start(bf16[4,256,128]{2,1,0:T(8,128)(2,1)S(1)} %get-tuple-element.154), channel_id=1, source_target_pairs={{0,3},{1,2},{2,1},{3,0},{4,7},{5,6},{6,5},{7,4},{8,11},{9,10},{10,... | collective-permute-start | bytes 786440 | tf_op jit(solution)/shard_map/ppermute | solution.py:247
  257.8 11.8 %collective-permute-start.64 = (bf16[4,256,128]{2,1,0:T(8,128)(2,1)S(1)}, bf16[4,256,128]{2,1,0:T(8,128)(2,1)S(1)}, u32[]{:S(2)}, u32[]{:S(2)}) collective-permute-start(bf16[4,256,128]{2,1,0:T(8,128)(2,1)S(1)} %get-tuple-element.157), channel_id=1, source_target_pairs={{0,2},{1,3},{2,0},{3,1},{4,6},{5,7},{6,4},{7,5},{8,10},{9,11},{10,... | collective-permute-start | bytes 786440 | tf_op jit(solution)/shard_map/ppermute | solution.py:247
  258.7 12.6 %collective-permute-start.65 = (bf16[4,256,128]{2,1,0:T(8,128)(2,1)S(1)}, bf16[4,256,128]{2,1,0:T(8,128)(2,1)S(1)}, u32[]{:S(2)}, u32[]{:S(2)}) collective-permute-start(bf16[4,256,128]{2,1,0:T(8,128)(2,1)S(1)} %get-tuple-element.158), channel_id=1, source_target_pairs={{0,3},{1,2},{2,1},{3,0},{4,7},{5,6},{6,5},{7,4},{8,11},{9,10},{10,... | collective-permute-start | bytes 786440 | tf_op jit(solution)/shard_map/ppermute | solution.py:247
  265.9 25.3 %collective-permute-start.74 = (bf16[8,256,128]{2,1,0:T(8,128)(2,1)S(1)}, bf16[8,256,128]{2,1,0:T(8,128)(2,1)S(1)}, u32[]{:S(2)}, u32[]{:S(2)}) collective-permute-start(bf16[8,256,128]{2,1,0:T(8,128)(2,1)S(1)} %collective-permute-done.70.refs_17_.refs_10_), channel_id=1, source_target_pairs={{0,4},{1,5},{2,6},{3,7},{4,8},{5,9},{6,10},{7,11},{8,12},{9,13},{1... | collective-permute-start | bytes 1572872 | tf_op jit(solution)/shard_map/ppermute | solution.py:240
  289.9 13.9 %collective-permute-start.72 = (bf16[4,256,128]{2,1,0:T(8,128)(2,1)S(1)}, bf16[4,256,128]{2,1,0:T(8,128)(2,1)S(1)}, u32[]{:S(2)}, u32[]{:S(2)}) collective-permute-start(bf16[4,256,128]{2,1,0:T(8,128)(2,1)S(1)} %get-tuple-element.167), channel_id=1, source_target_pairs={{0,2},{1,3},{2,0},{3,1},{4,6},{5,7},{6,4},{7,5},{8,10},{9,11},{10,... | collective-permute-start | bytes 786440 | tf_op jit(solution)/shard_map/ppermute | solution.py:247
  290.6 14.5 %collective-permute-start.73 = (bf16[4,256,128]{2,1,0:T(8,128)(2,1)S(1)}, bf16[4,256,128]{2,1,0:T(8,128)(2,1)S(1)}, u32[]{:S(2)}, u32[]{:S(2)}) collective-permute-start(bf16[4,256,128]{2,1,0:T(8,128)(2,1)S(1)} %get-tuple-element.168), channel_id=1, source_target_pairs={{0,3},{1,2},{2,1},{3,0},{4,7},{5,6},{6,5},{7,4},{8,11},{9,10},{10,... | collective-permute-start | bytes 786440 | tf_op jit(solution)/shard_map/ppermute | solution.py:247
  293.6 14.5 %collective-permute-start.75 = (bf16[4,256,128]{2,1,0:T(8,128)(2,1)S(1)}, bf16[4,256,128]{2,1,0:T(8,128)(2,1)S(1)}, u32[]{:S(2)}, u32[]{:S(2)}) collective-permute-start(bf16[4,256,128]{2,1,0:T(8,128)(2,1)S(1)} %get-tuple-element.170), channel_id=1, source_target_pairs={{0,1},{1,0},{2,3},{3,2},{4,5},{5,4},{6,7},{7,6},{8,9},{9,8},{10,11... | collective-permute-start | bytes 786440 | tf_op jit(solution)/shard_map/ppermute | solution.py:247
  295.1 20.0 %collective-permute-start.76 = (bf16[4,256,128]{2,1,0:T(8,128)(2,1)S(1)}, bf16[4,256,128]{2,1,0:T(8,128)(2,1)S(1)}, u32[]{:S(2)}, u32[]{:S(2)}) collective-permute-start(bf16[4,256,128]{2,1,0:T(8,128)(2,1)S(1)} %get-tuple-element.171), channel_id=1, source_target_pairs={{0,2},{1,3},{2,0},{3,1},{4,6},{5,7},{6,4},{7,5},{8,10},{9,11},{10,... | collective-permute-start | bytes 786440 | tf_op jit(solution)/shard_map/ppermute | solution.py:247
  296.8 19.8 %collective-permute-start.77 = (bf16[4,256,128]{2,1,0:T(8,128)(2,1)S(1)}, bf16[4,256,128]{2,1,0:T(8,128)(2,1)S(1)}, u32[]{:S(2)}, u32[]{:S(2)}) collective-permute-start(bf16[4,256,128]{2,1,0:T(8,128)(2,1)S(1)} %get-tuple-element.172), channel_id=1, source_target_pairs={{0,3},{1,2},{2,1},{3,0},{4,7},{5,6},{6,5},{7,4},{8,11},{9,10},{10,... | collective-permute-start | bytes 786440 | tf_op jit(solution)/shard_map/ppermute | solution.py:247
  303.9 12.8 %collective-permute-start.78 = (bf16[4,256,128]{2,1,0:T(8,128)(2,1)S(1)}, bf16[4,256,128]{2,1,0:T(8,128)(2,1)S(1)}, u32[]{:S(2)}, u32[]{:S(2)}) collective-permute-start(bf16[4,256,128]{2,1,0:T(8,128)(2,1)S(1)} %get-tuple-element.173), channel_id=1, source_target_pairs={{0,16},{1,17},{2,18},{3,19},{4,20},{5,21},{6,22},{7,23},{8,24},{9,... | collective-permute-start | bytes 786440 | tf_op jit(solution)/shard_map/ppermute | solution.py:254
  (44 other events, 396.0 us)
